TPU v7x, 32 devices: a whole 2x2x4 slice. The times are simulated.
32 devices in a mesh: gx: 16 (over z, y, core), gy: 2 (over x).
Axes of the slice: x: 2, y: 2, z: 4, core: 2. Of those that a mesh axis runs over, the one named last changes fastest.
Arguments:
- control: bfloat16 [2048, 8, 2048], P('gx', None, 'gy'), may hold values from -6 to 6
- innovation: float32 [2048, 8, 2048], P('gx', None, 'gy'), may hold values from -6 to 6
- obs_weight: float32 [2048, 8, 2048], P('gx', None, 'gy'), may hold values from 0.5 to 4
- courant_x: float32 [2048, 8, 2048], P('gx', None, 'gy'), may hold values from -0.9 to 0.9
- courant_y: float32 [2048, 8, 2048], P('gx', None, 'gy'), may hold values from -0.9 to 0.9
- filter_x: bfloat16 [2048, 2048], P('gx'), may hold values from -3 to 3
- filter_y: bfloat16 [2048, 2048], P('gy'), may hold values from -3 to 3
Outputs:
- end_state: float32 [2048, 8, 2048], P('gx', None, 'gy')
- gradient: float32 [2048, 8, 2048], P('gx', None, 'gy')
All inputs are finite; a program needn't handle non-finite values.
Results may differ from a plain program's by a relative error of at most 0.0029.
Values may be sent and summed in bfloat16 or wider, within the bound.
No kernel may reach another device: no remote copies, remote signals or barrier semaphores. Data moves between devices by JAX's collectives and lax.ppermute only.
A program may use at most 192 MiB of HBM per device.

v0:
```python
import functools

import jax
import jax.numpy as jnp
from jax import lax
from jax.experimental import pallas as pl
from jax.experimental.pallas import tpu as pltpu
from jax.sharding import PartitionSpec as P

BF16 = jnp.bfloat16
F32 = jnp.float32
STEP = 32
TILE = 16
GROUP = 8
CHUNKS = 2
PARAMS = pltpu.CompilerParams(vmem_limit_bytes=56 * 1024 * 1024)


def cost(flops, *arrays):
    return pl.CostEstimate(
        flops=flops,
        bytes_accessed=sum(a.size * a.dtype.itemsize for a in arrays),
        transcendentals=0,
    )


def chunk_spans(width, parts, chunk):
    part = width // parts
    piece = part // CHUNKS
    return [
        slice(s * part + chunk * piece, s * part + (chunk + 1) * piece)
        for s in range(parts)
    ]


def store_lines(turned, out, parts):
    piece = out.shape[2]

    @pl.loop(0, turned.shape[0] // TILE)
    def _(tile):
        at = pl.ds(tile * TILE, TILE)
        for l in range(turned.shape[1]):
            for s in range(parts):
                got = turned[at, l, s * piece : (s + 1) * piece]
                out[l * parts + s, at] = got.astype(BF16)


def lines_body(parts, chunk, block, out, turned):
    piece = out.shape[2]
    for s, span in enumerate(chunk_spans(block.shape[2], parts, chunk)):
        turned[:, :, s * piece : (s + 1) * piece] = block[:, :, span].astype(F32)
    store_lines(turned, out, parts)


def as_lines(block, parts, chunk):
    rows, levels, width = block.shape
    shape = (levels * parts, rows, width // parts // CHUNKS)
    return pl.pallas_call(
        functools.partial(lines_body, parts, chunk),
        grid=(rows // STEP,),
        in_specs=[pl.BlockSpec((STEP, levels, width), lambda i: (i, 0, 0))],
        out_specs=pl.BlockSpec((shape[0], STEP, shape[2]), lambda i: (0, i, 0)),
        out_shape=jax.ShapeDtypeStruct(shape, BF16),
        scratch_shapes=[pltpu.VMEM((STEP, levels, width // CHUNKS), F32)],
        compiler_params=PARAMS,
        cost_estimate=cost(0, block, block),
        name="as_lines",
    )(block)


def gradient_body(parts, lines, control, *rest):
    out, turned = rest[-2:]
    levels, width = control.shape[1:]
    part = width // parts
    for l in range(levels):
        for s in range(parts):
            turned[:, l, s * part : (s + 1) * part] = lines[l * parts + s].astype(F32)
    out[...] = control[...].astype(F32) + turned[...]


def add_lines(control, lines, parts, first, target):
    rows, levels, width = control.shape
    whole = (TILE, levels, width)
    cut = lines.shape[1]
    offset = first // TILE
    operands = [lines, control] + ([] if target is None else [target])
    return pl.pallas_call(
        functools.partial(gradient_body, parts),
        grid=(cut // TILE,),
        in_specs=[
            pl.BlockSpec((lines.shape[0], TILE, lines.shape[2]), lambda i: (0, i, 0)),
            pl.BlockSpec(whole, lambda i: (i + offset, 0, 0)),
        ]
        + [pl.BlockSpec(memory_space=pl.ANY)] * (len(operands) - 2),
        out_specs=pl.BlockSpec(whole, lambda i: (i + offset, 0, 0)),
        out_shape=jax.ShapeDtypeStruct(control.shape, F32),
        input_output_aliases={} if target is None else {2: 0},
        scratch_shapes=[pltpu.VMEM(whole, F32)],
        compiler_params=PARAMS,
        cost_estimate=cost(control.size // 2, control, control),
        name="add_lines",
    )(*operands)


def forward_body(*refs):
    starts = refs[:CHUNKS]
    rows_in, sides, innovation, weight, wind_x, wind_y = refs[CHUNKS : CHUNKS + 6]
    end, flat, row_flux, side_flux, state, carry = refs[CHUNKS + 6 :]
    step = pl.program_id(0)
    rows, levels, width = flat.shape
    cut = rows // CHUNKS

    @pl.when(step == 0)
    def _():
        state[pl.ds(0, 1)] = rows_in[pl.ds(0, 1)]
        state[pl.ds(rows + 1, 1)] = rows_in[pl.ds(1, 1)]
        for h in range(CHUNKS):
            state[pl.ds(1 + h * cut, cut)] = starts[h][...].astype(F32)
        carry[...] = jnp.zeros(carry.shape, F32)

    first = step * STEP
    place = lax.broadcasted_iota(jnp.int32, (GROUP, levels, width), 2)
    left_edge, right_edge = place == 0, place == width - 1
    @pl.loop(0, STEP // GROUP)
    def _(group):
        j = group * GROUP
        rows_j, at = pl.ds(j, GROUP), first + j
        here = state[pl.ds(at + 1, GROUP)]
        cx, cy = wind_x[rows_j], wind_y[rows_j]
        left = jnp.where(left_edge, sides[rows_j, :, 0:1], pltpu.roll(here, 1, 2))
        right = jnp.where(
            right_edge, sides[rows_j, :, 1:2], pltpu.roll(here, width - 1, 2)
        )
        dx = state[pl.ds(at + 2, GROUP)] - state[pl.ds(at, GROUP)]
        after = here - cx * dx * 0.5 - cy * (right - left) * 0.5
        end[rows_j] = after
        misfit = weight[rows_j] * (after - innovation[rows_j])
        p, q = cy * misfit, cx * misfit
        side_flux[rows_j, :, 0:1] = p[:, :, 0:1]
        side_flux[rows_j, :, 1:2] = p[:, :, width - 1 : width]
        left = jnp.where(left_edge, 0.0, pltpu.roll(p, 1, 2))
        right = jnp.where(right_edge, 0.0, pltpu.roll(p, width - 1, 2))
        flat_j = misfit + 0.5 * (right - left)
        flat[jnp.maximum(at - 1, 0)] = carry[2] + 0.5 * (q[0] - carry[0])
        flat[at] = flat_j[0] + 0.5 * (q[1] - carry[1])
        flat[pl.ds(at + 1, GROUP - 2)] = flat_j[1:-1] + 0.5 * (q[2:] - q[:-2])

        @pl.when(at == 0)
        def _():
            row_flux[0] = q[0]

        carry[0], carry[1], carry[2] = q[GROUP - 2], q[GROUP - 1], flat_j[GROUP - 1]

    @pl.when(step == rows // STEP - 1)
    def _():
        flat[rows - 1] = carry[2] - 0.5 * carry[0]
        row_flux[1] = carry[1]


def forward(starts, rows_in, sides, innovation, weight, wind_x, wind_y):
    rows, levels, width = innovation.shape
    blocked = pl.BlockSpec((STEP, levels, width), lambda i: (i, 0, 0))
    side = pl.BlockSpec((STEP, levels, 2), lambda i: (i, 0, 0))
    pair = pl.BlockSpec((2, levels, width), lambda i: (0, 0, 0))
    start = pl.BlockSpec(starts[0].shape, lambda i: (0, 0, 0))
    whole = pl.BlockSpec((rows, levels, width), lambda i: (0, 0, 0))
    return pl.pallas_call(
        forward_body,
        grid=(rows // STEP,),
        in_specs=[start] * CHUNKS + [pair, side, blocked, blocked, blocked, blocked],
        out_specs=[blocked, whole, pair, side],
        out_shape=[
            jax.ShapeDtypeStruct((rows, levels, width), F32),
            jax.ShapeDtypeStruct((rows, levels, width), F32),
            jax.ShapeDtypeStruct((2, levels, width), F32),
            jax.ShapeDtypeStruct((rows, levels, 2), F32),
        ],
        scratch_shapes=[
            pltpu.VMEM((rows + 2, levels, width), F32),
            pltpu.VMEM((3, levels, width), F32),
        ],
        compiler_params=PARAMS,
        cost_estimate=cost(30 * innovation.size, *[innovation] * 7),
        name="forward",
    )(*starts, rows_in, sides, innovation, weight, wind_x, wind_y)


def rim_body(parts, chunk, last, flat, rows_in, sides, out, turned):
    step = pl.program_id(0)
    levels, width = flat.shape[1:]
    piece = out.shape[2]
    place = lax.broadcasted_iota(jnp.int32, (STEP, levels, piece), 2)
    spans = chunk_spans(width, parts, chunk)
    for s, span in enumerate(spans):
        value = flat[:, :, span]
        if span.start == 0:
            value = value - jnp.where(place == 0, 0.5 * sides[:, :, 0:1], 0.0)
        if span.stop == width:
            value = value + jnp.where(place == piece - 1, 0.5 * sides[:, :, 1:2], 0.0)
        turned[:, :, s * piece : (s + 1) * piece] = value

    @pl.when(step == 0)
    def _():
        for s, span in enumerate(spans):
            at = slice(s * piece, (s + 1) * piece)
            turned[0, :, at] += -0.5 * rows_in[0, :, span]

    @pl.when(step == last)
    def _():
        for s, span in enumerate(spans):
            at = slice(s * piece, (s + 1) * piece)
            turned[STEP - 1, :, at] += 0.5 * rows_in[1, :, span]

    store_lines(turned, out, parts)


def rim_lines(flat, rows_in, sides, parts, chunk):
    rows, levels, width = flat.shape
    shape = (levels * parts, rows, width // parts // CHUNKS)
    return pl.pallas_call(
        functools.partial(rim_body, parts, chunk, rows // STEP - 1),
        grid=(rows // STEP,),
        in_specs=[
            pl.BlockSpec((STEP, levels, width), lambda i: (i, 0, 0)),
            pl.BlockSpec((2, levels, width), lambda i: (0, 0, 0)),
            pl.BlockSpec((STEP, levels, 2), lambda i: (i, 0, 0)),
        ],
        out_specs=pl.BlockSpec((shape[0], STEP, shape[2]), lambda i: (0, i, 0)),
        out_shape=jax.ShapeDtypeStruct(shape, BF16),
        scratch_shapes=[pltpu.VMEM((STEP, levels, width // CHUNKS), F32)],
        compiler_params=PARAMS,
        cost_estimate=cost(4 * flat.size, flat, flat),
        name="rim_lines",
    )(flat, rows_in, sides)


def swap_all(lines):
    return lax.all_to_all(lines, "gx", 0, 0, tiled=True)


def plane_pieces(lines, parts, after=None, near_first=False):
    n_x, n_y = lax.axis_size("gx"), lax.axis_size("gy")
    groups = [list(range(i, i + parts)) for i in range(0, n_x, parts)]
    if n_y == 2 and parts == 2:
        pairs = [(a, b) for g in groups for a, b in (g, g[::-1])]
        sent = lines if after is None else lax.optimization_barrier((lines, after))[0]
        far = lax.ppermute(sent, "gy", [(0, 1), (1, 0)])
        near = lax.ppermute(lines, "gx", pairs)
        if near_first:
            far, near = lax.optimization_barrier((far, near))
        cross = lax.ppermute(far, "gx", pairs)
        return [lines, near, far, cross]
    plane = lax.all_gather(lines, "gy", axis=0, tiled=False)
    plane = lax.all_gather(plane, "gx", axis=0, tiled=False, axis_index_groups=groups)
    return [plane[s, g] for s in range(parts) for g in range(n_y)]


def piece_order(parts):
    n_y = lax.axis_size("gy")
    sub, me = lax.rem(lax.axis_index("gx"), parts), lax.axis_index("gy")
    if n_y == 2 and parts == 2:
        return [(sub, me), (1 - sub, me), (sub, 1 - me), (1 - sub, 1 - me)]
    return [(s, g) for s in range(parts) for g in range(n_y)]


def filter_rows(filter_y, parts):
    width = filter_y.shape[0]
    part = width // parts
    sub = lax.rem(lax.axis_index("gx"), parts)
    return [
        lax.dynamic_slice(filter_y, (sub * part, g * width + s * part), (part, part))
        for s, g in piece_order(parts)
    ]


def send_columns(filter_y, parts):
    width, n_y = filter_y.shape[0], lax.axis_size("gy")
    part = width // parts
    sub, me = lax.rem(lax.axis_index("gx"), parts), lax.axis_index("gy")
    if n_y == 2 and parts == 2:
        sent = lax.dynamic_slice(
            filter_y, (0, (1 - me) * width + sub * part), (width, part)
        )
        return lax.ppermute(sent, "gy", [(0, 1), (1, 0)])
    split = filter_y.reshape(width, n_y, parts, part)
    split = lax.dynamic_index_in_dim(split, sub, axis=2, keepdims=False)
    return lax.all_to_all(split, "gy", 1, 0, tiled=True)


def filter_columns(filter_y, got, parts):
    width, n_y = filter_y.shape[0], lax.axis_size("gy")
    part = width // parts
    sub, me = lax.rem(lax.axis_index("gx"), parts), lax.axis_index("gy")
    order = piece_order(parts)
    if n_y == 2 and parts == 2:
        mine = lax.dynamic_slice(filter_y, (0, me * width + sub * part), (width, part))
        return [
            lax.dynamic_slice_in_dim(source, s * part, part, axis=0)
            for source, (s, _) in zip((mine, mine, got, got), order)
        ]
    split = got.reshape(n_y, parts, part, part)
    return [split[g, s] for s, g in order]


def row_halo(first, last):
    n_x = lax.axis_size("gx")
    up = [(i, i + 1) for i in range(n_x - 1)]
    down = [(i + 1, i) for i in range(n_x - 1)]
    return jnp.stack([lax.ppermute(last, "gx", up), lax.ppermute(first, "gx", down)])


def side_halo(first, last):
    n_y, me = lax.axis_size("gy"), lax.axis_index("gy")
    if n_y == 2:
        got = lax.ppermute(jnp.where(me == 0, last, first), "gy", [(0, 1), (1, 0)])
        none = jnp.zeros_like(got)
        return jnp.where(me == 0, none, got), jnp.where(me == 0, got, none)
    up = [(i, i + 1) for i in range(n_y - 1)]
    down = [(i + 1, i) for i in range(n_y - 1)]
    return lax.ppermute(last, "gy", up), lax.ppermute(first, "gy", down)


def per_device(control, innovation, obs_weight, courant_x, courant_y, filter_x, filter_y):
    rows, levels, width = control.shape
    n_x = lax.axis_size("gx")
    parts = n_x // levels
    part = width // parts
    cut, piece = rows // CHUNKS, part // CHUNKS
    spans = [slice(w * piece, (w + 1) * piece) for w in range(CHUNKS)]

    rows_y = filter_rows(filter_y, parts)
    matrix_x = [lax.all_gather(filter_x[:cut], "gx", axis=0, tiled=True)]
    lines = [swap_all(as_lines(control, parts, w)) for w in range(CHUNKS)]
    lines = [l.reshape(n_x * rows, piece) for l in lines]
    lines[-1], filter_x = lax.optimization_barrier((lines[-1], filter_x))
    for h in range(1, CHUNKS):
        share = filter_x[h * cut : (h + 1) * cut]
        matrix_x.append(lax.all_gather(share, "gx", axis=0, tiled=True))
    starts = []
    for h in range(CHUNKS):
        start = 0.0
        for w, span in enumerate(spans):
            smoothed = jnp.dot(matrix_x[h], lines[w], preferred_element_type=F32)
            smoothed = smoothed.astype(BF16).reshape(n_x, cut, piece)
            for plane, matrix in zip(plane_pieces(smoothed, parts), rows_y):
                start = start + jnp.einsum(
                    "brc,kc->brk", plane, matrix[:, span], preferred_element_type=F32
                )
        start = start.astype(BF16)
        if h == CHUNKS - 1:
            start, filter_y = lax.optimization_barrier((start, filter_y))
            columns_y = send_columns(filter_y, parts)
        came = swap_all(start).reshape(levels, parts, cut, part)
        came = came.transpose(2, 0, 1, 3).reshape(cut, levels, width)
        starts.append(came)

    rows_in = row_halo(starts[0][0], starts[-1][-1]).astype(F32)
    before, after = side_halo(
        jnp.concatenate([s[:, :, 0] for s in starts]),
        jnp.concatenate([s[:, :, -1] for s in starts]),
    )
    sides = jnp.stack([before, after], axis=2).astype(F32)
    end_state, flat, row_flux, side_flux = forward(
        starts, rows_in, sides, innovation, obs_weight, courant_x, courant_y
    )
    rows_in = row_halo(row_flux[0], row_flux[1])
    before, after = side_halo(side_flux[:, :, 0], side_flux[:, :, 1])
    sides = jnp.stack([before, after], axis=2)
    flat, columns_y = lax.optimization_barrier((flat, columns_y))
    columns_y = filter_columns(filter_y, columns_y, parts)

    pulled = []
    for w in range(CHUNKS):
        adjoint = swap_all(rim_lines(flat, rows_in, sides, parts, w))
        adjoint = adjoint.reshape(n_x, CHUNKS, cut, piece)
        total = 0.0
        for h in range(CHUNKS):
            total = total + jnp.einsum(
                "ij,ic->jc",
                matrix_x[h],
                adjoint[:, h].reshape(n_x * cut, piece),
                preferred_element_type=F32,
            )
        pulled.append(total.astype(BF16).reshape(n_x, rows, piece))
    gradient = far = None
    for h, (at, end) in enumerate(((0, rows // 4), (rows // 4, rows))):
        carried = 0.0
        for w, span in enumerate(spans):
            last = w == CHUNKS - 1
            held = far if h > 0 and last else None
            planes = plane_pieces(pulled[w][:, at:end], parts, held, h == 0 and last)
            far = planes[-2] if last else far
            for plane, matrix in zip(planes, columns_y):
                carried = carried + jnp.einsum(
                    "brk,kc->brc", plane, matrix[span], preferred_element_type=F32
                )
        carried = swap_all(carried.astype(BF16))
        gradient = add_lines(control, carried, parts, at, gradient)
    return (end_state, gradient)


def solution(mesh):
    placed = (
        P("gx", None, "gy"),
        P("gx", None, "gy"),
        P("gx", None, "gy"),
        P("gx", None, "gy"),
        P("gx", None, "gy"),
        P("gx", None),
        P("gy", None),
    )
    return jax.shard_map(
        per_device,
        mesh=mesh,
        in_specs=placed,
        out_specs=(P("gx", None, "gy"), P("gx", None, "gy")),
        check_vma=False,
    )
```

profile of v0, /device:TPU:9, one launch (start us, length us, event | category | flops | bytes accessed | tf_op | source)
XLA Modules:
  0.0 416.7 jit_solution(16245036347435308933)
XLA Ops:
  7.2 1.7 slice.126
  9.0 4.7 %as_lines.3 = bf16[16,128,256]{2,1,0:T(8,128)(2,1)} custom-call(bf16[128,8,1024]{2,1,0:T(8,128)(2,1)} %control.3), custom_call_target="tpu_custom_call" | custom-call | bytes 4194304 | tf_op jit(solution)/shard_map/as_lines/pallas_call | solution.py:58
  13.7 44.1 %all_to_all.40 = bf16[16,128,256]{2,1,0:T(8,128)(2,1)S(1)} all-to-all(bf16[16,128,256]{2,1,0:T(8,128)(2,1)} %as_lines.3), channel_id=1, replica_groups=mesh['gx'=16,'gy'=2] {'gx'}, dimensions={0} | all-to-all | bytes 2097152 | tf_op jit(solution)/shard_map/all_to_all | solution.py:238
  58.6 4.7 %as_lines.2 = bf16[16,128,256]{2,1,0:T(8,128)(2,1)} custom-call(bf16[128,8,1024]{2,1,0:T(8,128)(2,1)} %control.3), custom_call_target="tpu_custom_call" | custom-call | bytes 4194304 | tf_op jit(solution)/shard_map/as_lines/pallas_call | solution.py:58
  63.2 6.9 %all-to-all-start = ((bf16[16,128,256]{2,1,0:T(8,128)(2,1)}), bf16[16,128,256]{2,1,0:T(8,128)(2,1)S(1)}, u32[]{:S(2)}, u32[]{:S(2)}) async-start(bf16[16,128,256]{2,1,0:T(8,128)(2,1)} %as_lines.2), calls=%async_computation | async-start | bytes 2097152 | tf_op jit(solution)/shard_map/all_to_all | solution.py:238
  70.1 4.3 %all-gather.3.cloned.1.call-done = bf16[1024,2048]{1,0:T(8,128)(2,1)} async-done(((bf16[64,2048]{1,0:T(8,128)(2,1)}), bf16[1024,2048]{1,0:T(8,128)(2,1)}) %all-gather.3.cloned.1.call-update) | async-done | bytes 4194320 | tf_op jit(solution)/shard_map/all_gather | solution.py:332
  74.4 3.5 fusion.8
  79.9 23.5 %all-to-all-done = bf16[16,128,256]{2,1,0:T(8,128)(2,1)S(1)} async-done(((bf16[16,128,256]{2,1,0:T(8,128)(2,1)}), bf16[16,128,256]{2,1,0:T(8,128)(2,1)S(1)}, u32[]{:S(2)}, u32[]{:S(2)}) %all-to-all-start) | async-done | bytes 1048608 | tf_op jit(solution)/shard_map/all_to_all | solution.py:238
  103.4 3.9 convolution_convert_fusion.3
  109.7 11.5 %collective-permute-done.1 = bf16[16,64,256]{2,1,0:T(8,128)(2,1)S(1)} collective-permute-done((bf16[16,64,256]{2,1,0:T(8,128)(2,1)S(1)}, bf16[16,64,256]{2,1,0:T(8,128)(2,1)S(1)}, u32[]{:S(2)}, u32[]{:S(2)}) %collective-permute-start.1) | collective-permute-done | bytes 524320 | tf_op jit(solution)/shard_map/ppermute | solution.py:247
  125.2 1.9 add_convert_fusion.2
  127.1 5.3 %all-to-all-start.2 = ((bf16[16,64,512]{2,1,0:T(8,128)(2,1)}), bf16[16,64,512]{2,1,0:T(8,128)(2,1)S(1)}, u32[]{:S(2)}, u32[]{:S(2)}) async-start(bf16[16,64,512]{2,1,0:T(8,128)(2,1)} %add_convert_fusion.2), calls=%async_computation.2 | async-start | bytes 2097152 | tf_op jit(solution)/shard_map/all_to_all | solution.py:238
  132.4 3.6 convolution_convert_fusion
  140.7 8.5 %collective-permute-done.10 = bf16[16,64,256]{2,1,0:T(8,128)(2,1)S(1)} collective-permute-done((bf16[16,64,256]{2,1,0:T(8,128)(2,1)S(1)}, bf16[16,64,256]{2,1,0:T(8,128)(2,1)S(1)}, u32[]{:S(2)}, u32[]{:S(2)}) %collective-permute-start.10) | collective-permute-done | bytes 524320 | tf_op jit(solution)/shard_map/ppermute | solution.py:247
  149.7 2.0 collective-permute-start.11
  151.7 8.7 %collective-permute-done.7 = bf16[16,64,256]{2,1,0:T(8,128)(2,1)S(1)} collective-permute-done((bf16[16,64,256]{2,1,0:T(8,128)(2,1)S(1)}, bf16[16,64,256]{2,1,0:T(8,128)(2,1)S(1)}, u32[]{:S(2)}, u32[]{:S(2)}) %collective-permute-start.7) | collective-permute-done | bytes 524320 | tf_op jit(solution)/shard_map/ppermute | solution.py:247
  163.6 1.9 add_convert_fusion.1
  165.5 6.0 %all-to-all-start.3 = ((bf16[16,64,512]{2,1,0:T(8,128)(2,1)}), bf16[16,64,512]{2,1,0:T(8,128)(2,1)}, u32[]{:S(2)}, u32[]{:S(2)}) async-start(bf16[16,64,512]{2,1,0:T(8,128)(2,1)} %add_convert_fusion.1), calls=%async_computation.3 | async-start | bytes 2097152 | tf_op jit(solution)/shard_map/all_to_all | solution.py:238
  172.5 2.3 constant_dynamic-slice_fusion
  176.2 20.3 %all-to-all-done.3 = bf16[16,64,512]{2,1,0:T(8,128)(2,1)} async-done(((bf16[16,64,512]{2,1,0:T(8,128)(2,1)}), bf16[16,64,512]{2,1,0:T(8,128)(2,1)}, u32[]{:S(2)}, u32[]{:S(2)}) %all-to-all-start.3) | async-done | bytes 1048608 | tf_op jit(solution)/shard_map/all_to_all | solution.py:238
  196.5 1.8 copy.267
  200.2 1.9 collective-permute-start.13
  202.1 3.6 collective-permute-start.12
  207.5 14.5 %forward.1 = (f32[128,8,1024]{2,1,0:T(8,128)}, f32[128,8,1024]{2,1,0:T(8,128)}, f32[2,8,1024]{2,1,0:T(8,128)}, f32[128,8,2]{2,1,0:T(8,128)}) custom-call(bf16[64,8,1024]{2,1,0:T(8,128)(2,1)} %bitcast.181, bf16[64,8,1024]{2,1,0:T(8,128)(2,1)} %bitcast.184, f32[2,8,1024]{2,1,0:T(8,128)} %maximum_convert_fusion.refs_2_, f32[128,8,2]{2,1,0:T(8,128)} %copy.249.refs_3_, ...), custom_call_target="tpu_custom_call" | custom-call | flops 31457280 | bytes 29360128 | tf_op jit(solution)/shard_map/forward/pallas_call | solution.py:167
  224.6 3.5 collective-permute-start.17
  228.2 2.6 collective-permute-start.16
  232.5 5.7 %rim_lines.3 = bf16[16,128,256]{2,1,0:T(8,128)(2,1)} custom-call(f32[128,8,1024]{2,1,0:T(8,128)} %get-tuple-element.21.flat, f32[2,8,1024]{2,1,0:T(8,128)} %pad_maximum_fusion.rows_in, f32[128,8,2]{2,1,0:T(8,128)} %copy.251.sides), custom_call_target="tpu_custom_call" | custom-call | flops 4194304 | bytes 8388608 | tf_op jit(solution)/shard_map/rim_lines/pallas_call | solution.py:220
  238.2 7.9 %all-to-all-start.5 = ((bf16[16,128,256]{2,1,0:T(8,128)(2,1)}), bf16[16,128,256]{2,1,0:T(8,128)(2,1)S(1)}, u32[]{:S(2)}, u32[]{:S(2)}) async-start(bf16[16,128,256]{2,1,0:T(8,128)(2,1)} %rim_lines.3), calls=%async_computation.5 | async-start | bytes 2097152 | tf_op jit(solution)/shard_map/all_to_all | solution.py:238
  246.1 5.8 %rim_lines.2 = bf16[16,128,256]{2,1,0:T(8,128)(2,1)} custom-call(f32[128,8,1024]{2,1,0:T(8,128)} %get-tuple-element.21.flat, f32[2,8,1024]{2,1,0:T(8,128)} %pad_maximum_fusion.rows_in, f32[128,8,2]{2,1,0:T(8,128)} %copy.251.sides), custom_call_target="tpu_custom_call" | custom-call | flops 4194304 | bytes 8388608 | tf_op jit(solution)/shard_map/rim_lines/pallas_call | solution.py:220
  251.9 19.1 %all-to-all-done.5 = bf16[16,128,256]{2,1,0:T(8,128)(2,1)S(1)} async-done(((bf16[16,128,256]{2,1,0:T(8,128)(2,1)}), bf16[16,128,256]{2,1,0:T(8,128)(2,1)S(1)}, u32[]{:S(2)}, u32[]{:S(2)}) %all-to-all-start.5) | async-done | bytes 1048608 | tf_op jit(solution)/shard_map/all_to_all | solution.py:238
  271.0 5.0 %all-to-all-start.4 = ((bf16[16,128,256]{2,1,0:T(8,128)(2,1)}), bf16[16,128,256]{2,1,0:T(8,128)(2,1)S(1)}, u32[]{:S(2)}, u32[]{:S(2)}) async-start(bf16[16,128,256]{2,1,0:T(8,128)(2,1)} %rim_lines.2), calls=%async_computation.4 | async-start | bytes 2097152 | tf_op jit(solution)/shard_map/all_to_all | solution.py:238
  276.0 3.6 fusion.51
  284.3 16.5 %all-to-all-done.4 = bf16[16,128,256]{2,1,0:T(8,128)(2,1)S(1)} async-done(((bf16[16,128,256]{2,1,0:T(8,128)(2,1)}), bf16[16,128,256]{2,1,0:T(8,128)(2,1)S(1)}, u32[]{:S(2)}, u32[]{:S(2)}) %all-to-all-start.4) | async-done | bytes 1048608 | tf_op jit(solution)/shard_map/all_to_all | solution.py:238
  300.9 3.6 fusion.50
  308.7 1.9 fusion.29
  310.6 3.4 fusion.32
  325.0 2.2 fusion.7
  327.2 5.9 %all-to-all-start.7 = ((bf16[16,32,512]{2,1,0:T(8,128)(2,1)}), bf16[16,32,512]{2,1,0:T(8,128)(2,1)}, u32[]{:S(2)}, u32[]{:S(2)}) async-start(bf16[16,32,512]{2,1,0:T(8,128)(2,1)} %fusion.7), calls=%async_computation.7 | async-start | bytes 1048576 | tf_op jit(solution)/shard_map/all_to_all | solution.py:238
  333.1 3.8 collective-permute-done.20
  338.1 1.7 fusion.9
  339.8 1.9 fusion.33
  341.8 12.0 %collective-permute-done.25 = bf16[16,96,256]{2,1,0:T(8,128)(2,1)} collective-permute-done((bf16[16,96,256]{2,1,0:T(8,128)(2,1)}, bf16[16,96,256]{2,1,0:T(8,128)(2,1)}, u32[]{:S(2)}, u32[]{:S(2)}) %collective-permute-start.25) | collective-permute-done | bytes 786464 | tf_op jit(solution)/shard_map/ppermute | solution.py:247
  354.5 1.9 fusion.30
  360.1 2.6 add_convert_fusion
  362.7 4.9 %all-to-all-start.6 = ((bf16[16,96,512]{2,1,0:T(8,128)(2,1)}), bf16[16,96,512]{2,1,0:T(8,128)(2,1)S(1)}, u32[]{:S(2)}, u32[]{:S(2)}) async-start(bf16[16,96,512]{2,1,0:T(8,128)(2,1)} %add_convert_fusion), calls=%async_computation.6 | async-start | bytes 3145728 | tf_op jit(solution)/shard_map/all_to_all | solution.py:238
  367.5 2.3 add_lines.2.rest_0_
  369.8 33.2 %all-to-all-done.6.lines = bf16[16,96,512]{2,1,0:T(8,128)(2,1)S(1)} async-done(((bf16[16,96,512]{2,1,0:T(8,128)(2,1)}), bf16[16,96,512]{2,1,0:T(8,128)(2,1)S(1)}, u32[]{:S(2)}, u32[]{:S(2)}) %all-to-all-start.6) | async-done | bytes 1572896 | tf_op jit(solution)/shard_map/all_to_all | solution.py:238
  404.2 5.7 %add_lines.3 = f32[128,8,1024]{2,1,0:T(8,128)} custom-call(bf16[16,96,512]{2,1,0:T(8,128)(2,1)} %copy-done.7, bf16[128,8,1024]{2,1,0:T(8,128)(2,1)} %control.3, f32[128,8,1024]{2,1,0:T(8,128)} %add_lines.2.rest_0_), custom_call_target="tpu_custom_call", output_to_operand_aliasing={{}: (2, {})} | custom-call | flops 524288 | bytes 4194304 | tf_op jit(solution)/shard_map/add_lines/pallas_call | solution.py:87
  (154 shorter events, 54.3 us)
Async XLA Ops:
  7.2 50.7 %copy-start.15 = (bf16[128,2048]{1,0:T(8,128)(2,1)S(1)}, bf16[128,2048]{1,0:T(8,128)(2,1)}, u32[]{:S(2)}) copy-start(bf16[128,2048]{1,0:T(8,128)(2,1)} %param.12) | copy-start | bytes 1572868
  7.2 67.2 %all-gather.3.cloned.1.call-start = ((), (), s32[]{:S(2)}) async-start(), calls=%async_computation.8 | async-start | bytes 4456448 | tf_op jit(solution)/shard_map/all_gather | solution.py:332
  9.0 123.4 %all-gather.5.cloned.1.call-start = ((), (), s32[]{:S(2)}) async-start(), calls=%async_computation.9 | async-start | bytes 4456448 | tf_op jit(solution)/shard_map/all_gather | solution.py:338
  63.2 40.1 %all-to-all-start = ((bf16[16,128,256]{2,1,0:T(8,128)(2,1)}), bf16[16,128,256]{2,1,0:T(8,128)(2,1)S(1)}, u32[]{:S(2)}, u32[]{:S(2)}) async-start(bf16[16,128,256]{2,1,0:T(8,128)(2,1)} %as_lines.2), calls=%async_computation | async-start | bytes 2097152 | tf_op jit(solution)/shard_map/all_to_all | solution.py:238
  78.1 43.6 %collective-permute-start.4 = (bf16[16,64,256]{2,1,0:T(8,128)(2,1)S(1)}, bf16[16,64,256]{2,1,0:T(8,128)(2,1)S(1)}, u32[]{:S(2)}, u32[]{:S(2)}) collective-permute-start(bf16[16,64,256]{2,1,0:T(8,128)(2,1)S(1)} %bitcast.188), channel_id=1, source_target_pairs={{0,1},{1,0},{2,3},{3,2},{4,5},{5,4},{6,7},{7,6},{8,9},{9,8},{10,11... | collective-permute-start | bytes 1572872 | tf_op jit(solution)/shard_map/ppermute | solution.py:247
  79.4 43.8 %collective-permute-start.3 = (bf16[16,64,256]{2,1,0:T(8,128)(2,1)S(1)}, bf16[16,64,256]{2,1,0:T(8,128)(2,1)}, u32[]{:S(2)}, u32[]{:S(2)}) collective-permute-start(bf16[16,64,256]{2,1,0:T(8,128)(2,1)S(1)} %bitcast.189), channel_id=1, source_target_pairs={{0,2},{2,0},{4,6},{6,4},{8,10},{10,8},{12,14},{14,12},{16,18},{18,... | collective-permute-start | bytes 1572872 | tf_op jit(solution)/shard_map/ppermute | solution.py:248
  107.2 13.9 %collective-permute-start.1 = (bf16[16,64,256]{2,1,0:T(8,128)(2,1)S(1)}, bf16[16,64,256]{2,1,0:T(8,128)(2,1)S(1)}, u32[]{:S(2)}, u32[]{:S(2)}) collective-permute-start(bf16[16,64,256]{2,1,0:T(8,128)(2,1)S(1)} %bitcast.201), channel_id=1, source_target_pairs={{0,1},{1,0},{2,3},{3,2},{4,5},{5,4},{6,7},{7,6},{8,9},{9,8},{10,11... | collective-permute-start | bytes 1572872 | tf_op jit(solution)/shard_map/ppermute | solution.py:247
  108.7 14.0 %collective-permute-start = (bf16[16,64,256]{2,1,0:T(8,128)(2,1)S(1)}, bf16[16,64,256]{2,1,0:T(8,128)(2,1)S(1)}, u32[]{:S(2)}, u32[]{:S(2)}) collective-permute-start(bf16[16,64,256]{2,1,0:T(8,128)(2,1)S(1)} %bitcast.202), channel_id=1, source_target_pairs={{0,2},{2,0},{4,6},{6,4},{8,10},{10,8},{12,14},{14,12},{16,18},{18,... | collective-permute-start | bytes 1572872 | tf_op jit(solution)/shard_map/ppermute | solution.py:248
  121.2 3.5 collective-permute-start.2
  121.7 3.5 collective-permute-start.5
  127.1 38.4 %all-to-all-start.2 = ((bf16[16,64,512]{2,1,0:T(8,128)(2,1)}), bf16[16,64,512]{2,1,0:T(8,128)(2,1)S(1)}, u32[]{:S(2)}, u32[]{:S(2)}) async-start(bf16[16,64,512]{2,1,0:T(8,128)(2,1)} %add_convert_fusion.2), calls=%async_computation.2 | async-start | bytes 2097152 | tf_op jit(solution)/shard_map/all_to_all | solution.py:238
  132.3 5.7 %copy-start.14 = (bf16[16,128,256]{2,1,0:T(8,128)(2,1)S(1)}, bf16[16,128,256]{2,1,0:T(8,128)(2,1)}, u32[]{:S(2)}) copy-start(bf16[16,128,256]{2,1,0:T(8,128)(2,1)} %copy-done.13) | copy-start | bytes 3145732
  136.0 13.2 %collective-permute-start.10 = (bf16[16,64,256]{2,1,0:T(8,128)(2,1)S(1)}, bf16[16,64,256]{2,1,0:T(8,128)(2,1)S(1)}, u32[]{:S(2)}, u32[]{:S(2)}) collective-permute-start(bf16[16,64,256]{2,1,0:T(8,128)(2,1)S(1)} %bitcast.195), channel_id=1, source_target_pairs={{0,1},{1,0},{2,3},{3,2},{4,5},{5,4},{6,7},{7,6},{8,9},{9,8},{10,11... | collective-permute-start | bytes 1572872 | tf_op jit(solution)/shard_map/ppermute | solution.py:247
  137.4 24.7 %collective-permute-start.9 = (bf16[16,64,256]{2,1,0:T(8,128)(2,1)S(1)}, bf16[16,64,256]{2,1,0:T(8,128)(2,1)S(1)}, u32[]{:S(2)}, u32[]{:S(2)}) collective-permute-start(bf16[16,64,256]{2,1,0:T(8,128)(2,1)S(1)} %bitcast.196), channel_id=1, source_target_pairs={{0,2},{2,0},{4,6},{6,4},{8,10},{10,8},{12,14},{14,12},{16,18},{18,... | collective-permute-start | bytes 1572872 | tf_op jit(solution)/shard_map/ppermute | solution.py:248
  139.3 21.1 %collective-permute-start.7 = (bf16[16,64,256]{2,1,0:T(8,128)(2,1)S(1)}, bf16[16,64,256]{2,1,0:T(8,128)(2,1)S(1)}, u32[]{:S(2)}, u32[]{:S(2)}) collective-permute-start(bf16[16,64,256]{2,1,0:T(8,128)(2,1)S(1)} %bitcast.198), channel_id=1, source_target_pairs={{0,1},{1,0},{2,3},{3,2},{4,5},{5,4},{6,7},{7,6},{8,9},{9,8},{10,11... | collective-permute-start | bytes 1572872 | tf_op jit(solution)/shard_map/ppermute | solution.py:247
  139.5 23.1 %collective-permute-start.6 = (bf16[16,64,256]{2,1,0:T(8,128)(2,1)S(1)}, bf16[16,64,256]{2,1,0:T(8,128)(2,1)S(1)}, u32[]{:S(2)}, u32[]{:S(2)}) collective-permute-start(bf16[16,64,256]{2,1,0:T(8,128)(2,1)S(1)} %bitcast.199), channel_id=1, source_target_pairs={{0,2},{2,0},{4,6},{6,4},{8,10},{10,8},{12,14},{14,12},{16,18},{18,... | collective-permute-start | bytes 1572872 | tf_op jit(solution)/shard_map/ppermute | solution.py:248
  149.7 14.0 %collective-permute-start.11 = (bf16[16,64,256]{2,1,0:T(8,128)(2,1)S(1)}, bf16[16,64,256]{2,1,0:T(8,128)(2,1)S(1)}, u32[]{:S(2)}, u32[]{:S(2)}) collective-permute-start(bf16[16,64,256]{2,1,0:T(8,128)(2,1)S(1)} %collective-permute-done.10), channel_id=1, source_target_pairs={{0,2},{2,0},{4,6},{6,4},{8,10},{10,8},{12,14},{14,12},{16,18},{18,... | collective-permute-start | bytes 1572872 | tf_op jit(solution)/shard_map/ppermute | solution.py:251
  160.4 2.7 collective-permute-start.8
  165.5 31.0 %all-to-all-start.3 = ((bf16[16,64,512]{2,1,0:T(8,128)(2,1)}), bf16[16,64,512]{2,1,0:T(8,128)(2,1)}, u32[]{:S(2)}, u32[]{:S(2)}) async-start(bf16[16,64,512]{2,1,0:T(8,128)(2,1)} %add_convert_fusion.1), calls=%async_computation.3 | async-start | bytes 2097152 | tf_op jit(solution)/shard_map/all_to_all | solution.py:238
  172.1 34.7 %copy-start.8 = (bf16[8,2,64,512]{3,0,1,2:T(8,128)(2,1)}, bf16[8,2,64,512]{3,0,1,2:T(8,128)(2,1)S(1)}, u32[]{:S(2)}) copy-start(bf16[8,2,64,512]{3,0,1,2:T(8,128)(2,1)S(1)} %copy.268) | copy-start | bytes 3145732
  174.8 49.8 %collective-permute-start.15 = (bf16[1024,512]{1,0:T(8,128)(2,1)}, bf16[1024,512]{1,0:T(8,128)(2,1)S(1)}, u32[]{:S(2)}, u32[]{:S(2)}) collective-permute-start(bf16[1024,512]{1,0:T(8,128)(2,1)} %constant_dynamic-slice_fusion), channel_id=1, source_target_pairs={{0,1},{1,0},{2,3},{3,2},{4,5},{5,4},{6,7},{7,6},{8,9},{9,8},{10,11... | collective-permute-start | bytes 3145736 | tf_op jit(solution)/shard_map/ppermute | solution.py:284
  198.3 9.2 %copy-start.9 = (bf16[8,2,64,512]{3,0,1,2:T(8,128)(2,1)}, bf16[8,2,64,512]{3,0,1,2:T(8,128)(2,1)S(1)}, u32[]{:S(2)}) copy-start(bf16[8,2,64,512]{3,0,1,2:T(8,128)(2,1)S(1)} %copy.267) | copy-start | bytes 3145732
  198.8 6.9 %collective-permute-start.14 = (bf16[128,8]{0,1:T(8,128)(2,1)S(1)}, bf16[128,8]{0,1:T(8,128)(2,1)S(1)}, u32[]{:S(2)}, u32[]{:S(2)}) collective-permute-start(bf16[128,8]{0,1:T(8,128)(2,1)S(1)} %maximum_select_fusion), channel_id=1, source_target_pairs={{0,1},{1,0},{2,3},{3,2},{4,5},{5,4},{6,7},{7,6},{8,9},{9,8},{10,11... | collective-permute-start | bytes 6152 | tf_op jit(solution)/shard_map/ppermute | solution.py:315
  200.2 6.7 %collective-permute-start.13 = (bf16[8,1024]{1,0:T(8,128)(2,1)S(1)}, bf16[8,1024]{1,0:T(8,128)(2,1)S(1)}, u32[]{:S(2)}, u32[]{:S(2)}) collective-permute-start(bf16[8,1024]{1,0:T(8,128)(2,1)S(1)} %bitcast.210), channel_id=1, source_target_pairs={{2,0},{4,2},{6,4},{8,6},{10,8},{12,10},{14,12},{16,14},{18,16},{20... | collective-permute-start | bytes 49160 | tf_op jit(solution)/shard_map/ppermute | solution.py:309
  202.1 4.7 %collective-permute-start.12 = (bf16[8,1024]{1,0:T(8,128)(2,1)S(1)}, bf16[8,1024]{1,0:T(8,128)(2,1)S(1)}, u32[]{:S(2)}, u32[]{:S(2)}) collective-permute-start(bf16[8,1024]{1,0:T(8,128)(2,1)S(1)} %bitcast.211), channel_id=1, source_target_pairs={{0,2},{2,4},{4,6},{6,8},{8,10},{10,12},{12,14},{14,16},{16,18},{18... | collective-permute-start | bytes 49160 | tf_op jit(solution)/shard_map/ppermute | solution.py:309
  223.6 7.1 %collective-permute-start.18 = (f32[128,8]{0,1:T(8,128)S(1)}, f32[128,8]{0,1:T(8,128)S(1)}, u32[]{:S(2)}, u32[]{:S(2)}) collective-permute-start(f32[128,8]{0,1:T(8,128)S(1)} %bitcast.218), channel_id=1, source_target_pairs={{0,1},{1,0},{2,3},{3,2},{4,5},{5,4},{6,7},{7,6},{8,9},{9,8},{10,11... | collective-permute-start | bytes 12296 | tf_op jit(solution)/shard_map/ppermute | solution.py:315
  224.6 13.6 %copy-start.10 = (bf16[1024,512]{1,0:T(8,128)(2,1)}, bf16[1024,512]{1,0:T(8,128)(2,1)S(1)}, u32[]{:S(2)}) copy-start(bf16[1024,512]{1,0:T(8,128)(2,1)S(1)} %collective-permute-done.15) | copy-start | bytes 3145732
  224.6 7.3 %collective-permute-start.17 = (f32[8,1024]{1,0:T(8,128)S(1)}, f32[8,1024]{1,0:T(8,128)S(1)}, u32[]{:S(2)}, u32[]{:S(2)}) collective-permute-start(f32[8,1024]{1,0:T(8,128)S(1)} %get-tuple-element.41), channel_id=1, source_target_pairs={{2,0},{4,2},{6,4},{8,6},{10,8},{12,10},{14,12},{16,14},{18,16},{20... | collective-permute-start | bytes 98312 | tf_op jit(solution)/shard_map/ppermute | solution.py:309
  228.2 3.7 collective-permute-start.16
  238.2 32.8 %all-to-all-start.5 = ((bf16[16,128,256]{2,1,0:T(8,128)(2,1)}), bf16[16,128,256]{2,1,0:T(8,128)(2,1)S(1)}, u32[]{:S(2)}, u32[]{:S(2)}) async-start(bf16[16,128,256]{2,1,0:T(8,128)(2,1)} %rim_lines.3), calls=%async_computation.5 | async-start | bytes 2097152 | tf_op jit(solution)/shard_map/all_to_all | solution.py:238
  271.0 29.8 %all-to-all-start.4 = ((bf16[16,128,256]{2,1,0:T(8,128)(2,1)}), bf16[16,128,256]{2,1,0:T(8,128)(2,1)S(1)}, u32[]{:S(2)}, u32[]{:S(2)}) async-start(bf16[16,128,256]{2,1,0:T(8,128)(2,1)} %rim_lines.2), calls=%async_computation.4 | async-start | bytes 2097152 | tf_op jit(solution)/shard_map/all_to_all | solution.py:238
  281.5 23.0 %copy-start.3 = (bf16[2048,256]{1,0:T(8,128)(2,1)}, bf16[2048,256]{1,0:T(8,128)(2,1)S(1)}, u32[]{:S(2)}) copy-start(bf16[2048,256]{1,0:T(8,128)(2,1)S(1)} %copy.262) | copy-start | bytes 3145732
  282.3 36.6 %collective-permute-start.23 = (bf16[16,32,256]{2,1,0:T(8,128)(2,1)}, bf16[16,32,256]{2,1,0:T(8,128)(2,1)}, u32[]{:S(2)}, u32[]{:S(2)}) collective-permute-start(bf16[16,32,256]{2,1,0:T(8,128)(2,1)} %slice.174), channel_id=1, source_target_pairs={{0,1},{1,0},{2,3},{3,2},{4,5},{5,4},{6,7},{7,6},{8,9},{9,8},{10,11... | collective-permute-start | bytes 786440 | tf_op jit(solution)/shard_map/ppermute | solution.py:247
  283.6 35.7 %collective-permute-start.24 = (bf16[16,32,256]{2,1,0:T(8,128)(2,1)}, bf16[16,32,256]{2,1,0:T(8,128)(2,1)S(1)}, u32[]{:S(2)}, u32[]{:S(2)}) collective-permute-start(bf16[16,32,256]{2,1,0:T(8,128)(2,1)} %slice.174), channel_id=1, source_target_pairs={{0,2},{2,0},{4,6},{6,4},{8,10},{10,8},{12,14},{14,12},{16,18},{18,... | collective-permute-start | bytes 786440 | tf_op jit(solution)/shard_map/ppermute | solution.py:248
  306.4 13.1 %collective-permute-start.27 = (bf16[16,32,256]{2,1,0:T(8,128)(2,1)S(1)}, bf16[16,32,256]{2,1,0:T(8,128)(2,1)S(1)}, u32[]{:S(2)}, u32[]{:S(2)}) collective-permute-start(bf16[16,32,256]{2,1,0:T(8,128)(2,1)S(1)} %slice.175), channel_id=1, source_target_pairs={{0,2},{2,0},{4,6},{6,4},{8,10},{10,8},{12,14},{14,12},{16,18},{18,... | collective-permute-start | bytes 786440 | tf_op jit(solution)/shard_map/ppermute | solution.py:248
  307.3 12.5 %collective-permute-start.28 = (bf16[16,32,256]{2,1,0:T(8,128)(2,1)S(1)}, bf16[16,32,256]{2,1,0:T(8,128)(2,1)S(1)}, u32[]{:S(2)}, u32[]{:S(2)}) collective-permute-start(bf16[16,32,256]{2,1,0:T(8,128)(2,1)S(1)} %slice.175), channel_id=1, source_target_pairs={{0,1},{1,0},{2,3},{3,2},{4,5},{5,4},{6,7},{7,6},{8,9},{9,8},{10,11... | collective-permute-start | bytes 786440 | tf_op jit(solution)/shard_map/ppermute | solution.py:247
  310.6 5.8 %copy-start.6 = (bf16[2048,256]{1,0:T(8,128)(2,1)S(1)}, bf16[2048,256]{1,0:T(8,128)(2,1)}, u32[]{:S(2)}) copy-start(bf16[2048,256]{1,0:T(8,128)(2,1)} %copy-done.5) | copy-start | bytes 3145732
  317.4 19.5 %collective-permute-start.20 = (bf16[16,96,256]{2,1,0:T(8,128)(2,1)}, bf16[16,96,256]{2,1,0:T(8,128)(2,1)}, u32[]{:S(2)}, u32[]{:S(2)}) collective-permute-start(bf16[16,96,256]{2,1,0:T(8,128)(2,1)} %slice.170), channel_id=1, source_target_pairs={{0,1},{1,0},{2,3},{3,2},{4,5},{5,4},{6,7},{7,6},{8,9},{9,8},{10,11... | collective-permute-start | bytes 2359304 | tf_op jit(solution)/shard_map/ppermute | solution.py:247
  318.9 35.7 %collective-permute-start.19 = (bf16[16,96,256]{2,1,0:T(8,128)(2,1)}, bf16[16,96,256]{2,1,0:T(8,128)(2,1)}, u32[]{:S(2)}, u32[]{:S(2)}) collective-permute-start(bf16[16,96,256]{2,1,0:T(8,128)(2,1)} %slice.170), channel_id=1, source_target_pairs={{0,2},{2,0},{4,6},{6,4},{8,10},{10,8},{12,14},{14,12},{16,18},{18,... | collective-permute-start | bytes 2359304 | tf_op jit(solution)/shard_map/ppermute | solution.py:248
  319.3 20.5 %collective-permute-start.22 = (bf16[16,96,256]{2,1,0:T(8,128)(2,1)}, bf16[16,96,256]{2,1,0:T(8,128)(2,1)}, u32[]{:S(2)}, u32[]{:S(2)}) collective-permute-start(bf16[16,96,256]{2,1,0:T(8,128)(2,1)} %slice.173), channel_id=1, source_target_pairs={{0,2},{2,0},{4,6},{6,4},{8,10},{10,8},{12,14},{14,12},{16,18},{18,... | collective-permute-start | bytes 2359304 | tf_op jit(solution)/shard_map/ppermute | solution.py:248
  319.4 5.2 %collective-permute-start.30 = (bf16[16,32,256]{2,1,0:T(8,128)(2,1)}, bf16[16,32,256]{2,1,0:T(8,128)(2,1)S(1)}, u32[]{:S(2)}, u32[]{:S(2)}) collective-permute-start(bf16[16,32,256]{2,1,0:T(8,128)(2,1)} %collective-permute-done.23), channel_id=1, source_target_pairs={{0,2},{2,0},{4,6},{6,4},{8,10},{10,8},{12,14},{14,12},{16,18},{18,... | collective-permute-start | bytes 786440 | tf_op jit(solution)/shard_map/ppermute | solution.py:251
  319.8 3.1 collective-permute-start.29
  323.0 30.8 %collective-permute-start.25 = (bf16[16,96,256]{2,1,0:T(8,128)(2,1)}, bf16[16,96,256]{2,1,0:T(8,128)(2,1)}, u32[]{:S(2)}, u32[]{:S(2)}) collective-permute-start(bf16[16,96,256]{2,1,0:T(8,128)(2,1)} %slice.173), channel_id=1, source_target_pairs={{0,1},{1,0},{2,3},{3,2},{4,5},{5,4},{6,7},{7,6},{8,9},{9,8},{10,11... | collective-permute-start | bytes 2359304 | tf_op jit(solution)/shard_map/ppermute | solution.py:247
  327.2 35.4 %all-to-all-start.7 = ((bf16[16,32,512]{2,1,0:T(8,128)(2,1)}), bf16[16,32,512]{2,1,0:T(8,128)(2,1)}, u32[]{:S(2)}, u32[]{:S(2)}) async-start(bf16[16,32,512]{2,1,0:T(8,128)(2,1)} %fusion.7), calls=%async_computation.7 | async-start | bytes 1048576 | tf_op jit(solution)/shard_map/all_to_all | solution.py:238
  336.9 21.3 %collective-permute-start.21 = (bf16[16,96,256]{2,1,0:T(8,128)(2,1)}, bf16[16,96,256]{2,1,0:T(8,128)(2,1)S(1)}, u32[]{:S(2)}, u32[]{:S(2)}) collective-permute-start(bf16[16,96,256]{2,1,0:T(8,128)(2,1)} %collective-permute-done.20), channel_id=1, source_target_pairs={{0,2},{2,0},{4,6},{6,4},{8,10},{10,8},{12,14},{14,12},{16,18},{18,... | collective-permute-start | bytes 2359304 | tf_op jit(solution)/shard_map/ppermute | solution.py:251
  341.8 14.7 %copy-start.12 = (bf16[1024,512]{1,0:T(8,128)(2,1)S(1)}, bf16[1024,512]{1,0:T(8,128)(2,1)}, u32[]{:S(2)}) copy-start(bf16[1024,512]{1,0:T(8,128)(2,1)} %copy-done.10) | copy-start | bytes 3145732
  353.7 5.0 %collective-permute-start.26 = (bf16[16,96,256]{2,1,0:T(8,128)(2,1)}, bf16[16,96,256]{2,1,0:T(8,128)(2,1)S(1)}, u32[]{:S(2)}, u32[]{:S(2)}) collective-permute-start(bf16[16,96,256]{2,1,0:T(8,128)(2,1)} %collective-permute-done.25), channel_id=1, source_target_pairs={{0,2},{2,0},{4,6},{6,4},{8,10},{10,8},{12,14},{14,12},{16,18},{18,... | collective-permute-start | bytes 2359304 | tf_op jit(solution)/shard_map/ppermute | solution.py:251
  362.7 40.3 %all-to-all-start.6 = ((bf16[16,96,512]{2,1,0:T(8,128)(2,1)}), bf16[16,96,512]{2,1,0:T(8,128)(2,1)S(1)}, u32[]{:S(2)}, u32[]{:S(2)}) async-start(bf16[16,96,512]{2,1,0:T(8,128)(2,1)} %add_convert_fusion), calls=%async_computation.6 | async-start | bytes 3145728 | tf_op jit(solution)/shard_map/all_to_all | solution.py:238
  (11 other events, 39.3 us)
Sparse Core Ops, SparseCore 0:
  10.7 63.5 all-gather.2
  76.5 54.8 all-gather.4
where the time goes:
time: 419 us; the launch traced here: 417 us
  waiting for transfers between devices  161 us (38%)
  starting transfers between devices  73.9 us (18%)
  matrix products  57.9 us (14%)
  blocking collectives  44.1 us (11%)
  Pallas kernels  43.4 us (10%)
  local copies, waits for them, and re-layouts  18.5 us (4%)
  between operations  14.7 us (4%)
    all_to_all x7, waiting for transfers between devices, swap_all(): return lax.all_to_all(lines, 'gx', 0, 0, tiled=True)  113 us
    ppermute x8, waiting for transfers between devices, plane_pieces(): far = lax.ppermute(sent, 'gy', [(0, 1), (1, 0)])  44.4 us
    all_to_all x1, blocking collectives, swap_all(): return lax.all_to_all(lines, 'gx', 0, 0, tiled=True)  44.1 us
    all_to_all x7, starting transfers between devices, swap_all(): return lax.all_to_all(lines, 'gx', 0, 0, tiled=True)  41.8 us
    dot_general x16, matrix products, per_device(): jnp.einsum('brk,kc->brc', plane, matrix[span], preferred_element_type=F32)  24.4 us
    pallas_call x1, Pallas kernels, forward(): pl.pallas_call(forward_body, grid=(rows // STEP,), in_specs=[start] * CHU...  14.5 us
    dot_general x4, matrix products, per_device(): smoothed = jnp.dot(matrix_x[h], lines[w], preferred_element_type=F32)  12.2 us
    dot_general x16, matrix products, per_device(): jnp.einsum('brc,kc->brk', plane, matrix[:, span], preferred_element_type=...  11.5 us
  transfers between devices with their start and end apart: 40, of which 12 were waited for; matrix products, arithmetic and copies ran while one was open for 18% of the time, Pallas kernels for 8%

commit v1 on v0

--- a/solution.py
+++ b/solution.py
@@ -72,23 +72,29 @@
     out, turned = rest[-2:]
     levels, width = control.shape[1:]
     part = width // parts
-    for l in range(levels):
-        for s in range(parts):
-            turned[:, l, s * part : (s + 1) * part] = lines[l * parts + s].astype(F32)
+
+    @pl.loop(0, STEP // TILE)
+    def _(tile):
+        at = pl.ds(tile * TILE, TILE)
+        for l in range(levels):
+            for s in range(parts):
+                got = lines[l * parts + s, at].astype(F32)
+                turned[at, l, s * part : (s + 1) * part] = got
+
     out[...] = control[...].astype(F32) + turned[...]
 
 
 def add_lines(control, lines, parts, first, target):
     rows, levels, width = control.shape
-    whole = (TILE, levels, width)
+    whole = (STEP, levels, width)
     cut = lines.shape[1]
-    offset = first // TILE
+    offset = first // STEP
     operands = [lines, control] + ([] if target is None else [target])
     return pl.pallas_call(
         functools.partial(gradient_body, parts),
-        grid=(cut // TILE,),
+        grid=(cut // STEP,),
         in_specs=[
-            pl.BlockSpec((lines.shape[0], TILE, lines.shape[2]), lambda i: (0, i, 0)),
+            pl.BlockSpec((lines.shape[0], STEP, lines.shape[2]), lambda i: (0, i, 0)),
             pl.BlockSpec(whole, lambda i: (i + offset, 0, 0)),
         ]
         + [pl.BlockSpec(memory_space=pl.ANY)] * (len(operands) - 2),
@@ -383,7 +389,8 @@
             )
         pulled.append(total.astype(BF16).reshape(n_x, rows, piece))
     gradient = far = None
-    for h, (at, end) in enumerate(((0, rows // 4), (rows // 4, rows))):
+    for h in range(CHUNKS):
+        at, end = h * cut, (h + 1) * cut
         carried = 0.0
         for w, span in enumerate(spans):
             last = w == CHUNKS - 1

time: 419 us -> 408 us (0.974)
  waiting for transfers between devices: 161 us -> 152 us
    ppermute x8, waiting for transfers between devices: 44.4 us -> 36.4 us  [plane_pieces(): far = lax.ppermute(sent, 'gy', [(0, 1), (1, 0)])]
  transfers between devices with their start and end apart: 40 -> 40, of which waited for: 12 -> 14; matrix products, arithmetic and copies ran while one was open for 18% -> 19% of each run, Pallas kernels for 8% -> 8%
where the time goes in v1:
time: 408 us; the launch traced here: 406 us
  waiting for transfers between devices  152 us (37%)
  starting transfers between devices  73 us (18%)
  matrix products  59.9 us (15%)
  blocking collectives  44.1 us (11%)
  Pallas kernels  41.4 us (10%)
  local copies, waits for them, and re-layouts  18.6 us (5%)
  between operations  14.6 us (4%)
    all_to_all x7, waiting for transfers between devices, swap_all(): return lax.all_to_all(lines, 'gx', 0, 0, tiled=True)  109 us
    all_to_all x1, blocking collectives, swap_all(): return lax.all_to_all(lines, 'gx', 0, 0, tiled=True)  44.1 us
    all_to_all x7, starting transfers between devices, swap_all(): return lax.all_to_all(lines, 'gx', 0, 0, tiled=True)  40.2 us
    ppermute x8, waiting for transfers between devices, plane_pieces(): far = lax.ppermute(sent, 'gy', [(0, 1), (1, 0)])  36.4 us
    dot_general x16, matrix products, per_device(): jnp.einsum('brk,kc->brc', plane, matrix[span], preferred_element_type=F32)  23.8 us
    pallas_call x1, Pallas kernels, forward(): pl.pallas_call(forward_body, grid=(rows // STEP,), in_specs=[start] * CHU...  14.6 us
    dot_general x16, matrix products, per_device(): jnp.einsum('brc,kc->brk', plane, matrix[:, span], preferred_element_type=...  12.5 us
    dot_general x4, matrix products, per_device(): smoothed = jnp.dot(matrix_x[h], lines[w], preferred_element_type=F32)  11.9 us
  transfers between devices with their start and end apart: 40, of which 14 were waited for; matrix products, arithmetic and copies ran while one was open for 19% of the time, Pallas kernels for 8%

profile of v1, /device:TPU:9, one launch (start us, length us, event | category | flops | bytes accessed | tf_op | source)
XLA Modules:
  0.0 406.1 jit_solution(16690138288609550718)
XLA Ops:
  9.0 4.7 %as_lines.3 = bf16[16,128,256]{2,1,0:T(8,128)(2,1)} custom-call(bf16[128,8,1024]{2,1,0:T(8,128)(2,1)} %control.3), custom_call_target="tpu_custom_call" | custom-call | bytes 4194304 | tf_op jit(solution)/shard_map/as_lines/pallas_call | solution.py:58
  13.7 44.1 %all_to_all.40 = bf16[16,128,256]{2,1,0:T(8,128)(2,1)S(1)} all-to-all(bf16[16,128,256]{2,1,0:T(8,128)(2,1)} %as_lines.3), channel_id=1, replica_groups=mesh['gx'=16,'gy'=2] {'gx'}, dimensions={0} | all-to-all | bytes 2097152 | tf_op jit(solution)/shard_map/all_to_all | solution.py:244
  58.6 4.7 %as_lines.2 = bf16[16,128,256]{2,1,0:T(8,128)(2,1)} custom-call(bf16[128,8,1024]{2,1,0:T(8,128)(2,1)} %control.3), custom_call_target="tpu_custom_call" | custom-call | bytes 4194304 | tf_op jit(solution)/shard_map/as_lines/pallas_call | solution.py:58
  63.2 6.9 %all-to-all-start = ((bf16[16,128,256]{2,1,0:T(8,128)(2,1)}), bf16[16,128,256]{2,1,0:T(8,128)(2,1)S(1)}, u32[]{:S(2)}, u32[]{:S(2)}) async-start(bf16[16,128,256]{2,1,0:T(8,128)(2,1)} %as_lines.2), calls=%async_computation | async-start | bytes 2097152 | tf_op jit(solution)/shard_map/all_to_all | solution.py:244
  70.1 4.3 %all-gather.3.cloned.1.call-done = bf16[1024,2048]{1,0:T(8,128)(2,1)} async-done(((bf16[64,2048]{1,0:T(8,128)(2,1)}), bf16[1024,2048]{1,0:T(8,128)(2,1)}) %all-gather.3.cloned.1.call-update) | async-done | bytes 4194320 | tf_op jit(solution)/shard_map/all_gather | solution.py:338
  74.4 3.5 fusion.4
  79.9 23.5 %all-to-all-done = bf16[16,128,256]{2,1,0:T(8,128)(2,1)S(1)} async-done(((bf16[16,128,256]{2,1,0:T(8,128)(2,1)}), bf16[16,128,256]{2,1,0:T(8,128)(2,1)S(1)}, u32[]{:S(2)}, u32[]{:S(2)}) %all-to-all-start) | async-done | bytes 1048608 | tf_op jit(solution)/shard_map/all_to_all | solution.py:244
  103.4 3.6 convolution_convert_fusion.3
  109.4 11.5 %collective-permute-done.1 = bf16[16,64,256]{2,1,0:T(8,128)(2,1)S(1)} collective-permute-done((bf16[16,64,256]{2,1,0:T(8,128)(2,1)S(1)}, bf16[16,64,256]{2,1,0:T(8,128)(2,1)S(1)}, u32[]{:S(2)}, u32[]{:S(2)}) %collective-permute-start.1) | collective-permute-done | bytes 524320 | tf_op jit(solution)/shard_map/ppermute | solution.py:253
  125.9 1.9 add_convert_fusion.3
  127.8 5.2 %all-to-all-start.2 = ((bf16[16,64,512]{2,1,0:T(8,128)(2,1)}), bf16[16,64,512]{2,1,0:T(8,128)(2,1)S(1)}, u32[]{:S(2)}, u32[]{:S(2)}) async-start(bf16[16,64,512]{2,1,0:T(8,128)(2,1)} %add_convert_fusion.3), calls=%async_computation.2 | async-start | bytes 2097152 | tf_op jit(solution)/shard_map/all_to_all | solution.py:244
  133.1 3.6 convolution_convert_fusion
  141.5 8.5 %collective-permute-done.10 = bf16[16,64,256]{2,1,0:T(8,128)(2,1)S(1)} collective-permute-done((bf16[16,64,256]{2,1,0:T(8,128)(2,1)S(1)}, bf16[16,64,256]{2,1,0:T(8,128)(2,1)S(1)}, u32[]{:S(2)}, u32[]{:S(2)}) %collective-permute-start.10) | collective-permute-done | bytes 524320 | tf_op jit(solution)/shard_map/ppermute | solution.py:253
  150.4 2.0 collective-permute-start.11
  152.4 8.7 %collective-permute-done.7 = bf16[16,64,256]{2,1,0:T(8,128)(2,1)S(1)} collective-permute-done((bf16[16,64,256]{2,1,0:T(8,128)(2,1)S(1)}, bf16[16,64,256]{2,1,0:T(8,128)(2,1)S(1)}, u32[]{:S(2)}, u32[]{:S(2)}) %collective-permute-start.7) | collective-permute-done | bytes 524320 | tf_op jit(solution)/shard_map/ppermute | solution.py:253
  164.4 1.9 add_convert_fusion.2
  166.2 6.0 %all-to-all-start.3 = ((bf16[16,64,512]{2,1,0:T(8,128)(2,1)}), bf16[16,64,512]{2,1,0:T(8,128)(2,1)S(1)}, u32[]{:S(2)}, u32[]{:S(2)}) async-start(bf16[16,64,512]{2,1,0:T(8,128)(2,1)} %add_convert_fusion.2), calls=%async_computation.3 | async-start | bytes 2097152 | tf_op jit(solution)/shard_map/all_to_all | solution.py:244
  173.3 2.3 constant_dynamic-slice_fusion
  177.0 20.1 %all-to-all-done.3 = bf16[16,64,512]{2,1,0:T(8,128)(2,1)S(1)} async-done(((bf16[16,64,512]{2,1,0:T(8,128)(2,1)}), bf16[16,64,512]{2,1,0:T(8,128)(2,1)S(1)}, u32[]{:S(2)}, u32[]{:S(2)}) %all-to-all-start.3) | async-done | bytes 1048608 | tf_op jit(solution)/shard_map/all_to_all | solution.py:244
  198.1 1.8 copy.267
  201.8 1.9 collective-permute-start.13
  203.8 3.6 collective-permute-start.12
  209.2 14.6 %forward.1 = (f32[128,8,1024]{2,1,0:T(8,128)}, f32[128,8,1024]{2,1,0:T(8,128)}, f32[2,8,1024]{2,1,0:T(8,128)}, f32[128,8,2]{2,1,0:T(8,128)}) custom-call(bf16[64,8,1024]{2,1,0:T(8,128)(2,1)} %bitcast.179, bf16[64,8,1024]{2,1,0:T(8,128)(2,1)} %bitcast.182, f32[2,8,1024]{2,1,0:T(8,128)} %maximum_convert_fusion.refs_2_, f32[128,8,2]{2,1,0:T(8,128)} %copy.249.refs_3_, ...), custom_call_target="tpu_custom_call" | custom-call | flops 31457280 | bytes 29360128 | tf_op jit(solution)/shard_map/forward/pallas_call | solution.py:173
  225.5 4.2 %collective-permute-start.16 = (f32[8,1024]{1,0:T(8,128)S(1)}, f32[8,1024]{1,0:T(8,128)S(1)}, u32[]{:S(2)}, u32[]{:S(2)}) collective-permute-start(f32[8,1024]{1,0:T(8,128)S(1)} %get-tuple-element.44), channel_id=1, source_target_pairs={{0,2},{2,4},{4,6},{6,8},{8,10},{10,12},{12,14},{14,16},{16,18},{18... | collective-permute-start | bytes 98312 | tf_op jit(solution)/shard_map/ppermute | solution.py:315
  229.7 1.9 collective-permute-start.17
  232.7 2.2 collective-permute-done.17
  235.6 5.7 %rim_lines.2 = bf16[16,128,256]{2,1,0:T(8,128)(2,1)} custom-call(f32[128,8,1024]{2,1,0:T(8,128)} %get-tuple-element.21.flat, f32[2,8,1024]{2,1,0:T(8,128)} %pad_maximum_fusion.rows_in, f32[128,8,2]{2,1,0:T(8,128)} %copy.251.sides), custom_call_target="tpu_custom_call" | custom-call | flops 4194304 | bytes 8388608 | tf_op jit(solution)/shard_map/rim_lines/pallas_call | solution.py:226
  241.3 7.0 %all-to-all-start.4 = ((bf16[16,128,256]{2,1,0:T(8,128)(2,1)}), bf16[16,128,256]{2,1,0:T(8,128)(2,1)S(1)}, u32[]{:S(2)}, u32[]{:S(2)}) async-start(bf16[16,128,256]{2,1,0:T(8,128)(2,1)} %rim_lines.2), calls=%async_computation.4 | async-start | bytes 2097152 | tf_op jit(solution)/shard_map/all_to_all | solution.py:244
  248.3 5.7 %rim_lines.3 = bf16[16,128,256]{2,1,0:T(8,128)(2,1)} custom-call(f32[128,8,1024]{2,1,0:T(8,128)} %get-tuple-element.21.flat, f32[2,8,1024]{2,1,0:T(8,128)} %pad_maximum_fusion.rows_in, f32[128,8,2]{2,1,0:T(8,128)} %copy.251.sides), custom_call_target="tpu_custom_call" | custom-call | flops 4194304 | bytes 8388608 | tf_op jit(solution)/shard_map/rim_lines/pallas_call | solution.py:226
  254.0 19.1 %all-to-all-done.4 = bf16[16,128,256]{2,1,0:T(8,128)(2,1)S(1)} async-done(((bf16[16,128,256]{2,1,0:T(8,128)(2,1)}), bf16[16,128,256]{2,1,0:T(8,128)(2,1)S(1)}, u32[]{:S(2)}, u32[]{:S(2)}) %all-to-all-start.4) | async-done | bytes 1048608 | tf_op jit(solution)/shard_map/all_to_all | solution.py:244
  273.1 5.0 %all-to-all-start.5 = ((bf16[16,128,256]{2,1,0:T(8,128)(2,1)}), bf16[16,128,256]{2,1,0:T(8,128)(2,1)S(1)}, u32[]{:S(2)}, u32[]{:S(2)}) async-start(bf16[16,128,256]{2,1,0:T(8,128)(2,1)} %rim_lines.3), calls=%async_computation.5 | async-start | bytes 2097152 | tf_op jit(solution)/shard_map/all_to_all | solution.py:244
  278.2 3.6 fusion.51
  281.8 2.2 fusion.3
  288.4 14.5 %all-to-all-done.5 = bf16[16,128,256]{2,1,0:T(8,128)(2,1)S(1)} async-done(((bf16[16,128,256]{2,1,0:T(8,128)(2,1)}), bf16[16,128,256]{2,1,0:T(8,128)(2,1)S(1)}, u32[]{:S(2)}, u32[]{:S(2)}) %all-to-all-start.5) | async-done | bytes 1048608 | tf_op jit(solution)/shard_map/all_to_all | solution.py:244
  303.0 3.6 fusion.52
  306.7 2.2 fusion.2
  314.3 2.9 fusion.26
  319.2 2.9 fusion.30
  322.1 3.0 collective-permute-done.23
  333.7 1.8 add_convert_fusion
  335.5 5.1 %all-to-all-start.7 = ((bf16[16,64,512]{2,1,0:T(8,128)(2,1)}), bf16[16,64,512]{2,1,0:T(8,128)(2,1)S(1)}, u32[]{:S(2)}, u32[]{:S(2)}) async-start(bf16[16,64,512]{2,1,0:T(8,128)(2,1)} %add_convert_fusion), calls=%async_computation.7 | async-start | bytes 2097152 | tf_op jit(solution)/shard_map/all_to_all | solution.py:244
  344.7 4.7 %collective-permute-done.25 = bf16[16,64,256]{2,1,0:T(8,128)(2,1)} collective-permute-done((bf16[16,64,256]{2,1,0:T(8,128)(2,1)}, bf16[16,64,256]{2,1,0:T(8,128)(2,1)}, u32[]{:S(2)}, u32[]{:S(2)}) %collective-permute-start.25) | collective-permute-done | bytes 524320 | tf_op jit(solution)/shard_map/ppermute | solution.py:253
  354.2 1.8 add_convert_fusion.1
  356.0 9.4 %all-to-all-done.7.lines = bf16[16,64,512]{2,1,0:T(8,128)(2,1)S(1)} async-done(((bf16[16,64,512]{2,1,0:T(8,128)(2,1)}), bf16[16,64,512]{2,1,0:T(8,128)(2,1)S(1)}, u32[]{:S(2)}, u32[]{:S(2)}) %all-to-all-start.7) | async-done | bytes 1048608 | tf_op jit(solution)/shard_map/all_to_all | solution.py:244
  365.4 5.0 %all-to-all-start.6 = ((bf16[16,64,512]{2,1,0:T(8,128)(2,1)}), bf16[16,64,512]{2,1,0:T(8,128)(2,1)S(1)}, u32[]{:S(2)}, u32[]{:S(2)}) async-start(bf16[16,64,512]{2,1,0:T(8,128)(2,1)} %add_convert_fusion.1), calls=%async_computation.6 | async-start | bytes 2097152 | tf_op jit(solution)/shard_map/all_to_all | solution.py:244
  370.4 3.0 add_lines.2.rest_0_
  373.4 21.8 %all-to-all-done.6.lines = bf16[16,64,512]{2,1,0:T(8,128)(2,1)S(1)} async-done(((bf16[16,64,512]{2,1,0:T(8,128)(2,1)}), bf16[16,64,512]{2,1,0:T(8,128)(2,1)S(1)}, u32[]{:S(2)}, u32[]{:S(2)}) %all-to-all-start.6) | async-done | bytes 1048608 | tf_op jit(solution)/shard_map/all_to_all | solution.py:244
  396.3 3.0 add_lines.3
  (142 shorter events, 61.0 us)
Async XLA Ops:
  7.2 67.2 %all-gather.3.cloned.1.call-start = ((), (), s32[]{:S(2)}) async-start(), calls=%async_computation.8 | async-start | bytes 4456448 | tf_op jit(solution)/shard_map/all_gather | solution.py:338
  8.9 48.9 %copy-start.9 = (bf16[128,2048]{1,0:T(8,128)(2,1)S(1)}, bf16[128,2048]{1,0:T(8,128)(2,1)}, u32[]{:S(2)}) copy-start(bf16[128,2048]{1,0:T(8,128)(2,1)} %param.12) | copy-start | bytes 1572868
  8.9 124.2 %all-gather.5.cloned.1.call-start = ((), (), s32[]{:S(2)}) async-start(), calls=%async_computation.9 | async-start | bytes 4456448 | tf_op jit(solution)/shard_map/all_gather | solution.py:344
  63.2 40.1 %all-to-all-start = ((bf16[16,128,256]{2,1,0:T(8,128)(2,1)}), bf16[16,128,256]{2,1,0:T(8,128)(2,1)S(1)}, u32[]{:S(2)}, u32[]{:S(2)}) async-start(bf16[16,128,256]{2,1,0:T(8,128)(2,1)} %as_lines.2), calls=%async_computation | async-start | bytes 2097152 | tf_op jit(solution)/shard_map/all_to_all | solution.py:244
  78.1 43.3 %collective-permute-start.4 = (bf16[16,64,256]{2,1,0:T(8,128)(2,1)S(1)}, bf16[16,64,256]{2,1,0:T(8,128)(2,1)}, u32[]{:S(2)}, u32[]{:S(2)}) collective-permute-start(bf16[16,64,256]{2,1,0:T(8,128)(2,1)S(1)} %bitcast.187), channel_id=1, source_target_pairs={{0,1},{1,0},{2,3},{3,2},{4,5},{5,4},{6,7},{7,6},{8,9},{9,8},{10,11... | collective-permute-start | bytes 1572872 | tf_op jit(solution)/shard_map/ppermute | solution.py:253
  79.3 44.5 %collective-permute-start.3 = (bf16[16,64,256]{2,1,0:T(8,128)(2,1)S(1)}, bf16[16,64,256]{2,1,0:T(8,128)(2,1)}, u32[]{:S(2)}, u32[]{:S(2)}) collective-permute-start(bf16[16,64,256]{2,1,0:T(8,128)(2,1)S(1)} %bitcast.188), channel_id=1, source_target_pairs={{0,2},{2,0},{4,6},{6,4},{8,10},{10,8},{12,14},{14,12},{16,18},{18,... | collective-permute-start | bytes 1572872 | tf_op jit(solution)/shard_map/ppermute | solution.py:254
  103.4 5.0 %copy-start = (bf16[1024,2048]{1,0:T(8,128)(2,1)S(1)}, bf16[1024,2048]{1,0:T(8,128)(2,1)}, u32[]{:S(2)}) copy-start(bf16[1024,2048]{1,0:T(8,128)(2,1)} %param.13) | copy-start | bytes 12582916
  107.0 13.9 %collective-permute-start.1 = (bf16[16,64,256]{2,1,0:T(8,128)(2,1)S(1)}, bf16[16,64,256]{2,1,0:T(8,128)(2,1)S(1)}, u32[]{:S(2)}, u32[]{:S(2)}) collective-permute-start(bf16[16,64,256]{2,1,0:T(8,128)(2,1)S(1)} %bitcast.200), channel_id=1, source_target_pairs={{0,1},{1,0},{2,3},{3,2},{4,5},{5,4},{6,7},{7,6},{8,9},{9,8},{10,11... | collective-permute-start | bytes 1572872 | tf_op jit(solution)/shard_map/ppermute | solution.py:253
  108.4 15.0 %collective-permute-start = (bf16[16,64,256]{2,1,0:T(8,128)(2,1)S(1)}, bf16[16,64,256]{2,1,0:T(8,128)(2,1)S(1)}, u32[]{:S(2)}, u32[]{:S(2)}) collective-permute-start(bf16[16,64,256]{2,1,0:T(8,128)(2,1)S(1)} %bitcast.201), channel_id=1, source_target_pairs={{0,2},{2,0},{4,6},{6,4},{8,10},{10,8},{12,14},{14,12},{16,18},{18,... | collective-permute-start | bytes 1572872 | tf_op jit(solution)/shard_map/ppermute | solution.py:254
  120.9 4.5 %collective-permute-start.2 = (bf16[16,64,256]{2,1,0:T(8,128)(2,1)S(1)}, bf16[16,64,256]{2,1,0:T(8,128)(2,1)S(1)}, u32[]{:S(2)}, u32[]{:S(2)}) collective-permute-start(bf16[16,64,256]{2,1,0:T(8,128)(2,1)S(1)} %collective-permute-done.1), channel_id=1, source_target_pairs={{0,2},{2,0},{4,6},{6,4},{8,10},{10,8},{12,14},{14,12},{16,18},{18,... | collective-permute-start | bytes 1572872 | tf_op jit(solution)/shard_map/ppermute | solution.py:257
  121.4 4.6 %collective-permute-start.5 = (bf16[16,64,256]{2,1,0:T(8,128)(2,1)}, bf16[16,64,256]{2,1,0:T(8,128)(2,1)S(1)}, u32[]{:S(2)}, u32[]{:S(2)}) collective-permute-start(bf16[16,64,256]{2,1,0:T(8,128)(2,1)} %collective-permute-done.4), channel_id=1, source_target_pairs={{0,2},{2,0},{4,6},{6,4},{8,10},{10,8},{12,14},{14,12},{16,18},{18,... | collective-permute-start | bytes 1572872 | tf_op jit(solution)/shard_map/ppermute | solution.py:257
  127.8 38.4 %all-to-all-start.2 = ((bf16[16,64,512]{2,1,0:T(8,128)(2,1)}), bf16[16,64,512]{2,1,0:T(8,128)(2,1)S(1)}, u32[]{:S(2)}, u32[]{:S(2)}) async-start(bf16[16,64,512]{2,1,0:T(8,128)(2,1)} %add_convert_fusion.3), calls=%async_computation.2 | async-start | bytes 2097152 | tf_op jit(solution)/shard_map/all_to_all | solution.py:244
  133.1 5.8 %copy-start.13 = (bf16[1024,2048]{1,0:T(8,128)(2,1)S(1)}, bf16[1024,2048]{1,0:T(8,128)(2,1)}, u32[]{:S(2)}) copy-start(bf16[1024,2048]{1,0:T(8,128)(2,1)} %all-gather.5.cloned.1.call-done) | copy-start | bytes 12582916
  136.7 3.8 copy-start.1
  136.7 13.2 %collective-permute-start.10 = (bf16[16,64,256]{2,1,0:T(8,128)(2,1)S(1)}, bf16[16,64,256]{2,1,0:T(8,128)(2,1)S(1)}, u32[]{:S(2)}, u32[]{:S(2)}) collective-permute-start(bf16[16,64,256]{2,1,0:T(8,128)(2,1)S(1)} %bitcast.194), channel_id=1, source_target_pairs={{0,1},{1,0},{2,3},{3,2},{4,5},{5,4},{6,7},{7,6},{8,9},{9,8},{10,11... | collective-permute-start | bytes 1572872 | tf_op jit(solution)/shard_map/ppermute | solution.py:253
  138.2 24.6 %collective-permute-start.9 = (bf16[16,64,256]{2,1,0:T(8,128)(2,1)S(1)}, bf16[16,64,256]{2,1,0:T(8,128)(2,1)S(1)}, u32[]{:S(2)}, u32[]{:S(2)}) collective-permute-start(bf16[16,64,256]{2,1,0:T(8,128)(2,1)S(1)} %bitcast.195), channel_id=1, source_target_pairs={{0,2},{2,0},{4,6},{6,4},{8,10},{10,8},{12,14},{14,12},{16,18},{18,... | collective-permute-start | bytes 1572872 | tf_op jit(solution)/shard_map/ppermute | solution.py:254
  140.1 21.0 %collective-permute-start.7 = (bf16[16,64,256]{2,1,0:T(8,128)(2,1)S(1)}, bf16[16,64,256]{2,1,0:T(8,128)(2,1)S(1)}, u32[]{:S(2)}, u32[]{:S(2)}) collective-permute-start(bf16[16,64,256]{2,1,0:T(8,128)(2,1)S(1)} %bitcast.197), channel_id=1, source_target_pairs={{0,1},{1,0},{2,3},{3,2},{4,5},{5,4},{6,7},{7,6},{8,9},{9,8},{10,11... | collective-permute-start | bytes 1572872 | tf_op jit(solution)/shard_map/ppermute | solution.py:253
  140.2 23.1 %collective-permute-start.6 = (bf16[16,64,256]{2,1,0:T(8,128)(2,1)S(1)}, bf16[16,64,256]{2,1,0:T(8,128)(2,1)S(1)}, u32[]{:S(2)}, u32[]{:S(2)}) collective-permute-start(bf16[16,64,256]{2,1,0:T(8,128)(2,1)S(1)} %bitcast.198), channel_id=1, source_target_pairs={{0,2},{2,0},{4,6},{6,4},{8,10},{10,8},{12,14},{14,12},{16,18},{18,... | collective-permute-start | bytes 1572872 | tf_op jit(solution)/shard_map/ppermute | solution.py:254
  150.4 14.0 %collective-permute-start.11 = (bf16[16,64,256]{2,1,0:T(8,128)(2,1)S(1)}, bf16[16,64,256]{2,1,0:T(8,128)(2,1)S(1)}, u32[]{:S(2)}, u32[]{:S(2)}) collective-permute-start(bf16[16,64,256]{2,1,0:T(8,128)(2,1)S(1)} %collective-permute-done.10), channel_id=1, source_target_pairs={{0,2},{2,0},{4,6},{6,4},{8,10},{10,8},{12,14},{14,12},{16,18},{18,... | collective-permute-start | bytes 1572872 | tf_op jit(solution)/shard_map/ppermute | solution.py:257
  161.2 2.7 collective-permute-start.8
  166.2 30.9 %all-to-all-start.3 = ((bf16[16,64,512]{2,1,0:T(8,128)(2,1)}), bf16[16,64,512]{2,1,0:T(8,128)(2,1)S(1)}, u32[]{:S(2)}, u32[]{:S(2)}) async-start(bf16[16,64,512]{2,1,0:T(8,128)(2,1)} %add_convert_fusion.2), calls=%async_computation.3 | async-start | bytes 2097152 | tf_op jit(solution)/shard_map/all_to_all | solution.py:244
  172.9 29.0 %copy-start.4 = (bf16[8,2,64,512]{3,0,1,2:T(8,128)(2,1)}, bf16[8,2,64,512]{3,0,1,2:T(8,128)(2,1)S(1)}, u32[]{:S(2)}) copy-start(bf16[8,2,64,512]{3,0,1,2:T(8,128)(2,1)S(1)} %copy.268) | copy-start | bytes 3145732
  175.5 56.1 %collective-permute-start.15 = (bf16[1024,512]{1,0:T(8,128)(2,1)}, bf16[1024,512]{1,0:T(8,128)(2,1)S(1)}, u32[]{:S(2)}, u32[]{:S(2)}) collective-permute-start(bf16[1024,512]{1,0:T(8,128)(2,1)} %constant_dynamic-slice_fusion), channel_id=1, source_target_pairs={{0,1},{1,0},{2,3},{3,2},{4,5},{5,4},{6,7},{7,6},{8,9},{9,8},{10,11... | collective-permute-start | bytes 3145736 | tf_op jit(solution)/shard_map/ppermute | solution.py:290
  199.9 9.3 %copy-start.5 = (bf16[8,2,64,512]{3,0,1,2:T(8,128)(2,1)}, bf16[8,2,64,512]{3,0,1,2:T(8,128)(2,1)S(1)}, u32[]{:S(2)}) copy-start(bf16[8,2,64,512]{3,0,1,2:T(8,128)(2,1)S(1)} %copy.267) | copy-start | bytes 3145732
  200.4 7.0 %collective-permute-start.14 = (bf16[128,8]{0,1:T(8,128)(2,1)S(1)}, bf16[128,8]{0,1:T(8,128)(2,1)S(1)}, u32[]{:S(2)}, u32[]{:S(2)}) collective-permute-start(bf16[128,8]{0,1:T(8,128)(2,1)S(1)} %maximum_select_fusion), channel_id=1, source_target_pairs={{0,1},{1,0},{2,3},{3,2},{4,5},{5,4},{6,7},{7,6},{8,9},{9,8},{10,11... | collective-permute-start | bytes 6152 | tf_op jit(solution)/shard_map/ppermute | solution.py:321
  201.8 6.7 %collective-permute-start.13 = (bf16[8,1024]{1,0:T(8,128)(2,1)S(1)}, bf16[8,1024]{1,0:T(8,128)(2,1)S(1)}, u32[]{:S(2)}, u32[]{:S(2)}) collective-permute-start(bf16[8,1024]{1,0:T(8,128)(2,1)S(1)} %bitcast.209), channel_id=1, source_target_pairs={{2,0},{4,2},{6,4},{8,6},{10,8},{12,10},{14,12},{16,14},{18,16},{20... | collective-permute-start | bytes 49160 | tf_op jit(solution)/shard_map/ppermute | solution.py:315
  203.8 4.7 %collective-permute-start.12 = (bf16[8,1024]{1,0:T(8,128)(2,1)S(1)}, bf16[8,1024]{1,0:T(8,128)(2,1)S(1)}, u32[]{:S(2)}, u32[]{:S(2)}) collective-permute-start(bf16[8,1024]{1,0:T(8,128)(2,1)S(1)} %bitcast.210), channel_id=1, source_target_pairs={{0,2},{2,4},{4,6},{6,8},{8,10},{10,12},{12,14},{14,16},{16,18},{18... | collective-permute-start | bytes 49160 | tf_op jit(solution)/shard_map/ppermute | solution.py:315
  225.4 6.3 %collective-permute-start.18 = (f32[128,8]{0,1:T(8,128)S(1)}, f32[128,8]{0,1:T(8,128)S(1)}, u32[]{:S(2)}, u32[]{:S(2)}) collective-permute-start(f32[128,8]{0,1:T(8,128)S(1)} %bitcast.217), channel_id=1, source_target_pairs={{0,1},{1,0},{2,3},{3,2},{4,5},{5,4},{6,7},{7,6},{8,9},{9,8},{10,11... | collective-permute-start | bytes 12296 | tf_op jit(solution)/shard_map/ppermute | solution.py:321
  225.5 7.2 %collective-permute-start.16 = (f32[8,1024]{1,0:T(8,128)S(1)}, f32[8,1024]{1,0:T(8,128)S(1)}, u32[]{:S(2)}, u32[]{:S(2)}) collective-permute-start(f32[8,1024]{1,0:T(8,128)S(1)} %get-tuple-element.44), channel_id=1, source_target_pairs={{0,2},{2,4},{4,6},{6,8},{8,10},{10,12},{12,14},{14,16},{16,18},{18... | collective-permute-start | bytes 98312 | tf_op jit(solution)/shard_map/ppermute | solution.py:315
  229.7 5.2 %collective-permute-start.17 = (f32[8,1024]{1,0:T(8,128)S(1)}, f32[8,1024]{1,0:T(8,128)S(1)}, u32[]{:S(2)}, u32[]{:S(2)}) collective-permute-start(f32[8,1024]{1,0:T(8,128)S(1)} %get-tuple-element.45), channel_id=1, source_target_pairs={{2,0},{4,2},{6,4},{8,6},{10,8},{12,10},{14,12},{16,14},{18,16},{20... | collective-permute-start | bytes 98312 | tf_op jit(solution)/shard_map/ppermute | solution.py:315
  241.3 31.8 %all-to-all-start.4 = ((bf16[16,128,256]{2,1,0:T(8,128)(2,1)}), bf16[16,128,256]{2,1,0:T(8,128)(2,1)S(1)}, u32[]{:S(2)}, u32[]{:S(2)}) async-start(bf16[16,128,256]{2,1,0:T(8,128)(2,1)} %rim_lines.2), calls=%async_computation.4 | async-start | bytes 2097152 | tf_op jit(solution)/shard_map/all_to_all | solution.py:244
  273.1 29.8 %all-to-all-start.5 = ((bf16[16,128,256]{2,1,0:T(8,128)(2,1)}), bf16[16,128,256]{2,1,0:T(8,128)(2,1)S(1)}, u32[]{:S(2)}, u32[]{:S(2)}) async-start(bf16[16,128,256]{2,1,0:T(8,128)(2,1)} %rim_lines.3), calls=%async_computation.5 | async-start | bytes 2097152 | tf_op jit(solution)/shard_map/all_to_all | solution.py:244
  278.2 3.7 copy-start.11
  286.6 44.2 %collective-permute-start.27 = (bf16[16,64,256]{2,1,0:T(8,128)(2,1)}, bf16[16,64,256]{2,1,0:T(8,128)(2,1)}, u32[]{:S(2)}, u32[]{:S(2)}) collective-permute-start(bf16[16,64,256]{2,1,0:T(8,128)(2,1)} %get-tuple-element.28), channel_id=1, source_target_pairs={{0,2},{2,0},{4,6},{6,4},{8,10},{10,8},{12,14},{14,12},{16,18},{18,... | collective-permute-start | bytes 1572872 | tf_op jit(solution)/shard_map/ppermute | solution.py:254
  287.0 42.3 %collective-permute-start.28 = (bf16[16,64,256]{2,1,0:T(8,128)(2,1)}, bf16[16,64,256]{2,1,0:T(8,128)(2,1)}, u32[]{:S(2)}, u32[]{:S(2)}) collective-permute-start(bf16[16,64,256]{2,1,0:T(8,128)(2,1)} %get-tuple-element.28), channel_id=1, source_target_pairs={{0,1},{1,0},{2,3},{3,2},{4,5},{5,4},{6,7},{7,6},{8,9},{9,8},{10,11... | collective-permute-start | bytes 1572872 | tf_op jit(solution)/shard_map/ppermute | solution.py:253
  311.3 13.7 %collective-permute-start.23 = (bf16[16,64,256]{2,1,0:T(8,128)(2,1)S(1)}, bf16[16,64,256]{2,1,0:T(8,128)(2,1)S(1)}, u32[]{:S(2)}, u32[]{:S(2)}) collective-permute-start(bf16[16,64,256]{2,1,0:T(8,128)(2,1)S(1)} %get-tuple-element.32), channel_id=1, source_target_pairs={{0,1},{1,0},{2,3},{3,2},{4,5},{5,4},{6,7},{7,6},{8,9},{9,8},{10,11... | collective-permute-start | bytes 1572872 | tf_op jit(solution)/shard_map/ppermute | solution.py:253
  312.7 13.7 %collective-permute-start.24 = (bf16[16,64,256]{2,1,0:T(8,128)(2,1)S(1)}, bf16[16,64,256]{2,1,0:T(8,128)(2,1)S(1)}, u32[]{:S(2)}, u32[]{:S(2)}) collective-permute-start(bf16[16,64,256]{2,1,0:T(8,128)(2,1)S(1)} %get-tuple-element.32), channel_id=1, source_target_pairs={{0,2},{2,0},{4,6},{6,4},{8,10},{10,8},{12,14},{14,12},{16,18},{18,... | collective-permute-start | bytes 1572872 | tf_op jit(solution)/shard_map/ppermute | solution.py:254
  317.1 24.3 %collective-permute-start.19 = (bf16[16,64,256]{2,1,0:T(8,128)(2,1)}, bf16[16,64,256]{2,1,0:T(8,128)(2,1)S(1)}, u32[]{:S(2)}, u32[]{:S(2)}) collective-permute-start(bf16[16,64,256]{2,1,0:T(8,128)(2,1)} %get-tuple-element.29), channel_id=1, source_target_pairs={{0,2},{2,0},{4,6},{6,4},{8,10},{10,8},{12,14},{14,12},{16,18},{18,... | collective-permute-start | bytes 1572872 | tf_op jit(solution)/shard_map/ppermute | solution.py:254
  325.0 15.6 %collective-permute-start.20 = (bf16[16,64,256]{2,1,0:T(8,128)(2,1)}, bf16[16,64,256]{2,1,0:T(8,128)(2,1)S(1)}, u32[]{:S(2)}, u32[]{:S(2)}) collective-permute-start(bf16[16,64,256]{2,1,0:T(8,128)(2,1)} %get-tuple-element.29), channel_id=1, source_target_pairs={{0,1},{1,0},{2,3},{3,2},{4,5},{5,4},{6,7},{7,6},{8,9},{9,8},{10,11... | collective-permute-start | bytes 1572872 | tf_op jit(solution)/shard_map/ppermute | solution.py:253
  326.5 16.5 %collective-permute-start.22 = (bf16[16,64,256]{2,1,0:T(8,128)(2,1)}, bf16[16,64,256]{2,1,0:T(8,128)(2,1)}, u32[]{:S(2)}, u32[]{:S(2)}) collective-permute-start(bf16[16,64,256]{2,1,0:T(8,128)(2,1)} %get-tuple-element.26), channel_id=1, source_target_pairs={{0,2},{2,0},{4,6},{6,4},{8,10},{10,8},{12,14},{14,12},{16,18},{18,... | collective-permute-start | bytes 1572872 | tf_op jit(solution)/shard_map/ppermute | solution.py:254
  329.3 3.8 collective-permute-start.30
  330.9 2.8 collective-permute-start.29
  333.2 16.3 %collective-permute-start.25 = (bf16[16,64,256]{2,1,0:T(8,128)(2,1)}, bf16[16,64,256]{2,1,0:T(8,128)(2,1)}, u32[]{:S(2)}, u32[]{:S(2)}) collective-permute-start(bf16[16,64,256]{2,1,0:T(8,128)(2,1)} %get-tuple-element.26), channel_id=1, source_target_pairs={{0,1},{1,0},{2,3},{3,2},{4,5},{5,4},{6,7},{7,6},{8,9},{9,8},{10,11... | collective-permute-start | bytes 1572872 | tf_op jit(solution)/shard_map/ppermute | solution.py:253
  335.5 29.9 %all-to-all-start.7 = ((bf16[16,64,512]{2,1,0:T(8,128)(2,1)}), bf16[16,64,512]{2,1,0:T(8,128)(2,1)S(1)}, u32[]{:S(2)}, u32[]{:S(2)}) async-start(bf16[16,64,512]{2,1,0:T(8,128)(2,1)} %add_convert_fusion), calls=%async_computation.7 | async-start | bytes 2097152 | tf_op jit(solution)/shard_map/all_to_all | solution.py:244
  341.0 11.5 %collective-permute-start.21 = (bf16[16,64,256]{2,1,0:T(8,128)(2,1)S(1)}, bf16[16,64,256]{2,1,0:T(8,128)(2,1)S(1)}, u32[]{:S(2)}, u32[]{:S(2)}) collective-permute-start(bf16[16,64,256]{2,1,0:T(8,128)(2,1)S(1)} %collective-permute-done.20), channel_id=1, source_target_pairs={{0,2},{2,0},{4,6},{6,4},{8,10},{10,8},{12,14},{14,12},{16,18},{18,... | collective-permute-start | bytes 1572872 | tf_op jit(solution)/shard_map/ppermute | solution.py:257
  349.5 3.5 collective-permute-start.26
  365.4 5.0 %copy-start.6 = (bf16[16,64,512]{2,1,0:T(8,128)(2,1)}, bf16[16,64,512]{2,1,0:T(8,128)(2,1)S(1)}, u32[]{:S(2)}) copy-start(bf16[16,64,512]{2,1,0:T(8,128)(2,1)S(1)} %all-to-all-done.7.lines) | copy-start | bytes 3145732
  365.4 29.8 %all-to-all-start.6 = ((bf16[16,64,512]{2,1,0:T(8,128)(2,1)}), bf16[16,64,512]{2,1,0:T(8,128)(2,1)S(1)}, u32[]{:S(2)}, u32[]{:S(2)}) async-start(bf16[16,64,512]{2,1,0:T(8,128)(2,1)} %add_convert_fusion.1), calls=%async_computation.6 | async-start | bytes 2097152 | tf_op jit(solution)/shard_map/all_to_all | solution.py:244
  (6 other events, 11.1 us)
Sparse Core Ops, SparseCore 0:
  10.7 63.5 all-gather.2
  76.5 56.2 all-gather.4

commit v2 on v1

--- a/solution.py
+++ b/solution.py
@@ -33,23 +33,22 @@
     ]
 
 
-def store_lines(turned, out, parts):
-    piece = out.shape[2]
-
-    @pl.loop(0, turned.shape[0] // TILE)
+def store_lines(block, out, parts, chunk, finish):
+    levels, width = block.shape[1:]
+
+    @pl.loop(0, block.shape[0] // TILE)
     def _(tile):
         at = pl.ds(tile * TILE, TILE)
-        for l in range(turned.shape[1]):
-            for s in range(parts):
-                got = turned[at, l, s * piece : (s + 1) * piece]
-                out[l * parts + s, at] = got.astype(BF16)
-
-
-def lines_body(parts, chunk, block, out, turned):
-    piece = out.shape[2]
-    for s, span in enumerate(chunk_spans(block.shape[2], parts, chunk)):
-        turned[:, :, s * piece : (s + 1) * piece] = block[:, :, span].astype(F32)
-    store_lines(turned, out, parts)
+        for s, span in enumerate(chunk_spans(width, parts, chunk)):
+            turned = jnp.swapaxes(finish(at, span), 0, 1)
+            for l in range(levels):
+                out[l * parts + s, at] = turned[l].astype(BF16)
+
+
+def lines_body(parts, chunk, block, out):
+    store_lines(
+        block, out, parts, chunk, lambda at, span: block[at, :, span].astype(F32)
+    )
 
 
 def as_lines(block, parts, chunk):
@@ -61,7 +60,6 @@
         in_specs=[pl.BlockSpec((STEP, levels, width), lambda i: (i, 0, 0))],
         out_specs=pl.BlockSpec((shape[0], STEP, shape[2]), lambda i: (0, i, 0)),
         out_shape=jax.ShapeDtypeStruct(shape, BF16),
-        scratch_shapes=[pltpu.VMEM((STEP, levels, width // CHUNKS), F32)],
         compiler_params=PARAMS,
         cost_estimate=cost(0, block, block),
         name="as_lines",
@@ -69,19 +67,18 @@
 
 
 def gradient_body(parts, lines, control, *rest):
-    out, turned = rest[-2:]
+    out = rest[-1]
     levels, width = control.shape[1:]
     part = width // parts
 
     @pl.loop(0, STEP // TILE)
     def _(tile):
         at = pl.ds(tile * TILE, TILE)
-        for l in range(levels):
-            for s in range(parts):
-                got = lines[l * parts + s, at].astype(F32)
-                turned[at, l, s * part : (s + 1) * part] = got
-
-    out[...] = control[...].astype(F32) + turned[...]
+        for s in range(parts):
+            span = slice(s * part, (s + 1) * part)
+            got = [lines[l * parts + s, at].astype(F32) for l in range(levels)]
+            got = jnp.swapaxes(jnp.stack(got), 0, 1)
+            out[at, :, span] = control[at, :, span].astype(F32) + got
 
 
 def add_lines(control, lines, parts, first, target):
@@ -101,7 +98,6 @@
         out_specs=pl.BlockSpec(whole, lambda i: (i + offset, 0, 0)),
         out_shape=jax.ShapeDtypeStruct(control.shape, F32),
         input_output_aliases={} if target is None else {2: 0},
-        scratch_shapes=[pltpu.VMEM(whole, F32)],
         compiler_params=PARAMS,
         cost_estimate=cost(control.size // 2, control, control),
         name="add_lines",
@@ -191,40 +187,31 @@
     )(*starts, rows_in, sides, innovation, weight, wind_x, wind_y)
 
 
-def rim_body(parts, chunk, last, flat, rows_in, sides, out, turned):
+def rim_body(parts, chunk, rows, flat, rows_in, sides, out):
     step = pl.program_id(0)
-    levels, width = flat.shape[1:]
-    piece = out.shape[2]
-    place = lax.broadcasted_iota(jnp.int32, (STEP, levels, piece), 2)
-    spans = chunk_spans(width, parts, chunk)
-    for s, span in enumerate(spans):
-        value = flat[:, :, span]
+    width = flat.shape[2]
+
+    def finish(at, span):
+        value = flat[at, :, span]
+        row = step * STEP + at.start + lax.broadcasted_iota(jnp.int32, value.shape, 0)
+        value = value - jnp.where(row == 0, 0.5 * rows_in[0:1, :, span], 0.0)
+        value = value + jnp.where(row == rows - 1, 0.5 * rows_in[1:2, :, span], 0.0)
+        place = lax.broadcasted_iota(jnp.int32, value.shape, 2)
         if span.start == 0:
-            value = value - jnp.where(place == 0, 0.5 * sides[:, :, 0:1], 0.0)
+            value = value - jnp.where(place == 0, 0.5 * sides[at, :, 0:1], 0.0)
         if span.stop == width:
-            value = value + jnp.where(place == piece - 1, 0.5 * sides[:, :, 1:2], 0.0)
-        turned[:, :, s * piece : (s + 1) * piece] = value
-
-    @pl.when(step == 0)
-    def _():
-        for s, span in enumerate(spans):
-            at = slice(s * piece, (s + 1) * piece)
-            turned[0, :, at] += -0.5 * rows_in[0, :, span]
-
-    @pl.when(step == last)
-    def _():
-        for s, span in enumerate(spans):
-            at = slice(s * piece, (s + 1) * piece)
-            turned[STEP - 1, :, at] += 0.5 * rows_in[1, :, span]
-
-    store_lines(turned, out, parts)
+            edge = place == span.stop - span.start - 1
+            value = value + jnp.where(edge, 0.5 * sides[at, :, 1:2], 0.0)
+        return value
+
+    store_lines(flat, out, parts, chunk, finish)
 
 
 def rim_lines(flat, rows_in, sides, parts, chunk):
     rows, levels, width = flat.shape
     shape = (levels * parts, rows, width // parts // CHUNKS)
     return pl.pallas_call(
-        functools.partial(rim_body, parts, chunk, rows // STEP - 1),
+        functools.partial(rim_body, parts, chunk, rows),
         grid=(rows // STEP,),
         in_specs=[
             pl.BlockSpec((STEP, levels, width), lambda i: (i, 0, 0)),
@@ -233,7 +220,6 @@
         ],
         out_specs=pl.BlockSpec((shape[0], STEP, shape[2]), lambda i: (0, i, 0)),
         out_shape=jax.ShapeDtypeStruct(shape, BF16),
-        scratch_shapes=[pltpu.VMEM((STEP, levels, width // CHUNKS), F32)],
         compiler_params=PARAMS,
         cost_estimate=cost(4 * flat.size, flat, flat),
         name="rim_lines",

time: 408 us -> 405 us (level)
  starting transfers between devices: 73 us -> 77.2 us
  Pallas kernels: 41.4 us -> 37.3 us
    all_to_all x7, waiting for transfers between devices: 109 us -> 100 us  [swap_all(): return lax.all_to_all(lines, 'gx', 0, 0, tiled=True)]
    all_gather x1, waiting for transfers between devices: 0.02 us -> 5.39 us  [per_device(): matrix_x.append(lax.all_gather(share, 'gx', axis=0, tiled=True))]
    all_gather x1, waiting for transfers between devices: 4.27 us -> 8.4 us  [per_device(): matrix_x = [lax.all_gather(filter_x[:cut], 'gx', axis=0, tiled=True)]]
  transfers between devices with their start and end apart: 40 -> 40, of which waited for: 14 -> 15; matrix products, arithmetic and copies ran while one was open for 19% -> 19% of each run, Pallas kernels for 8% -> 7%
where the time goes in v2:
time: 405 us; the launch traced here: 403 us
  waiting for transfers between devices  151 us (37%)
  starting transfers between devices  77.2 us (19%)
  matrix products  60 us (15%)
  blocking collectives  42.3 us (10%)
  Pallas kernels  37.3 us (9%)
  local copies, waits for them, and re-layouts  18.6 us (5%)
  between operations  14.6 us (4%)
    all_to_all x7, waiting for transfers between devices, swap_all(): return lax.all_to_all(lines, 'gx', 0, 0, tiled=True)  100 us
    all_to_all x1, blocking collectives, swap_all(): return lax.all_to_all(lines, 'gx', 0, 0, tiled=True)  42.3 us
    all_to_all x7, starting transfers between devices, swap_all(): return lax.all_to_all(lines, 'gx', 0, 0, tiled=True)  41.7 us
    ppermute x8, waiting for transfers between devices, plane_pieces(): far = lax.ppermute(sent, 'gy', [(0, 1), (1, 0)])  34.1 us
    dot_general x16, matrix products, per_device(): jnp.einsum('brk,kc->brc', plane, matrix[span], preferred_element_type=F32)  23.8 us
    pallas_call x1, Pallas kernels, forward(): pl.pallas_call(forward_body, grid=(rows // STEP,), in_specs=[start] * CHU...  14.6 us
    dot_general x16, matrix products, per_device(): jnp.einsum('brc,kc->brk', plane, matrix[:, span], preferred_element_type=...  12.5 us
    dot_general x4, matrix products, per_device(): smoothed = jnp.dot(matrix_x[h], lines[w], preferred_element_type=F32)  11.9 us
  transfers between devices with their start and end apart: 40, of which 15 were waited for; matrix products, arithmetic and copies ran while one was open for 19% of the time, Pallas kernels for 7%

profile of v2, /device:TPU:9, one launch (start us, length us, event | category | flops | bytes accessed | tf_op | source)
XLA Modules:
  0.0 403.4 jit_solution(15775557590514148222)
XLA Ops:
  9.0 3.8 as_lines.3
  12.8 42.3 %all_to_all.40 = bf16[16,128,256]{2,1,0:T(8,128)(2,1)S(1)} all-to-all(bf16[16,128,256]{2,1,0:T(8,128)(2,1)} %as_lines.3), channel_id=1, replica_groups=mesh['gx'=16,'gy'=2] {'gx'}, dimensions={0} | all-to-all | bytes 2097152 | tf_op jit(solution)/shard_map/all_to_all | solution.py:230
  55.9 3.8 as_lines.2
  59.7 7.6 %all-to-all-start = ((bf16[16,128,256]{2,1,0:T(8,128)(2,1)}), bf16[16,128,256]{2,1,0:T(8,128)(2,1)S(1)}, u32[]{:S(2)}, u32[]{:S(2)}) async-start(bf16[16,128,256]{2,1,0:T(8,128)(2,1)} %as_lines.2), calls=%async_computation | async-start | bytes 2097152 | tf_op jit(solution)/shard_map/all_to_all | solution.py:230
  67.3 8.4 %all-gather.3.cloned.1.call-done = bf16[1024,2048]{1,0:T(8,128)(2,1)} async-done(((bf16[64,2048]{1,0:T(8,128)(2,1)}), bf16[1024,2048]{1,0:T(8,128)(2,1)}) %all-gather.3.cloned.1.call-update) | async-done | bytes 4194320 | tf_op jit(solution)/shard_map/all_gather | solution.py:324
  75.7 3.5 fusion.4
  79.4 2.1 collective-permute-start.4
  82.0 13.6 %all-to-all-done = bf16[16,128,256]{2,1,0:T(8,128)(2,1)S(1)} async-done(((bf16[16,128,256]{2,1,0:T(8,128)(2,1)}), bf16[16,128,256]{2,1,0:T(8,128)(2,1)S(1)}, u32[]{:S(2)}, u32[]{:S(2)}) %all-to-all-start) | async-done | bytes 1048608 | tf_op jit(solution)/shard_map/all_to_all | solution.py:230
  95.7 3.6 convolution_convert_fusion.3
  103.0 8.5 %collective-permute-done.1 = bf16[16,64,256]{2,1,0:T(8,128)(2,1)S(1)} collective-permute-done((bf16[16,64,256]{2,1,0:T(8,128)(2,1)S(1)}, bf16[16,64,256]{2,1,0:T(8,128)(2,1)S(1)}, u32[]{:S(2)}, u32[]{:S(2)}) %collective-permute-start.1) | collective-permute-done | bytes 524320 | tf_op jit(solution)/shard_map/ppermute | solution.py:239
  111.6 2.1 collective-permute-start.2
  118.3 1.9 add_convert_fusion.3
  120.2 8.0 %all-to-all-start.2 = ((bf16[16,64,512]{2,1,0:T(8,128)(2,1)}), bf16[16,64,512]{2,1,0:T(8,128)(2,1)S(1)}, u32[]{:S(2)}, u32[]{:S(2)}) async-start(bf16[16,64,512]{2,1,0:T(8,128)(2,1)} %add_convert_fusion.3), calls=%async_computation.2 | async-start | bytes 2097152 | tf_op jit(solution)/shard_map/all_to_all | solution.py:230
  128.2 5.4 %all-gather.5.cloned.1.call-done = bf16[1024,2048]{1,0:T(8,128)(2,1)} async-done(((bf16[64,2048]{1,0:T(8,128)(2,1)}), bf16[1024,2048]{1,0:T(8,128)(2,1)}) %all-gather.5.cloned.1.call-update) | async-done | bytes 4194320 | tf_op jit(solution)/shard_map/all_gather | solution.py:330
  133.6 3.6 convolution_convert_fusion
  141.8 8.7 %collective-permute-done.10 = bf16[16,64,256]{2,1,0:T(8,128)(2,1)S(1)} collective-permute-done((bf16[16,64,256]{2,1,0:T(8,128)(2,1)S(1)}, bf16[16,64,256]{2,1,0:T(8,128)(2,1)S(1)}, u32[]{:S(2)}, u32[]{:S(2)}) %collective-permute-start.10) | collective-permute-done | bytes 524320 | tf_op jit(solution)/shard_map/ppermute | solution.py:239
  152.8 9.0 %collective-permute-done.7 = bf16[16,64,256]{2,1,0:T(8,128)(2,1)S(1)} collective-permute-done((bf16[16,64,256]{2,1,0:T(8,128)(2,1)S(1)}, bf16[16,64,256]{2,1,0:T(8,128)(2,1)S(1)}, u32[]{:S(2)}, u32[]{:S(2)}) %collective-permute-start.7) | collective-permute-done | bytes 524320 | tf_op jit(solution)/shard_map/ppermute | solution.py:239
  164.8 1.9 add_convert_fusion.2
  166.7 4.0 all-to-all-start.3
  171.7 2.3 constant_dynamic-slice_fusion
  175.2 20.4 %all-to-all-done.3 = bf16[16,64,512]{2,1,0:T(8,128)(2,1)S(1)} async-done(((bf16[16,64,512]{2,1,0:T(8,128)(2,1)}), bf16[16,64,512]{2,1,0:T(8,128)(2,1)S(1)}, u32[]{:S(2)}, u32[]{:S(2)}) %all-to-all-start.3) | async-done | bytes 1048608 | tf_op jit(solution)/shard_map/all_to_all | solution.py:230
  200.1 1.9 collective-permute-start.13
  202.0 3.6 collective-permute-start.12
  207.4 14.6 %forward.1 = (f32[128,8,1024]{2,1,0:T(8,128)}, f32[128,8,1024]{2,1,0:T(8,128)}, f32[2,8,1024]{2,1,0:T(8,128)}, f32[128,8,2]{2,1,0:T(8,128)}) custom-call(bf16[64,8,1024]{2,1,0:T(8,128)(2,1)} %bitcast.179, bf16[64,8,1024]{2,1,0:T(8,128)(2,1)} %bitcast.182, f32[2,8,1024]{2,1,0:T(8,128)} %maximum_convert_fusion.refs_2_, f32[128,8,2]{2,1,0:T(8,128)} %copy.249.refs_3_, ...), custom_call_target="tpu_custom_call" | custom-call | flops 31457280 | bytes 29360128 | tf_op jit(solution)/shard_map/forward/pallas_call | solution.py:169
  223.9 4.2 %collective-permute-start.16 = (f32[8,1024]{1,0:T(8,128)S(1)}, f32[8,1024]{1,0:T(8,128)S(1)}, u32[]{:S(2)}, u32[]{:S(2)}) collective-permute-start(f32[8,1024]{1,0:T(8,128)S(1)} %get-tuple-element.44), channel_id=1, source_target_pairs={{0,2},{2,4},{4,6},{6,8},{8,10},{10,12},{12,14},{14,16},{16,18},{18... | collective-permute-start | bytes 98312 | tf_op jit(solution)/shard_map/ppermute | solution.py:301
  228.2 1.9 collective-permute-start.17
  231.2 2.2 collective-permute-done.17
  234.0 4.8 %rim_lines.2 = bf16[16,128,256]{2,1,0:T(8,128)(2,1)} custom-call(f32[128,8,1024]{2,1,0:T(8,128)} %get-tuple-element.21.flat, f32[2,8,1024]{2,1,0:T(8,128)} %pad_maximum_fusion.rows_in, f32[128,8,2]{2,1,0:T(8,128)} %copy.251.sides), custom_call_target="tpu_custom_call" | custom-call | flops 4194304 | bytes 8388608 | tf_op jit(solution)/shard_map/rim_lines/pallas_call | solution.py:213
  238.8 7.0 %all-to-all-start.4 = ((bf16[16,128,256]{2,1,0:T(8,128)(2,1)}), bf16[16,128,256]{2,1,0:T(8,128)(2,1)S(1)}, u32[]{:S(2)}, u32[]{:S(2)}) async-start(bf16[16,128,256]{2,1,0:T(8,128)(2,1)} %rim_lines.2), calls=%async_computation.4 | async-start | bytes 2097152 | tf_op jit(solution)/shard_map/all_to_all | solution.py:230
  245.8 4.7 %rim_lines.3 = bf16[16,128,256]{2,1,0:T(8,128)(2,1)} custom-call(f32[128,8,1024]{2,1,0:T(8,128)} %get-tuple-element.21.flat, f32[2,8,1024]{2,1,0:T(8,128)} %pad_maximum_fusion.rows_in, f32[128,8,2]{2,1,0:T(8,128)} %copy.251.sides), custom_call_target="tpu_custom_call" | custom-call | flops 4194304 | bytes 8388608 | tf_op jit(solution)/shard_map/rim_lines/pallas_call | solution.py:213
  250.5 20.2 %all-to-all-done.4 = bf16[16,128,256]{2,1,0:T(8,128)(2,1)S(1)} async-done(((bf16[16,128,256]{2,1,0:T(8,128)(2,1)}), bf16[16,128,256]{2,1,0:T(8,128)(2,1)S(1)}, u32[]{:S(2)}, u32[]{:S(2)}) %all-to-all-start.4) | async-done | bytes 1048608 | tf_op jit(solution)/shard_map/all_to_all | solution.py:230
  270.6 5.0 %all-to-all-start.5 = ((bf16[16,128,256]{2,1,0:T(8,128)(2,1)}), bf16[16,128,256]{2,1,0:T(8,128)(2,1)S(1)}, u32[]{:S(2)}, u32[]{:S(2)}) async-start(bf16[16,128,256]{2,1,0:T(8,128)(2,1)} %rim_lines.3), calls=%async_computation.5 | async-start | bytes 2097152 | tf_op jit(solution)/shard_map/all_to_all | solution.py:230
  275.7 3.6 fusion.51
  279.3 2.2 fusion.3
  285.7 14.8 %all-to-all-done.5 = bf16[16,128,256]{2,1,0:T(8,128)(2,1)S(1)} async-done(((bf16[16,128,256]{2,1,0:T(8,128)(2,1)}), bf16[16,128,256]{2,1,0:T(8,128)(2,1)S(1)}, u32[]{:S(2)}, u32[]{:S(2)}) %all-to-all-start.5) | async-done | bytes 1048608 | tf_op jit(solution)/shard_map/all_to_all | solution.py:230
  300.5 3.6 fusion.52
  304.2 2.2 fusion.2
  311.5 2.9 fusion.26
  316.4 2.9 fusion.30
  319.3 3.2 collective-permute-done.23
  331.2 1.8 add_convert_fusion
  333.0 5.1 %all-to-all-start.7 = ((bf16[16,64,512]{2,1,0:T(8,128)(2,1)}), bf16[16,64,512]{2,1,0:T(8,128)(2,1)S(1)}, u32[]{:S(2)}, u32[]{:S(2)}) async-start(bf16[16,64,512]{2,1,0:T(8,128)(2,1)} %add_convert_fusion), calls=%async_computation.7 | async-start | bytes 2097152 | tf_op jit(solution)/shard_map/all_to_all | solution.py:230
  342.2 4.7 %collective-permute-done.25 = bf16[16,64,256]{2,1,0:T(8,128)(2,1)} collective-permute-done((bf16[16,64,256]{2,1,0:T(8,128)(2,1)}, bf16[16,64,256]{2,1,0:T(8,128)(2,1)}, u32[]{:S(2)}, u32[]{:S(2)}) %collective-permute-start.25) | collective-permute-done | bytes 524320 | tf_op jit(solution)/shard_map/ppermute | solution.py:239
  353.5 9.4 %all-to-all-done.7.lines = bf16[16,64,512]{2,1,0:T(8,128)(2,1)S(1)} async-done(((bf16[16,64,512]{2,1,0:T(8,128)(2,1)}), bf16[16,64,512]{2,1,0:T(8,128)(2,1)S(1)}, u32[]{:S(2)}, u32[]{:S(2)}) %all-to-all-start.7) | async-done | bytes 1048608 | tf_op jit(solution)/shard_map/all_to_all | solution.py:230
  362.9 5.0 %all-to-all-start.6 = ((bf16[16,64,512]{2,1,0:T(8,128)(2,1)}), bf16[16,64,512]{2,1,0:T(8,128)(2,1)S(1)}, u32[]{:S(2)}, u32[]{:S(2)}) async-start(bf16[16,64,512]{2,1,0:T(8,128)(2,1)} %add_convert_fusion.1), calls=%async_computation.6 | async-start | bytes 2097152 | tf_op jit(solution)/shard_map/all_to_all | solution.py:230
  367.9 2.8 add_lines.2.rest_0_
  370.7 22.0 %all-to-all-done.6.lines = bf16[16,64,512]{2,1,0:T(8,128)(2,1)S(1)} async-done(((bf16[16,64,512]{2,1,0:T(8,128)(2,1)}), bf16[16,64,512]{2,1,0:T(8,128)(2,1)S(1)}, u32[]{:S(2)}, u32[]{:S(2)}) %all-to-all-start.6) | async-done | bytes 1048608 | tf_op jit(solution)/shard_map/all_to_all | solution.py:230
  393.8 2.8 add_lines.3
  (142 shorter events, 65.0 us)
Async XLA Ops:
  7.2 68.5 %all-gather.3.cloned.1.call-start = ((), (), s32[]{:S(2)}) async-start(), calls=%async_computation.8 | async-start | bytes 4456448 | tf_op jit(solution)/shard_map/all_gather | solution.py:324
  8.9 46.2 %copy-start.9 = (bf16[128,2048]{1,0:T(8,128)(2,1)S(1)}, bf16[128,2048]{1,0:T(8,128)(2,1)}, u32[]{:S(2)}) copy-start(bf16[128,2048]{1,0:T(8,128)(2,1)} %param.12) | copy-start | bytes 1572868
  8.9 124.6 %all-gather.5.cloned.1.call-start = ((), (), s32[]{:S(2)}) async-start(), calls=%async_computation.9 | async-start | bytes 4456448 | tf_op jit(solution)/shard_map/all_gather | solution.py:330
  59.7 36.0 %all-to-all-start = ((bf16[16,128,256]{2,1,0:T(8,128)(2,1)}), bf16[16,128,256]{2,1,0:T(8,128)(2,1)S(1)}, u32[]{:S(2)}, u32[]{:S(2)}) async-start(bf16[16,128,256]{2,1,0:T(8,128)(2,1)} %as_lines.2), calls=%async_computation | async-start | bytes 2097152 | tf_op jit(solution)/shard_map/all_to_all | solution.py:230
  79.4 34.3 %collective-permute-start.4 = (bf16[16,64,256]{2,1,0:T(8,128)(2,1)S(1)}, bf16[16,64,256]{2,1,0:T(8,128)(2,1)}, u32[]{:S(2)}, u32[]{:S(2)}) collective-permute-start(bf16[16,64,256]{2,1,0:T(8,128)(2,1)S(1)} %bitcast.187), channel_id=1, source_target_pairs={{0,1},{1,0},{2,3},{3,2},{4,5},{5,4},{6,7},{7,6},{8,9},{9,8},{10,11... | collective-permute-start | bytes 1572872 | tf_op jit(solution)/shard_map/ppermute | solution.py:239
  81.5 34.7 %collective-permute-start.3 = (bf16[16,64,256]{2,1,0:T(8,128)(2,1)S(1)}, bf16[16,64,256]{2,1,0:T(8,128)(2,1)}, u32[]{:S(2)}, u32[]{:S(2)}) collective-permute-start(bf16[16,64,256]{2,1,0:T(8,128)(2,1)S(1)} %bitcast.188), channel_id=1, source_target_pairs={{0,2},{2,0},{4,6},{6,4},{8,10},{10,8},{12,14},{14,12},{16,18},{18,... | collective-permute-start | bytes 1572872 | tf_op jit(solution)/shard_map/ppermute | solution.py:240
  95.7 6.4 %copy-start = (bf16[1024,2048]{1,0:T(8,128)(2,1)S(1)}, bf16[1024,2048]{1,0:T(8,128)(2,1)}, u32[]{:S(2)}) copy-start(bf16[1024,2048]{1,0:T(8,128)(2,1)} %param.13) | copy-start | bytes 12582916
  99.3 12.3 %collective-permute-start.1 = (bf16[16,64,256]{2,1,0:T(8,128)(2,1)S(1)}, bf16[16,64,256]{2,1,0:T(8,128)(2,1)S(1)}, u32[]{:S(2)}, u32[]{:S(2)}) collective-permute-start(bf16[16,64,256]{2,1,0:T(8,128)(2,1)S(1)} %bitcast.200), channel_id=1, source_target_pairs={{0,1},{1,0},{2,3},{3,2},{4,5},{5,4},{6,7},{7,6},{8,9},{9,8},{10,11... | collective-permute-start | bytes 1572872 | tf_op jit(solution)/shard_map/ppermute | solution.py:239
  100.5 15.2 %collective-permute-start = (bf16[16,64,256]{2,1,0:T(8,128)(2,1)S(1)}, bf16[16,64,256]{2,1,0:T(8,128)(2,1)S(1)}, u32[]{:S(2)}, u32[]{:S(2)}) collective-permute-start(bf16[16,64,256]{2,1,0:T(8,128)(2,1)S(1)} %bitcast.201), channel_id=1, source_target_pairs={{0,2},{2,0},{4,6},{6,4},{8,10},{10,8},{12,14},{14,12},{16,18},{18,... | collective-permute-start | bytes 1572872 | tf_op jit(solution)/shard_map/ppermute | solution.py:240
  111.6 6.2 %collective-permute-start.2 = (bf16[16,64,256]{2,1,0:T(8,128)(2,1)S(1)}, bf16[16,64,256]{2,1,0:T(8,128)(2,1)S(1)}, u32[]{:S(2)}, u32[]{:S(2)}) collective-permute-start(bf16[16,64,256]{2,1,0:T(8,128)(2,1)S(1)} %collective-permute-done.1), channel_id=1, source_target_pairs={{0,2},{2,0},{4,6},{6,4},{8,10},{10,8},{12,14},{14,12},{16,18},{18,... | collective-permute-start | bytes 1572872 | tf_op jit(solution)/shard_map/ppermute | solution.py:243
  113.7 4.5 %collective-permute-start.5 = (bf16[16,64,256]{2,1,0:T(8,128)(2,1)}, bf16[16,64,256]{2,1,0:T(8,128)(2,1)S(1)}, u32[]{:S(2)}, u32[]{:S(2)}) collective-permute-start(bf16[16,64,256]{2,1,0:T(8,128)(2,1)} %collective-permute-done.4), channel_id=1, source_target_pairs={{0,2},{2,0},{4,6},{6,4},{8,10},{10,8},{12,14},{14,12},{16,18},{18,... | collective-permute-start | bytes 1572872 | tf_op jit(solution)/shard_map/ppermute | solution.py:243
  120.2 46.5 %all-to-all-start.2 = ((bf16[16,64,512]{2,1,0:T(8,128)(2,1)}), bf16[16,64,512]{2,1,0:T(8,128)(2,1)S(1)}, u32[]{:S(2)}, u32[]{:S(2)}) async-start(bf16[16,64,512]{2,1,0:T(8,128)(2,1)} %add_convert_fusion.3), calls=%async_computation.2 | async-start | bytes 2097152 | tf_op jit(solution)/shard_map/all_to_all | solution.py:230
  133.6 5.4 %copy-start.13 = (bf16[1024,2048]{1,0:T(8,128)(2,1)S(1)}, bf16[1024,2048]{1,0:T(8,128)(2,1)}, u32[]{:S(2)}) copy-start(bf16[1024,2048]{1,0:T(8,128)(2,1)} %all-gather.5.cloned.1.call-done) | copy-start | bytes 12582916
  137.2 3.7 copy-start.1
  137.2 13.3 %collective-permute-start.10 = (bf16[16,64,256]{2,1,0:T(8,128)(2,1)S(1)}, bf16[16,64,256]{2,1,0:T(8,128)(2,1)S(1)}, u32[]{:S(2)}, u32[]{:S(2)}) collective-permute-start(bf16[16,64,256]{2,1,0:T(8,128)(2,1)S(1)} %bitcast.194), channel_id=1, source_target_pairs={{0,1},{1,0},{2,3},{3,2},{4,5},{5,4},{6,7},{7,6},{8,9},{9,8},{10,11... | collective-permute-start | bytes 1572872 | tf_op jit(solution)/shard_map/ppermute | solution.py:239
  138.4 24.9 %collective-permute-start.9 = (bf16[16,64,256]{2,1,0:T(8,128)(2,1)S(1)}, bf16[16,64,256]{2,1,0:T(8,128)(2,1)S(1)}, u32[]{:S(2)}, u32[]{:S(2)}) collective-permute-start(bf16[16,64,256]{2,1,0:T(8,128)(2,1)S(1)} %bitcast.195), channel_id=1, source_target_pairs={{0,2},{2,0},{4,6},{6,4},{8,10},{10,8},{12,14},{14,12},{16,18},{18,... | collective-permute-start | bytes 1572872 | tf_op jit(solution)/shard_map/ppermute | solution.py:240
  140.2 21.5 %collective-permute-start.7 = (bf16[16,64,256]{2,1,0:T(8,128)(2,1)S(1)}, bf16[16,64,256]{2,1,0:T(8,128)(2,1)S(1)}, u32[]{:S(2)}, u32[]{:S(2)}) collective-permute-start(bf16[16,64,256]{2,1,0:T(8,128)(2,1)S(1)} %bitcast.197), channel_id=1, source_target_pairs={{0,1},{1,0},{2,3},{3,2},{4,5},{5,4},{6,7},{7,6},{8,9},{9,8},{10,11... | collective-permute-start | bytes 1572872 | tf_op jit(solution)/shard_map/ppermute | solution.py:239
  140.6 23.2 %collective-permute-start.6 = (bf16[16,64,256]{2,1,0:T(8,128)(2,1)S(1)}, bf16[16,64,256]{2,1,0:T(8,128)(2,1)S(1)}, u32[]{:S(2)}, u32[]{:S(2)}) collective-permute-start(bf16[16,64,256]{2,1,0:T(8,128)(2,1)S(1)} %bitcast.198), channel_id=1, source_target_pairs={{0,2},{2,0},{4,6},{6,4},{8,10},{10,8},{12,14},{14,12},{16,18},{18,... | collective-permute-start | bytes 1572872 | tf_op jit(solution)/shard_map/ppermute | solution.py:240
  151.0 13.8 %collective-permute-start.11 = (bf16[16,64,256]{2,1,0:T(8,128)(2,1)S(1)}, bf16[16,64,256]{2,1,0:T(8,128)(2,1)S(1)}, u32[]{:S(2)}, u32[]{:S(2)}) collective-permute-start(bf16[16,64,256]{2,1,0:T(8,128)(2,1)S(1)} %collective-permute-done.10), channel_id=1, source_target_pairs={{0,2},{2,0},{4,6},{6,4},{8,10},{10,8},{12,14},{14,12},{16,18},{18,... | collective-permute-start | bytes 1572872 | tf_op jit(solution)/shard_map/ppermute | solution.py:243
  161.7 2.6 collective-permute-start.8
  166.7 28.9 %all-to-all-start.3 = ((bf16[16,64,512]{2,1,0:T(8,128)(2,1)}), bf16[16,64,512]{2,1,0:T(8,128)(2,1)S(1)}, u32[]{:S(2)}, u32[]{:S(2)}) async-start(bf16[16,64,512]{2,1,0:T(8,128)(2,1)} %add_convert_fusion.2), calls=%async_computation.3 | async-start | bytes 2097152 | tf_op jit(solution)/shard_map/all_to_all | solution.py:230
  171.3 28.8 %copy-start.4 = (bf16[8,2,64,512]{3,0,1,2:T(8,128)(2,1)}, bf16[8,2,64,512]{3,0,1,2:T(8,128)(2,1)S(1)}, u32[]{:S(2)}) copy-start(bf16[8,2,64,512]{3,0,1,2:T(8,128)(2,1)S(1)} %copy.268) | copy-start | bytes 3145732
  174.0 56.1 %collective-permute-start.15 = (bf16[1024,512]{1,0:T(8,128)(2,1)}, bf16[1024,512]{1,0:T(8,128)(2,1)S(1)}, u32[]{:S(2)}, u32[]{:S(2)}) collective-permute-start(bf16[1024,512]{1,0:T(8,128)(2,1)} %constant_dynamic-slice_fusion), channel_id=1, source_target_pairs={{0,1},{1,0},{2,3},{3,2},{4,5},{5,4},{6,7},{7,6},{8,9},{9,8},{10,11... | collective-permute-start | bytes 3145736 | tf_op jit(solution)/shard_map/ppermute | solution.py:276
  198.4 9.0 %copy-start.5 = (bf16[8,2,64,512]{3,0,1,2:T(8,128)(2,1)}, bf16[8,2,64,512]{3,0,1,2:T(8,128)(2,1)S(1)}, u32[]{:S(2)}) copy-start(bf16[8,2,64,512]{3,0,1,2:T(8,128)(2,1)S(1)} %copy.267) | copy-start | bytes 3145732
  198.9 6.8 %collective-permute-start.14 = (bf16[128,8]{0,1:T(8,128)(2,1)S(1)}, bf16[128,8]{0,1:T(8,128)(2,1)S(1)}, u32[]{:S(2)}, u32[]{:S(2)}) collective-permute-start(bf16[128,8]{0,1:T(8,128)(2,1)S(1)} %maximum_select_fusion), channel_id=1, source_target_pairs={{0,1},{1,0},{2,3},{3,2},{4,5},{5,4},{6,7},{7,6},{8,9},{9,8},{10,11... | collective-permute-start | bytes 6152 | tf_op jit(solution)/shard_map/ppermute | solution.py:307
  200.1 6.7 %collective-permute-start.13 = (bf16[8,1024]{1,0:T(8,128)(2,1)S(1)}, bf16[8,1024]{1,0:T(8,128)(2,1)S(1)}, u32[]{:S(2)}, u32[]{:S(2)}) collective-permute-start(bf16[8,1024]{1,0:T(8,128)(2,1)S(1)} %bitcast.209), channel_id=1, source_target_pairs={{2,0},{4,2},{6,4},{8,6},{10,8},{12,10},{14,12},{16,14},{18,16},{20... | collective-permute-start | bytes 49160 | tf_op jit(solution)/shard_map/ppermute | solution.py:301
  202.0 4.7 %collective-permute-start.12 = (bf16[8,1024]{1,0:T(8,128)(2,1)S(1)}, bf16[8,1024]{1,0:T(8,128)(2,1)S(1)}, u32[]{:S(2)}, u32[]{:S(2)}) collective-permute-start(bf16[8,1024]{1,0:T(8,128)(2,1)S(1)} %bitcast.210), channel_id=1, source_target_pairs={{0,2},{2,4},{4,6},{6,8},{8,10},{10,12},{12,14},{14,16},{16,18},{18... | collective-permute-start | bytes 49160 | tf_op jit(solution)/shard_map/ppermute | solution.py:301
  223.6 6.5 %collective-permute-start.18 = (f32[128,8]{0,1:T(8,128)S(1)}, f32[128,8]{0,1:T(8,128)S(1)}, u32[]{:S(2)}, u32[]{:S(2)}) collective-permute-start(f32[128,8]{0,1:T(8,128)S(1)} %bitcast.217), channel_id=1, source_target_pairs={{0,1},{1,0},{2,3},{3,2},{4,5},{5,4},{6,7},{7,6},{8,9},{9,8},{10,11... | collective-permute-start | bytes 12296 | tf_op jit(solution)/shard_map/ppermute | solution.py:307
  223.9 7.2 %collective-permute-start.16 = (f32[8,1024]{1,0:T(8,128)S(1)}, f32[8,1024]{1,0:T(8,128)S(1)}, u32[]{:S(2)}, u32[]{:S(2)}) collective-permute-start(f32[8,1024]{1,0:T(8,128)S(1)} %get-tuple-element.44), channel_id=1, source_target_pairs={{0,2},{2,4},{4,6},{6,8},{8,10},{10,12},{12,14},{14,16},{16,18},{18... | collective-permute-start | bytes 98312 | tf_op jit(solution)/shard_map/ppermute | solution.py:301
  228.2 5.2 %collective-permute-start.17 = (f32[8,1024]{1,0:T(8,128)S(1)}, f32[8,1024]{1,0:T(8,128)S(1)}, u32[]{:S(2)}, u32[]{:S(2)}) collective-permute-start(f32[8,1024]{1,0:T(8,128)S(1)} %get-tuple-element.45), channel_id=1, source_target_pairs={{2,0},{4,2},{6,4},{8,6},{10,8},{12,10},{14,12},{16,14},{18,16},{20... | collective-permute-start | bytes 98312 | tf_op jit(solution)/shard_map/ppermute | solution.py:301
  238.8 31.8 %all-to-all-start.4 = ((bf16[16,128,256]{2,1,0:T(8,128)(2,1)}), bf16[16,128,256]{2,1,0:T(8,128)(2,1)S(1)}, u32[]{:S(2)}, u32[]{:S(2)}) async-start(bf16[16,128,256]{2,1,0:T(8,128)(2,1)} %rim_lines.2), calls=%async_computation.4 | async-start | bytes 2097152 | tf_op jit(solution)/shard_map/all_to_all | solution.py:230
  270.6 29.8 %all-to-all-start.5 = ((bf16[16,128,256]{2,1,0:T(8,128)(2,1)}), bf16[16,128,256]{2,1,0:T(8,128)(2,1)S(1)}, u32[]{:S(2)}, u32[]{:S(2)}) async-start(bf16[16,128,256]{2,1,0:T(8,128)(2,1)} %rim_lines.3), calls=%async_computation.5 | async-start | bytes 2097152 | tf_op jit(solution)/shard_map/all_to_all | solution.py:230
  275.7 3.7 copy-start.11
  284.1 44.0 %collective-permute-start.27 = (bf16[16,64,256]{2,1,0:T(8,128)(2,1)}, bf16[16,64,256]{2,1,0:T(8,128)(2,1)}, u32[]{:S(2)}, u32[]{:S(2)}) collective-permute-start(bf16[16,64,256]{2,1,0:T(8,128)(2,1)} %get-tuple-element.28), channel_id=1, source_target_pairs={{0,2},{2,0},{4,6},{6,4},{8,10},{10,8},{12,14},{14,12},{16,18},{18,... | collective-permute-start | bytes 1572872 | tf_op jit(solution)/shard_map/ppermute | solution.py:240
  284.5 42.1 %collective-permute-start.28 = (bf16[16,64,256]{2,1,0:T(8,128)(2,1)}, bf16[16,64,256]{2,1,0:T(8,128)(2,1)}, u32[]{:S(2)}, u32[]{:S(2)}) collective-permute-start(bf16[16,64,256]{2,1,0:T(8,128)(2,1)} %get-tuple-element.28), channel_id=1, source_target_pairs={{0,1},{1,0},{2,3},{3,2},{4,5},{5,4},{6,7},{7,6},{8,9},{9,8},{10,11... | collective-permute-start | bytes 1572872 | tf_op jit(solution)/shard_map/ppermute | solution.py:239
  308.8 13.7 %collective-permute-start.23 = (bf16[16,64,256]{2,1,0:T(8,128)(2,1)S(1)}, bf16[16,64,256]{2,1,0:T(8,128)(2,1)S(1)}, u32[]{:S(2)}, u32[]{:S(2)}) collective-permute-start(bf16[16,64,256]{2,1,0:T(8,128)(2,1)S(1)} %get-tuple-element.32), channel_id=1, source_target_pairs={{0,1},{1,0},{2,3},{3,2},{4,5},{5,4},{6,7},{7,6},{8,9},{9,8},{10,11... | collective-permute-start | bytes 1572872 | tf_op jit(solution)/shard_map/ppermute | solution.py:239
  310.0 13.7 %collective-permute-start.24 = (bf16[16,64,256]{2,1,0:T(8,128)(2,1)S(1)}, bf16[16,64,256]{2,1,0:T(8,128)(2,1)S(1)}, u32[]{:S(2)}, u32[]{:S(2)}) collective-permute-start(bf16[16,64,256]{2,1,0:T(8,128)(2,1)S(1)} %get-tuple-element.32), channel_id=1, source_target_pairs={{0,2},{2,0},{4,6},{6,4},{8,10},{10,8},{12,14},{14,12},{16,18},{18,... | collective-permute-start | bytes 1572872 | tf_op jit(solution)/shard_map/ppermute | solution.py:240
  314.4 24.5 %collective-permute-start.19 = (bf16[16,64,256]{2,1,0:T(8,128)(2,1)}, bf16[16,64,256]{2,1,0:T(8,128)(2,1)S(1)}, u32[]{:S(2)}, u32[]{:S(2)}) collective-permute-start(bf16[16,64,256]{2,1,0:T(8,128)(2,1)} %get-tuple-element.29), channel_id=1, source_target_pairs={{0,2},{2,0},{4,6},{6,4},{8,10},{10,8},{12,14},{14,12},{16,18},{18,... | collective-permute-start | bytes 1572872 | tf_op jit(solution)/shard_map/ppermute | solution.py:240
  322.5 15.6 %collective-permute-start.20 = (bf16[16,64,256]{2,1,0:T(8,128)(2,1)}, bf16[16,64,256]{2,1,0:T(8,128)(2,1)S(1)}, u32[]{:S(2)}, u32[]{:S(2)}) collective-permute-start(bf16[16,64,256]{2,1,0:T(8,128)(2,1)} %get-tuple-element.29), channel_id=1, source_target_pairs={{0,1},{1,0},{2,3},{3,2},{4,5},{5,4},{6,7},{7,6},{8,9},{9,8},{10,11... | collective-permute-start | bytes 1572872 | tf_op jit(solution)/shard_map/ppermute | solution.py:239
  323.7 16.8 %collective-permute-start.22 = (bf16[16,64,256]{2,1,0:T(8,128)(2,1)}, bf16[16,64,256]{2,1,0:T(8,128)(2,1)}, u32[]{:S(2)}, u32[]{:S(2)}) collective-permute-start(bf16[16,64,256]{2,1,0:T(8,128)(2,1)} %get-tuple-element.26), channel_id=1, source_target_pairs={{0,2},{2,0},{4,6},{6,4},{8,10},{10,8},{12,14},{14,12},{16,18},{18,... | collective-permute-start | bytes 1572872 | tf_op jit(solution)/shard_map/ppermute | solution.py:240
  326.6 3.8 collective-permute-start.30
  328.2 3.0 collective-permute-start.29
  330.4 16.5 %collective-permute-start.25 = (bf16[16,64,256]{2,1,0:T(8,128)(2,1)}, bf16[16,64,256]{2,1,0:T(8,128)(2,1)}, u32[]{:S(2)}, u32[]{:S(2)}) collective-permute-start(bf16[16,64,256]{2,1,0:T(8,128)(2,1)} %get-tuple-element.26), channel_id=1, source_target_pairs={{0,1},{1,0},{2,3},{3,2},{4,5},{5,4},{6,7},{7,6},{8,9},{9,8},{10,11... | collective-permute-start | bytes 1572872 | tf_op jit(solution)/shard_map/ppermute | solution.py:239
  333.0 29.9 %all-to-all-start.7 = ((bf16[16,64,512]{2,1,0:T(8,128)(2,1)}), bf16[16,64,512]{2,1,0:T(8,128)(2,1)S(1)}, u32[]{:S(2)}, u32[]{:S(2)}) async-start(bf16[16,64,512]{2,1,0:T(8,128)(2,1)} %add_convert_fusion), calls=%async_computation.7 | async-start | bytes 2097152 | tf_op jit(solution)/shard_map/all_to_all | solution.py:230
  338.5 11.5 %collective-permute-start.21 = (bf16[16,64,256]{2,1,0:T(8,128)(2,1)S(1)}, bf16[16,64,256]{2,1,0:T(8,128)(2,1)S(1)}, u32[]{:S(2)}, u32[]{:S(2)}) collective-permute-start(bf16[16,64,256]{2,1,0:T(8,128)(2,1)S(1)} %collective-permute-done.20), channel_id=1, source_target_pairs={{0,2},{2,0},{4,6},{6,4},{8,10},{10,8},{12,14},{14,12},{16,18},{18,... | collective-permute-start | bytes 1572872 | tf_op jit(solution)/shard_map/ppermute | solution.py:243
  346.9 3.5 collective-permute-start.26
  362.9 5.0 %copy-start.6 = (bf16[16,64,512]{2,1,0:T(8,128)(2,1)}, bf16[16,64,512]{2,1,0:T(8,128)(2,1)S(1)}, u32[]{:S(2)}) copy-start(bf16[16,64,512]{2,1,0:T(8,128)(2,1)S(1)} %all-to-all-done.7.lines) | copy-start | bytes 3145732
  362.9 29.8 %all-to-all-start.6 = ((bf16[16,64,512]{2,1,0:T(8,128)(2,1)}), bf16[16,64,512]{2,1,0:T(8,128)(2,1)S(1)}, u32[]{:S(2)}, u32[]{:S(2)}) async-start(bf16[16,64,512]{2,1,0:T(8,128)(2,1)} %add_convert_fusion.1), calls=%async_computation.6 | async-start | bytes 2097152 | tf_op jit(solution)/shard_map/all_to_all | solution.py:230
  (6 other events, 11.3 us)
Sparse Core Ops, SparseCore 0:
  10.7 64.8 all-gather.2
  77.8 55.6 all-gather.4

commit v3 on v2

--- a/solution.py
+++ b/solution.py
@@ -374,15 +374,15 @@
                 preferred_element_type=F32,
             )
         pulled.append(total.astype(BF16).reshape(n_x, rows, piece))
-    gradient = far = None
+    gradient = cross = None
     for h in range(CHUNKS):
         at, end = h * cut, (h + 1) * cut
         carried = 0.0
         for w, span in enumerate(spans):
             last = w == CHUNKS - 1
-            held = far if h > 0 and last else None
+            held = cross if h > 0 and last else None
             planes = plane_pieces(pulled[w][:, at:end], parts, held, h == 0 and last)
-            far = planes[-2] if last else far
+            cross = planes[-1] if last else cross
             for plane, matrix in zip(planes, columns_y):
                 carried = carried + jnp.einsum(
                     "brk,kc->brc", plane, matrix[span], preferred_element_type=F32

time: 405 us -> 405 us (level)
    ppermute x8, waiting for transfers between devices: 34.1 us -> 39.4 us  [plane_pieces(): far = lax.ppermute(sent, 'gy', [(0, 1), (1, 0)])]
    all_to_all x7, waiting for transfers between devices: 100 us -> 96.2 us  [swap_all(): return lax.all_to_all(lines, 'gx', 0, 0, tiled=True)]
  transfers between devices with their start and end apart: 40 -> 40, of which waited for: 15 -> 16; matrix products, arithmetic and copies ran while one was open for 19% -> 19% of each run, Pallas kernels for 7% -> 7%
where the time goes in v3:
time: 405 us; the launch traced here: 403 us
  waiting for transfers between devices  152 us (38%)
  starting transfers between devices  76.5 us (19%)
  matrix products  58.8 us (15%)
  blocking collectives  42.3 us (10%)
  Pallas kernels  37.3 us (9%)
  local copies, waits for them, and re-layouts  18.2 us (4%)
  between operations  14.6 us (4%)
    all_to_all x7, waiting for transfers between devices, swap_all(): return lax.all_to_all(lines, 'gx', 0, 0, tiled=True)  96.2 us
    all_to_all x1, blocking collectives, swap_all(): return lax.all_to_all(lines, 'gx', 0, 0, tiled=True)  42.3 us
    all_to_all x7, starting transfers between devices, swap_all(): return lax.all_to_all(lines, 'gx', 0, 0, tiled=True)  41.5 us
    ppermute x8, waiting for transfers between devices, plane_pieces(): far = lax.ppermute(sent, 'gy', [(0, 1), (1, 0)])  39.4 us
    dot_general x16, matrix products, per_device(): jnp.einsum('brk,kc->brc', plane, matrix[span], preferred_element_type=F32)  22.6 us
    pallas_call x1, Pallas kernels, forward(): pl.pallas_call(forward_body, grid=(rows // STEP,), in_specs=[start] * CHU...  14.6 us
    dot_general x16, matrix products, per_device(): jnp.einsum('brc,kc->brk', plane, matrix[:, span], preferred_element_type=...  12.5 us
    dot_general x4, matrix products, per_device(): smoothed = jnp.dot(matrix_x[h], lines[w], preferred_element_type=F32)  11.9 us
  transfers between devices with their start and end apart: 40, of which 16 were waited for; matrix products, arithmetic and copies ran while one was open for 19% of the time, Pallas kernels for 7%

profile of v3, /device:TPU:9, one launch (start us, length us, event | category | flops | bytes accessed | tf_op | source)
XLA Modules:
  0.0 402.9 jit_solution(15392865809082310331)
XLA Ops:
  9.0 3.8 as_lines.3
  12.8 42.3 %all_to_all.40 = bf16[16,128,256]{2,1,0:T(8,128)(2,1)S(1)} all-to-all(bf16[16,128,256]{2,1,0:T(8,128)(2,1)} %as_lines.3), channel_id=1, replica_groups=mesh['gx'=16,'gy'=2] {'gx'}, dimensions={0} | all-to-all | bytes 2097152 | tf_op jit(solution)/shard_map/all_to_all | solution.py:230
  55.9 3.8 as_lines.2
  59.7 7.6 %all-to-all-start = ((bf16[16,128,256]{2,1,0:T(8,128)(2,1)}), bf16[16,128,256]{2,1,0:T(8,128)(2,1)S(1)}, u32[]{:S(2)}, u32[]{:S(2)}) async-start(bf16[16,128,256]{2,1,0:T(8,128)(2,1)} %as_lines.2), calls=%async_computation | async-start | bytes 2097152 | tf_op jit(solution)/shard_map/all_to_all | solution.py:230
  67.3 8.4 %all-gather.3.cloned.1.call-done = bf16[1024,2048]{1,0:T(8,128)(2,1)} async-done(((bf16[64,2048]{1,0:T(8,128)(2,1)}), bf16[1024,2048]{1,0:T(8,128)(2,1)}) %all-gather.3.cloned.1.call-update) | async-done | bytes 4194320 | tf_op jit(solution)/shard_map/all_gather | solution.py:324
  75.7 3.5 fusion.4
  79.4 2.1 collective-permute-start.4
  82.0 13.6 %all-to-all-done = bf16[16,128,256]{2,1,0:T(8,128)(2,1)S(1)} async-done(((bf16[16,128,256]{2,1,0:T(8,128)(2,1)}), bf16[16,128,256]{2,1,0:T(8,128)(2,1)S(1)}, u32[]{:S(2)}, u32[]{:S(2)}) %all-to-all-start) | async-done | bytes 1048608 | tf_op jit(solution)/shard_map/all_to_all | solution.py:230
  95.7 3.6 convolution_convert_fusion.3
  103.0 8.5 %collective-permute-done.1 = bf16[16,64,256]{2,1,0:T(8,128)(2,1)S(1)} collective-permute-done((bf16[16,64,256]{2,1,0:T(8,128)(2,1)S(1)}, bf16[16,64,256]{2,1,0:T(8,128)(2,1)S(1)}, u32[]{:S(2)}, u32[]{:S(2)}) %collective-permute-start.1) | collective-permute-done | bytes 524320 | tf_op jit(solution)/shard_map/ppermute | solution.py:239
  111.6 2.1 collective-permute-start.2
  118.3 1.9 add_convert_fusion.3
  120.2 8.0 %all-to-all-start.2 = ((bf16[16,64,512]{2,1,0:T(8,128)(2,1)}), bf16[16,64,512]{2,1,0:T(8,128)(2,1)S(1)}, u32[]{:S(2)}, u32[]{:S(2)}) async-start(bf16[16,64,512]{2,1,0:T(8,128)(2,1)} %add_convert_fusion.3), calls=%async_computation.2 | async-start | bytes 2097152 | tf_op jit(solution)/shard_map/all_to_all | solution.py:230
  128.2 5.4 %all-gather.5.cloned.1.call-done = bf16[1024,2048]{1,0:T(8,128)(2,1)} async-done(((bf16[64,2048]{1,0:T(8,128)(2,1)}), bf16[1024,2048]{1,0:T(8,128)(2,1)}) %all-gather.5.cloned.1.call-update) | async-done | bytes 4194320 | tf_op jit(solution)/shard_map/all_gather | solution.py:330
  133.6 3.6 convolution_convert_fusion
  141.8 8.7 %collective-permute-done.10 = bf16[16,64,256]{2,1,0:T(8,128)(2,1)S(1)} collective-permute-done((bf16[16,64,256]{2,1,0:T(8,128)(2,1)S(1)}, bf16[16,64,256]{2,1,0:T(8,128)(2,1)S(1)}, u32[]{:S(2)}, u32[]{:S(2)}) %collective-permute-start.10) | collective-permute-done | bytes 524320 | tf_op jit(solution)/shard_map/ppermute | solution.py:239
  152.8 9.0 %collective-permute-done.7 = bf16[16,64,256]{2,1,0:T(8,128)(2,1)S(1)} collective-permute-done((bf16[16,64,256]{2,1,0:T(8,128)(2,1)S(1)}, bf16[16,64,256]{2,1,0:T(8,128)(2,1)S(1)}, u32[]{:S(2)}, u32[]{:S(2)}) %collective-permute-start.7) | collective-permute-done | bytes 524320 | tf_op jit(solution)/shard_map/ppermute | solution.py:239
  164.8 1.9 add_convert_fusion.2
  166.7 4.0 all-to-all-start.3
  171.7 2.3 constant_dynamic-slice_fusion
  175.2 20.4 %all-to-all-done.3 = bf16[16,64,512]{2,1,0:T(8,128)(2,1)S(1)} async-done(((bf16[16,64,512]{2,1,0:T(8,128)(2,1)}), bf16[16,64,512]{2,1,0:T(8,128)(2,1)S(1)}, u32[]{:S(2)}, u32[]{:S(2)}) %all-to-all-start.3) | async-done | bytes 1048608 | tf_op jit(solution)/shard_map/all_to_all | solution.py:230
  200.1 1.9 collective-permute-start.13
  202.0 3.6 collective-permute-start.12
  207.4 14.6 %forward.1 = (f32[128,8,1024]{2,1,0:T(8,128)}, f32[128,8,1024]{2,1,0:T(8,128)}, f32[2,8,1024]{2,1,0:T(8,128)}, f32[128,8,2]{2,1,0:T(8,128)}) custom-call(bf16[64,8,1024]{2,1,0:T(8,128)(2,1)} %bitcast.179, bf16[64,8,1024]{2,1,0:T(8,128)(2,1)} %bitcast.182, f32[2,8,1024]{2,1,0:T(8,128)} %maximum_convert_fusion.refs_2_, f32[128,8,2]{2,1,0:T(8,128)} %copy.249.refs_3_, ...), custom_call_target="tpu_custom_call" | custom-call | flops 31457280 | bytes 29360128 | tf_op jit(solution)/shard_map/forward/pallas_call | solution.py:169
  223.9 4.2 %collective-permute-start.16 = (f32[8,1024]{1,0:T(8,128)S(1)}, f32[8,1024]{1,0:T(8,128)S(1)}, u32[]{:S(2)}, u32[]{:S(2)}) collective-permute-start(f32[8,1024]{1,0:T(8,128)S(1)} %get-tuple-element.44), channel_id=1, source_target_pairs={{0,2},{2,4},{4,6},{6,8},{8,10},{10,12},{12,14},{14,16},{16,18},{18... | collective-permute-start | bytes 98312 | tf_op jit(solution)/shard_map/ppermute | solution.py:301
  228.2 1.9 collective-permute-start.17
  231.2 2.2 collective-permute-done.17
  234.0 4.8 %rim_lines.2 = bf16[16,128,256]{2,1,0:T(8,128)(2,1)} custom-call(f32[128,8,1024]{2,1,0:T(8,128)} %get-tuple-element.21.flat, f32[2,8,1024]{2,1,0:T(8,128)} %pad_maximum_fusion.rows_in, f32[128,8,2]{2,1,0:T(8,128)} %copy.251.sides), custom_call_target="tpu_custom_call" | custom-call | flops 4194304 | bytes 8388608 | tf_op jit(solution)/shard_map/rim_lines/pallas_call | solution.py:213
  238.8 7.0 %all-to-all-start.4 = ((bf16[16,128,256]{2,1,0:T(8,128)(2,1)}), bf16[16,128,256]{2,1,0:T(8,128)(2,1)S(1)}, u32[]{:S(2)}, u32[]{:S(2)}) async-start(bf16[16,128,256]{2,1,0:T(8,128)(2,1)} %rim_lines.2), calls=%async_computation.4 | async-start | bytes 2097152 | tf_op jit(solution)/shard_map/all_to_all | solution.py:230
  245.8 4.7 %rim_lines.3 = bf16[16,128,256]{2,1,0:T(8,128)(2,1)} custom-call(f32[128,8,1024]{2,1,0:T(8,128)} %get-tuple-element.21.flat, f32[2,8,1024]{2,1,0:T(8,128)} %pad_maximum_fusion.rows_in, f32[128,8,2]{2,1,0:T(8,128)} %copy.251.sides), custom_call_target="tpu_custom_call" | custom-call | flops 4194304 | bytes 8388608 | tf_op jit(solution)/shard_map/rim_lines/pallas_call | solution.py:213
  250.5 20.2 %all-to-all-done.4 = bf16[16,128,256]{2,1,0:T(8,128)(2,1)S(1)} async-done(((bf16[16,128,256]{2,1,0:T(8,128)(2,1)}), bf16[16,128,256]{2,1,0:T(8,128)(2,1)S(1)}, u32[]{:S(2)}, u32[]{:S(2)}) %all-to-all-start.4) | async-done | bytes 1048608 | tf_op jit(solution)/shard_map/all_to_all | solution.py:230
  270.6 5.0 %all-to-all-start.5 = ((bf16[16,128,256]{2,1,0:T(8,128)(2,1)}), bf16[16,128,256]{2,1,0:T(8,128)(2,1)S(1)}, u32[]{:S(2)}, u32[]{:S(2)}) async-start(bf16[16,128,256]{2,1,0:T(8,128)(2,1)} %rim_lines.3), calls=%async_computation.5 | async-start | bytes 2097152 | tf_op jit(solution)/shard_map/all_to_all | solution.py:230
  275.7 3.6 fusion.51
  279.3 2.2 fusion.3
  285.7 14.8 %all-to-all-done.5 = bf16[16,128,256]{2,1,0:T(8,128)(2,1)S(1)} async-done(((bf16[16,128,256]{2,1,0:T(8,128)(2,1)}), bf16[16,128,256]{2,1,0:T(8,128)(2,1)S(1)}, u32[]{:S(2)}, u32[]{:S(2)}) %all-to-all-start.5) | async-done | bytes 1048608 | tf_op jit(solution)/shard_map/all_to_all | solution.py:230
  300.5 3.6 fusion.52
  304.2 2.2 fusion.2
  311.5 2.9 fusion.26
  316.4 2.9 fusion.30
  319.3 3.2 collective-permute-done.23
  332.7 4.9 %all-to-all-start.7 = ((bf16[16,64,512]{2,1,0:T(8,128)(2,1)}), bf16[16,64,512]{2,1,0:T(8,128)(2,1)S(1)}, u32[]{:S(2)}, u32[]{:S(2)}) async-start(bf16[16,64,512]{2,1,0:T(8,128)(2,1)} %add_convert_fusion), calls=%async_computation.7 | async-start | bytes 2097152 | tf_op jit(solution)/shard_map/all_to_all | solution.py:230
  342.0 10.0 %collective-permute-done.26 = bf16[16,64,256]{2,1,0:T(8,128)(2,1)S(1)} collective-permute-done((bf16[16,64,256]{2,1,0:T(8,128)(2,1)}, bf16[16,64,256]{2,1,0:T(8,128)(2,1)S(1)}, u32[]{:S(2)}, u32[]{:S(2)}) %collective-permute-start.26) | collective-permute-done | bytes 524320 | tf_op jit(solution)/shard_map/ppermute | solution.py:239
  355.3 1.8 add_convert_fusion.1
  357.2 5.2 %all-to-all-done.7.lines = bf16[16,64,512]{2,1,0:T(8,128)(2,1)S(1)} async-done(((bf16[16,64,512]{2,1,0:T(8,128)(2,1)}), bf16[16,64,512]{2,1,0:T(8,128)(2,1)S(1)}, u32[]{:S(2)}, u32[]{:S(2)}) %all-to-all-start.7) | async-done | bytes 1048608 | tf_op jit(solution)/shard_map/all_to_all | solution.py:230
  362.4 5.0 %all-to-all-start.6 = ((bf16[16,64,512]{2,1,0:T(8,128)(2,1)}), bf16[16,64,512]{2,1,0:T(8,128)(2,1)S(1)}, u32[]{:S(2)}, u32[]{:S(2)}) async-start(bf16[16,64,512]{2,1,0:T(8,128)(2,1)} %add_convert_fusion.1), calls=%async_computation.6 | async-start | bytes 2097152 | tf_op jit(solution)/shard_map/all_to_all | solution.py:230
  367.4 2.8 add_lines.2.rest_0_
  370.2 22.0 %all-to-all-done.6.lines = bf16[16,64,512]{2,1,0:T(8,128)(2,1)S(1)} async-done(((bf16[16,64,512]{2,1,0:T(8,128)(2,1)}), bf16[16,64,512]{2,1,0:T(8,128)(2,1)S(1)}, u32[]{:S(2)}, u32[]{:S(2)}) %all-to-all-start.6) | async-done | bytes 1048608 | tf_op jit(solution)/shard_map/all_to_all | solution.py:230
  393.2 2.8 add_lines.3
  (142 shorter events, 63.7 us)
Async XLA Ops:
  7.2 68.5 %all-gather.3.cloned.1.call-start = ((), (), s32[]{:S(2)}) async-start(), calls=%async_computation.8 | async-start | bytes 4456448 | tf_op jit(solution)/shard_map/all_gather | solution.py:324
  8.9 46.2 %copy-start.9 = (bf16[128,2048]{1,0:T(8,128)(2,1)S(1)}, bf16[128,2048]{1,0:T(8,128)(2,1)}, u32[]{:S(2)}) copy-start(bf16[128,2048]{1,0:T(8,128)(2,1)} %param.12) | copy-start | bytes 1572868
  8.9 124.6 %all-gather.5.cloned.1.call-start = ((), (), s32[]{:S(2)}) async-start(), calls=%async_computation.9 | async-start | bytes 4456448 | tf_op jit(solution)/shard_map/all_gather | solution.py:330
  59.7 36.0 %all-to-all-start = ((bf16[16,128,256]{2,1,0:T(8,128)(2,1)}), bf16[16,128,256]{2,1,0:T(8,128)(2,1)S(1)}, u32[]{:S(2)}, u32[]{:S(2)}) async-start(bf16[16,128,256]{2,1,0:T(8,128)(2,1)} %as_lines.2), calls=%async_computation | async-start | bytes 2097152 | tf_op jit(solution)/shard_map/all_to_all | solution.py:230
  79.4 34.3 %collective-permute-start.4 = (bf16[16,64,256]{2,1,0:T(8,128)(2,1)S(1)}, bf16[16,64,256]{2,1,0:T(8,128)(2,1)}, u32[]{:S(2)}, u32[]{:S(2)}) collective-permute-start(bf16[16,64,256]{2,1,0:T(8,128)(2,1)S(1)} %bitcast.187), channel_id=1, source_target_pairs={{0,1},{1,0},{2,3},{3,2},{4,5},{5,4},{6,7},{7,6},{8,9},{9,8},{10,11... | collective-permute-start | bytes 1572872 | tf_op jit(solution)/shard_map/ppermute | solution.py:239
  81.5 34.7 %collective-permute-start.3 = (bf16[16,64,256]{2,1,0:T(8,128)(2,1)S(1)}, bf16[16,64,256]{2,1,0:T(8,128)(2,1)}, u32[]{:S(2)}, u32[]{:S(2)}) collective-permute-start(bf16[16,64,256]{2,1,0:T(8,128)(2,1)S(1)} %bitcast.188), channel_id=1, source_target_pairs={{0,2},{2,0},{4,6},{6,4},{8,10},{10,8},{12,14},{14,12},{16,18},{18,... | collective-permute-start | bytes 1572872 | tf_op jit(solution)/shard_map/ppermute | solution.py:240
  95.7 6.4 %copy-start = (bf16[1024,2048]{1,0:T(8,128)(2,1)S(1)}, bf16[1024,2048]{1,0:T(8,128)(2,1)}, u32[]{:S(2)}) copy-start(bf16[1024,2048]{1,0:T(8,128)(2,1)} %param.13) | copy-start | bytes 12582916
  99.3 12.3 %collective-permute-start.1 = (bf16[16,64,256]{2,1,0:T(8,128)(2,1)S(1)}, bf16[16,64,256]{2,1,0:T(8,128)(2,1)S(1)}, u32[]{:S(2)}, u32[]{:S(2)}) collective-permute-start(bf16[16,64,256]{2,1,0:T(8,128)(2,1)S(1)} %bitcast.200), channel_id=1, source_target_pairs={{0,1},{1,0},{2,3},{3,2},{4,5},{5,4},{6,7},{7,6},{8,9},{9,8},{10,11... | collective-permute-start | bytes 1572872 | tf_op jit(solution)/shard_map/ppermute | solution.py:239
  100.5 15.2 %collective-permute-start = (bf16[16,64,256]{2,1,0:T(8,128)(2,1)S(1)}, bf16[16,64,256]{2,1,0:T(8,128)(2,1)S(1)}, u32[]{:S(2)}, u32[]{:S(2)}) collective-permute-start(bf16[16,64,256]{2,1,0:T(8,128)(2,1)S(1)} %bitcast.201), channel_id=1, source_target_pairs={{0,2},{2,0},{4,6},{6,4},{8,10},{10,8},{12,14},{14,12},{16,18},{18,... | collective-permute-start | bytes 1572872 | tf_op jit(solution)/shard_map/ppermute | solution.py:240
  111.6 6.2 %collective-permute-start.2 = (bf16[16,64,256]{2,1,0:T(8,128)(2,1)S(1)}, bf16[16,64,256]{2,1,0:T(8,128)(2,1)S(1)}, u32[]{:S(2)}, u32[]{:S(2)}) collective-permute-start(bf16[16,64,256]{2,1,0:T(8,128)(2,1)S(1)} %collective-permute-done.1), channel_id=1, source_target_pairs={{0,2},{2,0},{4,6},{6,4},{8,10},{10,8},{12,14},{14,12},{16,18},{18,... | collective-permute-start | bytes 1572872 | tf_op jit(solution)/shard_map/ppermute | solution.py:243
  113.7 4.5 %collective-permute-start.5 = (bf16[16,64,256]{2,1,0:T(8,128)(2,1)}, bf16[16,64,256]{2,1,0:T(8,128)(2,1)S(1)}, u32[]{:S(2)}, u32[]{:S(2)}) collective-permute-start(bf16[16,64,256]{2,1,0:T(8,128)(2,1)} %collective-permute-done.4), channel_id=1, source_target_pairs={{0,2},{2,0},{4,6},{6,4},{8,10},{10,8},{12,14},{14,12},{16,18},{18,... | collective-permute-start | bytes 1572872 | tf_op jit(solution)/shard_map/ppermute | solution.py:243
  120.2 46.5 %all-to-all-start.2 = ((bf16[16,64,512]{2,1,0:T(8,128)(2,1)}), bf16[16,64,512]{2,1,0:T(8,128)(2,1)S(1)}, u32[]{:S(2)}, u32[]{:S(2)}) async-start(bf16[16,64,512]{2,1,0:T(8,128)(2,1)} %add_convert_fusion.3), calls=%async_computation.2 | async-start | bytes 2097152 | tf_op jit(solution)/shard_map/all_to_all | solution.py:230
  133.6 5.4 %copy-start.13 = (bf16[1024,2048]{1,0:T(8,128)(2,1)S(1)}, bf16[1024,2048]{1,0:T(8,128)(2,1)}, u32[]{:S(2)}) copy-start(bf16[1024,2048]{1,0:T(8,128)(2,1)} %all-gather.5.cloned.1.call-done) | copy-start | bytes 12582916
  137.2 3.7 copy-start.1
  137.2 13.3 %collective-permute-start.10 = (bf16[16,64,256]{2,1,0:T(8,128)(2,1)S(1)}, bf16[16,64,256]{2,1,0:T(8,128)(2,1)S(1)}, u32[]{:S(2)}, u32[]{:S(2)}) collective-permute-start(bf16[16,64,256]{2,1,0:T(8,128)(2,1)S(1)} %bitcast.194), channel_id=1, source_target_pairs={{0,1},{1,0},{2,3},{3,2},{4,5},{5,4},{6,7},{7,6},{8,9},{9,8},{10,11... | collective-permute-start | bytes 1572872 | tf_op jit(solution)/shard_map/ppermute | solution.py:239
  138.4 24.9 %collective-permute-start.9 = (bf16[16,64,256]{2,1,0:T(8,128)(2,1)S(1)}, bf16[16,64,256]{2,1,0:T(8,128)(2,1)S(1)}, u32[]{:S(2)}, u32[]{:S(2)}) collective-permute-start(bf16[16,64,256]{2,1,0:T(8,128)(2,1)S(1)} %bitcast.195), channel_id=1, source_target_pairs={{0,2},{2,0},{4,6},{6,4},{8,10},{10,8},{12,14},{14,12},{16,18},{18,... | collective-permute-start | bytes 1572872 | tf_op jit(solution)/shard_map/ppermute | solution.py:240
  140.2 21.5 %collective-permute-start.7 = (bf16[16,64,256]{2,1,0:T(8,128)(2,1)S(1)}, bf16[16,64,256]{2,1,0:T(8,128)(2,1)S(1)}, u32[]{:S(2)}, u32[]{:S(2)}) collective-permute-start(bf16[16,64,256]{2,1,0:T(8,128)(2,1)S(1)} %bitcast.197), channel_id=1, source_target_pairs={{0,1},{1,0},{2,3},{3,2},{4,5},{5,4},{6,7},{7,6},{8,9},{9,8},{10,11... | collective-permute-start | bytes 1572872 | tf_op jit(solution)/shard_map/ppermute | solution.py:239
  140.6 23.2 %collective-permute-start.6 = (bf16[16,64,256]{2,1,0:T(8,128)(2,1)S(1)}, bf16[16,64,256]{2,1,0:T(8,128)(2,1)S(1)}, u32[]{:S(2)}, u32[]{:S(2)}) collective-permute-start(bf16[16,64,256]{2,1,0:T(8,128)(2,1)S(1)} %bitcast.198), channel_id=1, source_target_pairs={{0,2},{2,0},{4,6},{6,4},{8,10},{10,8},{12,14},{14,12},{16,18},{18,... | collective-permute-start | bytes 1572872 | tf_op jit(solution)/shard_map/ppermute | solution.py:240
  151.0 13.8 %collective-permute-start.11 = (bf16[16,64,256]{2,1,0:T(8,128)(2,1)S(1)}, bf16[16,64,256]{2,1,0:T(8,128)(2,1)S(1)}, u32[]{:S(2)}, u32[]{:S(2)}) collective-permute-start(bf16[16,64,256]{2,1,0:T(8,128)(2,1)S(1)} %collective-permute-done.10), channel_id=1, source_target_pairs={{0,2},{2,0},{4,6},{6,4},{8,10},{10,8},{12,14},{14,12},{16,18},{18,... | collective-permute-start | bytes 1572872 | tf_op jit(solution)/shard_map/ppermute | solution.py:243
  161.7 2.6 collective-permute-start.8
  166.7 28.9 %all-to-all-start.3 = ((bf16[16,64,512]{2,1,0:T(8,128)(2,1)}), bf16[16,64,512]{2,1,0:T(8,128)(2,1)S(1)}, u32[]{:S(2)}, u32[]{:S(2)}) async-start(bf16[16,64,512]{2,1,0:T(8,128)(2,1)} %add_convert_fusion.2), calls=%async_computation.3 | async-start | bytes 2097152 | tf_op jit(solution)/shard_map/all_to_all | solution.py:230
  171.3 28.8 %copy-start.4 = (bf16[8,2,64,512]{3,0,1,2:T(8,128)(2,1)}, bf16[8,2,64,512]{3,0,1,2:T(8,128)(2,1)S(1)}, u32[]{:S(2)}) copy-start(bf16[8,2,64,512]{3,0,1,2:T(8,128)(2,1)S(1)} %copy.268) | copy-start | bytes 3145732
  174.0 56.1 %collective-permute-start.15 = (bf16[1024,512]{1,0:T(8,128)(2,1)}, bf16[1024,512]{1,0:T(8,128)(2,1)S(1)}, u32[]{:S(2)}, u32[]{:S(2)}) collective-permute-start(bf16[1024,512]{1,0:T(8,128)(2,1)} %constant_dynamic-slice_fusion), channel_id=1, source_target_pairs={{0,1},{1,0},{2,3},{3,2},{4,5},{5,4},{6,7},{7,6},{8,9},{9,8},{10,11... | collective-permute-start | bytes 3145736 | tf_op jit(solution)/shard_map/ppermute | solution.py:276
  198.4 9.0 %copy-start.5 = (bf16[8,2,64,512]{3,0,1,2:T(8,128)(2,1)}, bf16[8,2,64,512]{3,0,1,2:T(8,128)(2,1)S(1)}, u32[]{:S(2)}) copy-start(bf16[8,2,64,512]{3,0,1,2:T(8,128)(2,1)S(1)} %copy.267) | copy-start | bytes 3145732
  198.9 6.8 %collective-permute-start.14 = (bf16[128,8]{0,1:T(8,128)(2,1)S(1)}, bf16[128,8]{0,1:T(8,128)(2,1)S(1)}, u32[]{:S(2)}, u32[]{:S(2)}) collective-permute-start(bf16[128,8]{0,1:T(8,128)(2,1)S(1)} %maximum_select_fusion), channel_id=1, source_target_pairs={{0,1},{1,0},{2,3},{3,2},{4,5},{5,4},{6,7},{7,6},{8,9},{9,8},{10,11... | collective-permute-start | bytes 6152 | tf_op jit(solution)/shard_map/ppermute | solution.py:307
  200.1 6.7 %collective-permute-start.13 = (bf16[8,1024]{1,0:T(8,128)(2,1)S(1)}, bf16[8,1024]{1,0:T(8,128)(2,1)S(1)}, u32[]{:S(2)}, u32[]{:S(2)}) collective-permute-start(bf16[8,1024]{1,0:T(8,128)(2,1)S(1)} %bitcast.209), channel_id=1, source_target_pairs={{2,0},{4,2},{6,4},{8,6},{10,8},{12,10},{14,12},{16,14},{18,16},{20... | collective-permute-start | bytes 49160 | tf_op jit(solution)/shard_map/ppermute | solution.py:301
  202.0 4.7 %collective-permute-start.12 = (bf16[8,1024]{1,0:T(8,128)(2,1)S(1)}, bf16[8,1024]{1,0:T(8,128)(2,1)S(1)}, u32[]{:S(2)}, u32[]{:S(2)}) collective-permute-start(bf16[8,1024]{1,0:T(8,128)(2,1)S(1)} %bitcast.210), channel_id=1, source_target_pairs={{0,2},{2,4},{4,6},{6,8},{8,10},{10,12},{12,14},{14,16},{16,18},{18... | collective-permute-start | bytes 49160 | tf_op jit(solution)/shard_map/ppermute | solution.py:301
  223.6 6.5 %collective-permute-start.18 = (f32[128,8]{0,1:T(8,128)S(1)}, f32[128,8]{0,1:T(8,128)S(1)}, u32[]{:S(2)}, u32[]{:S(2)}) collective-permute-start(f32[128,8]{0,1:T(8,128)S(1)} %bitcast.217), channel_id=1, source_target_pairs={{0,1},{1,0},{2,3},{3,2},{4,5},{5,4},{6,7},{7,6},{8,9},{9,8},{10,11... | collective-permute-start | bytes 12296 | tf_op jit(solution)/shard_map/ppermute | solution.py:307
  223.9 7.2 %collective-permute-start.16 = (f32[8,1024]{1,0:T(8,128)S(1)}, f32[8,1024]{1,0:T(8,128)S(1)}, u32[]{:S(2)}, u32[]{:S(2)}) collective-permute-start(f32[8,1024]{1,0:T(8,128)S(1)} %get-tuple-element.44), channel_id=1, source_target_pairs={{0,2},{2,4},{4,6},{6,8},{8,10},{10,12},{12,14},{14,16},{16,18},{18... | collective-permute-start | bytes 98312 | tf_op jit(solution)/shard_map/ppermute | solution.py:301
  228.2 5.2 %collective-permute-start.17 = (f32[8,1024]{1,0:T(8,128)S(1)}, f32[8,1024]{1,0:T(8,128)S(1)}, u32[]{:S(2)}, u32[]{:S(2)}) collective-permute-start(f32[8,1024]{1,0:T(8,128)S(1)} %get-tuple-element.45), channel_id=1, source_target_pairs={{2,0},{4,2},{6,4},{8,6},{10,8},{12,10},{14,12},{16,14},{18,16},{20... | collective-permute-start | bytes 98312 | tf_op jit(solution)/shard_map/ppermute | solution.py:301
  238.8 31.8 %all-to-all-start.4 = ((bf16[16,128,256]{2,1,0:T(8,128)(2,1)}), bf16[16,128,256]{2,1,0:T(8,128)(2,1)S(1)}, u32[]{:S(2)}, u32[]{:S(2)}) async-start(bf16[16,128,256]{2,1,0:T(8,128)(2,1)} %rim_lines.2), calls=%async_computation.4 | async-start | bytes 2097152 | tf_op jit(solution)/shard_map/all_to_all | solution.py:230
  270.6 29.8 %all-to-all-start.5 = ((bf16[16,128,256]{2,1,0:T(8,128)(2,1)}), bf16[16,128,256]{2,1,0:T(8,128)(2,1)S(1)}, u32[]{:S(2)}, u32[]{:S(2)}) async-start(bf16[16,128,256]{2,1,0:T(8,128)(2,1)} %rim_lines.3), calls=%async_computation.5 | async-start | bytes 2097152 | tf_op jit(solution)/shard_map/all_to_all | solution.py:230
  275.7 3.7 copy-start.11
  284.1 44.0 %collective-permute-start.28 = (bf16[16,64,256]{2,1,0:T(8,128)(2,1)}, bf16[16,64,256]{2,1,0:T(8,128)(2,1)}, u32[]{:S(2)}, u32[]{:S(2)}) collective-permute-start(bf16[16,64,256]{2,1,0:T(8,128)(2,1)} %get-tuple-element.28), channel_id=1, source_target_pairs={{0,2},{2,0},{4,6},{6,4},{8,10},{10,8},{12,14},{14,12},{16,18},{18,... | collective-permute-start | bytes 1572872 | tf_op jit(solution)/shard_map/ppermute | solution.py:240
  284.5 42.1 %collective-permute-start.29 = (bf16[16,64,256]{2,1,0:T(8,128)(2,1)}, bf16[16,64,256]{2,1,0:T(8,128)(2,1)}, u32[]{:S(2)}, u32[]{:S(2)}) collective-permute-start(bf16[16,64,256]{2,1,0:T(8,128)(2,1)} %get-tuple-element.28), channel_id=1, source_target_pairs={{0,1},{1,0},{2,3},{3,2},{4,5},{5,4},{6,7},{7,6},{8,9},{9,8},{10,11... | collective-permute-start | bytes 1572872 | tf_op jit(solution)/shard_map/ppermute | solution.py:239
  308.8 13.7 %collective-permute-start.23 = (bf16[16,64,256]{2,1,0:T(8,128)(2,1)S(1)}, bf16[16,64,256]{2,1,0:T(8,128)(2,1)S(1)}, u32[]{:S(2)}, u32[]{:S(2)}) collective-permute-start(bf16[16,64,256]{2,1,0:T(8,128)(2,1)S(1)} %get-tuple-element.32), channel_id=1, source_target_pairs={{0,1},{1,0},{2,3},{3,2},{4,5},{5,4},{6,7},{7,6},{8,9},{9,8},{10,11... | collective-permute-start | bytes 1572872 | tf_op jit(solution)/shard_map/ppermute | solution.py:239
  310.0 13.7 %collective-permute-start.24 = (bf16[16,64,256]{2,1,0:T(8,128)(2,1)S(1)}, bf16[16,64,256]{2,1,0:T(8,128)(2,1)S(1)}, u32[]{:S(2)}, u32[]{:S(2)}) collective-permute-start(bf16[16,64,256]{2,1,0:T(8,128)(2,1)S(1)} %get-tuple-element.32), channel_id=1, source_target_pairs={{0,2},{2,0},{4,6},{6,4},{8,10},{10,8},{12,14},{14,12},{16,18},{18,... | collective-permute-start | bytes 1572872 | tf_op jit(solution)/shard_map/ppermute | solution.py:240
  314.4 24.4 %collective-permute-start.19 = (bf16[16,64,256]{2,1,0:T(8,128)(2,1)}, bf16[16,64,256]{2,1,0:T(8,128)(2,1)S(1)}, u32[]{:S(2)}, u32[]{:S(2)}) collective-permute-start(bf16[16,64,256]{2,1,0:T(8,128)(2,1)} %get-tuple-element.29), channel_id=1, source_target_pairs={{0,2},{2,0},{4,6},{6,4},{8,10},{10,8},{12,14},{14,12},{16,18},{18,... | collective-permute-start | bytes 1572872 | tf_op jit(solution)/shard_map/ppermute | solution.py:240
  322.5 15.0 %collective-permute-start.20 = (bf16[16,64,256]{2,1,0:T(8,128)(2,1)}, bf16[16,64,256]{2,1,0:T(8,128)(2,1)S(1)}, u32[]{:S(2)}, u32[]{:S(2)}) collective-permute-start(bf16[16,64,256]{2,1,0:T(8,128)(2,1)} %get-tuple-element.29), channel_id=1, source_target_pairs={{0,1},{1,0},{2,3},{3,2},{4,5},{5,4},{6,7},{7,6},{8,9},{9,8},{10,11... | collective-permute-start | bytes 1572872 | tf_op jit(solution)/shard_map/ppermute | solution.py:239
  323.7 16.6 %collective-permute-start.22 = (bf16[16,64,256]{2,1,0:T(8,128)(2,1)}, bf16[16,64,256]{2,1,0:T(8,128)(2,1)}, u32[]{:S(2)}, u32[]{:S(2)}) collective-permute-start(bf16[16,64,256]{2,1,0:T(8,128)(2,1)} %get-tuple-element.26), channel_id=1, source_target_pairs={{0,2},{2,0},{4,6},{6,4},{8,10},{10,8},{12,14},{14,12},{16,18},{18,... | collective-permute-start | bytes 1572872 | tf_op jit(solution)/shard_map/ppermute | solution.py:240
  326.6 3.8 collective-permute-start.25
  328.2 2.7 collective-permute-start.30
  332.7 29.7 %all-to-all-start.7 = ((bf16[16,64,512]{2,1,0:T(8,128)(2,1)}), bf16[16,64,512]{2,1,0:T(8,128)(2,1)S(1)}, u32[]{:S(2)}, u32[]{:S(2)}) async-start(bf16[16,64,512]{2,1,0:T(8,128)(2,1)} %add_convert_fusion), calls=%async_computation.7 | async-start | bytes 2097152 | tf_op jit(solution)/shard_map/all_to_all | solution.py:230
  338.0 15.0 %collective-permute-start.21 = (bf16[16,64,256]{2,1,0:T(8,128)(2,1)S(1)}, bf16[16,64,256]{2,1,0:T(8,128)(2,1)S(1)}, u32[]{:S(2)}, u32[]{:S(2)}) collective-permute-start(bf16[16,64,256]{2,1,0:T(8,128)(2,1)S(1)} %collective-permute-done.20), channel_id=1, source_target_pairs={{0,2},{2,0},{4,6},{6,4},{8,10},{10,8},{12,14},{14,12},{16,18},{18,... | collective-permute-start | bytes 1572872 | tf_op jit(solution)/shard_map/ppermute | solution.py:243
  338.4 13.6 %collective-permute-start.26 = (bf16[16,64,256]{2,1,0:T(8,128)(2,1)}, bf16[16,64,256]{2,1,0:T(8,128)(2,1)S(1)}, u32[]{:S(2)}, u32[]{:S(2)}) collective-permute-start(bf16[16,64,256]{2,1,0:T(8,128)(2,1)} %get-tuple-element.26), channel_id=1, source_target_pairs={{0,1},{1,0},{2,3},{3,2},{4,5},{5,4},{6,7},{7,6},{8,9},{9,8},{10,11... | collective-permute-start | bytes 1572872 | tf_op jit(solution)/shard_map/ppermute | solution.py:239
  352.0 2.5 collective-permute-start.27
  362.4 5.0 %copy-start.6 = (bf16[16,64,512]{2,1,0:T(8,128)(2,1)}, bf16[16,64,512]{2,1,0:T(8,128)(2,1)S(1)}, u32[]{:S(2)}) copy-start(bf16[16,64,512]{2,1,0:T(8,128)(2,1)S(1)} %all-to-all-done.7.lines) | copy-start | bytes 3145732
  362.4 29.8 %all-to-all-start.6 = ((bf16[16,64,512]{2,1,0:T(8,128)(2,1)}), bf16[16,64,512]{2,1,0:T(8,128)(2,1)S(1)}, u32[]{:S(2)}, u32[]{:S(2)}) async-start(bf16[16,64,512]{2,1,0:T(8,128)(2,1)} %add_convert_fusion.1), calls=%async_computation.6 | async-start | bytes 2097152 | tf_op jit(solution)/shard_map/all_to_all | solution.py:230
  (6 other events, 11.1 us)
Sparse Core Ops, SparseCore 0:
  10.7 64.8 all-gather.2
  77.8 55.6 all-gather.4

commit v4 on v3

--- a/solution.py
+++ b/solution.py
@@ -230,7 +230,7 @@
     return lax.all_to_all(lines, "gx", 0, 0, tiled=True)
 
 
-def plane_pieces(lines, parts, after=None, near_first=False):
+def plane_pieces(lines, parts, after=None):
     n_x, n_y = lax.axis_size("gx"), lax.axis_size("gy")
     groups = [list(range(i, i + parts)) for i in range(0, n_x, parts)]
     if n_y == 2 and parts == 2:
@@ -238,8 +238,6 @@
         sent = lines if after is None else lax.optimization_barrier((lines, after))[0]
         far = lax.ppermute(sent, "gy", [(0, 1), (1, 0)])
         near = lax.ppermute(lines, "gx", pairs)
-        if near_first:
-            far, near = lax.optimization_barrier((far, near))
         cross = lax.ppermute(far, "gx", pairs)
         return [lines, near, far, cross]
     plane = lax.all_gather(lines, "gy", axis=0, tiled=False)
@@ -377,13 +375,15 @@
     gradient = cross = None
     for h in range(CHUNKS):
         at, end = h * cut, (h + 1) * cut
+        planes = [plane_pieces(p[:, at:end], parts) for p in pulled[:-1]]
+        planes.append(plane_pieces(pulled[-1][:, at:end], parts, cross))
+        cross = planes[-1][-1]
+        if h == 0:
+            early, near = lax.optimization_barrier((planes[0][-1], planes[-1][1]))
+            planes[0][-1], planes[-1][1] = early, near
         carried = 0.0
-        for w, span in enumerate(spans):
-            last = w == CHUNKS - 1
-            held = cross if h > 0 and last else None
-            planes = plane_pieces(pulled[w][:, at:end], parts, held, h == 0 and last)
-            cross = planes[-1] if last else cross
-            for plane, matrix in zip(planes, columns_y):
+        for pieces, span in zip(planes, spans):
+            for plane, matrix in zip(pieces, columns_y):
                 carried = carried + jnp.einsum(
                     "brk,kc->brc", plane, matrix[span], preferred_element_type=F32
                 )

time: 405 us -> 401 us (level)
  no operation moved by 1% of the time
where the time goes in v4:
time: 401 us; the launch traced here: 399 us
  waiting for transfers between devices  148 us (37%)
  starting transfers between devices  76.5 us (19%)
  matrix products  58.8 us (15%)
  blocking collectives  42.3 us (11%)
  Pallas kernels  37.3 us (9%)
  local copies, waits for them, and re-layouts  18.3 us (5%)
  between operations  14.6 us (4%)
    all_to_all x7, waiting for transfers between devices, swap_all(): return lax.all_to_all(lines, 'gx', 0, 0, tiled=True)  95.5 us
    all_to_all x1, blocking collectives, swap_all(): return lax.all_to_all(lines, 'gx', 0, 0, tiled=True)  42.3 us
    all_to_all x7, starting transfers between devices, swap_all(): return lax.all_to_all(lines, 'gx', 0, 0, tiled=True)  41.6 us
    ppermute x8, waiting for transfers between devices, plane_pieces(): far = lax.ppermute(sent, 'gy', [(0, 1), (1, 0)])  35.9 us
    dot_general x16, matrix products, per_device(): jnp.einsum('brk,kc->brc', plane, matrix[span], preferred_element_type=F32)  22.6 us
    pallas_call x1, Pallas kernels, forward(): pl.pallas_call(forward_body, grid=(rows // STEP,), in_specs=[start] * CHU...  14.6 us
    dot_general x16, matrix products, per_device(): jnp.einsum('brc,kc->brk', plane, matrix[:, span], preferred_element_type=...  12.5 us
    dot_general x4, matrix products, per_device(): smoothed = jnp.dot(matrix_x[h], lines[w], preferred_element_type=F32)  11.9 us
  transfers between devices with their start and end apart: 40, of which 16 were waited for; matrix products, arithmetic and copies ran while one was open for 19% of the time, Pallas kernels for 7%

profile of v4, /device:TPU:9, one launch (start us, length us, event | category | flops | bytes accessed | tf_op | source)
XLA Modules:
  0.0 398.6 jit_solution(1704638938945968900)
XLA Ops:
  9.0 3.8 as_lines.3
  12.8 42.3 %all_to_all.40 = bf16[16,128,256]{2,1,0:T(8,128)(2,1)S(1)} all-to-all(bf16[16,128,256]{2,1,0:T(8,128)(2,1)} %as_lines.3), channel_id=1, replica_groups=mesh['gx'=16,'gy'=2] {'gx'}, dimensions={0} | all-to-all | bytes 2097152 | tf_op jit(solution)/shard_map/all_to_all | solution.py:230
  55.9 3.8 as_lines.2
  59.7 7.6 %all-to-all-start = ((bf16[16,128,256]{2,1,0:T(8,128)(2,1)}), bf16[16,128,256]{2,1,0:T(8,128)(2,1)S(1)}, u32[]{:S(2)}, u32[]{:S(2)}) async-start(bf16[16,128,256]{2,1,0:T(8,128)(2,1)} %as_lines.2), calls=%async_computation | async-start | bytes 2097152 | tf_op jit(solution)/shard_map/all_to_all | solution.py:230
  67.3 8.4 %all-gather.3.cloned.1.call-done = bf16[1024,2048]{1,0:T(8,128)(2,1)} async-done(((bf16[64,2048]{1,0:T(8,128)(2,1)}), bf16[1024,2048]{1,0:T(8,128)(2,1)}) %all-gather.3.cloned.1.call-update) | async-done | bytes 4194320 | tf_op jit(solution)/shard_map/all_gather | solution.py:322
  75.7 3.5 fusion.4
  79.4 2.1 collective-permute-start.4
  82.0 13.6 %all-to-all-done = bf16[16,128,256]{2,1,0:T(8,128)(2,1)S(1)} async-done(((bf16[16,128,256]{2,1,0:T(8,128)(2,1)}), bf16[16,128,256]{2,1,0:T(8,128)(2,1)S(1)}, u32[]{:S(2)}, u32[]{:S(2)}) %all-to-all-start) | async-done | bytes 1048608 | tf_op jit(solution)/shard_map/all_to_all | solution.py:230
  95.7 3.6 convolution_convert_fusion.3
  103.0 8.5 %collective-permute-done.1 = bf16[16,64,256]{2,1,0:T(8,128)(2,1)S(1)} collective-permute-done((bf16[16,64,256]{2,1,0:T(8,128)(2,1)S(1)}, bf16[16,64,256]{2,1,0:T(8,128)(2,1)S(1)}, u32[]{:S(2)}, u32[]{:S(2)}) %collective-permute-start.1) | collective-permute-done | bytes 524320 | tf_op jit(solution)/shard_map/ppermute | solution.py:239
  111.6 2.1 collective-permute-start.2
  118.3 1.9 add_convert_fusion.3
  120.2 8.0 %all-to-all-start.2 = ((bf16[16,64,512]{2,1,0:T(8,128)(2,1)}), bf16[16,64,512]{2,1,0:T(8,128)(2,1)S(1)}, u32[]{:S(2)}, u32[]{:S(2)}) async-start(bf16[16,64,512]{2,1,0:T(8,128)(2,1)} %add_convert_fusion.3), calls=%async_computation.2 | async-start | bytes 2097152 | tf_op jit(solution)/shard_map/all_to_all | solution.py:230
  128.2 5.4 %all-gather.5.cloned.1.call-done = bf16[1024,2048]{1,0:T(8,128)(2,1)} async-done(((bf16[64,2048]{1,0:T(8,128)(2,1)}), bf16[1024,2048]{1,0:T(8,128)(2,1)}) %all-gather.5.cloned.1.call-update) | async-done | bytes 4194320 | tf_op jit(solution)/shard_map/all_gather | solution.py:328
  133.6 3.6 convolution_convert_fusion
  141.8 8.7 %collective-permute-done.10 = bf16[16,64,256]{2,1,0:T(8,128)(2,1)S(1)} collective-permute-done((bf16[16,64,256]{2,1,0:T(8,128)(2,1)S(1)}, bf16[16,64,256]{2,1,0:T(8,128)(2,1)S(1)}, u32[]{:S(2)}, u32[]{:S(2)}) %collective-permute-start.10) | collective-permute-done | bytes 524320 | tf_op jit(solution)/shard_map/ppermute | solution.py:239
  152.8 9.0 %collective-permute-done.7 = bf16[16,64,256]{2,1,0:T(8,128)(2,1)S(1)} collective-permute-done((bf16[16,64,256]{2,1,0:T(8,128)(2,1)S(1)}, bf16[16,64,256]{2,1,0:T(8,128)(2,1)S(1)}, u32[]{:S(2)}, u32[]{:S(2)}) %collective-permute-start.7) | collective-permute-done | bytes 524320 | tf_op jit(solution)/shard_map/ppermute | solution.py:239
  164.8 1.9 add_convert_fusion.2
  166.7 4.0 %all-to-all-start.3 = ((bf16[16,64,512]{2,1,0:T(8,128)(2,1)}), bf16[16,64,512]{2,1,0:T(8,128)(2,1)S(1)}, u32[]{:S(2)}, u32[]{:S(2)}) async-start(bf16[16,64,512]{2,1,0:T(8,128)(2,1)} %add_convert_fusion.2), calls=%async_computation.3 | async-start | bytes 2097152 | tf_op jit(solution)/shard_map/all_to_all | solution.py:230
  171.7 2.3 constant_dynamic-slice_fusion
  175.2 20.4 %all-to-all-done.3 = bf16[16,64,512]{2,1,0:T(8,128)(2,1)S(1)} async-done(((bf16[16,64,512]{2,1,0:T(8,128)(2,1)}), bf16[16,64,512]{2,1,0:T(8,128)(2,1)S(1)}, u32[]{:S(2)}, u32[]{:S(2)}) %all-to-all-start.3) | async-done | bytes 1048608 | tf_op jit(solution)/shard_map/all_to_all | solution.py:230
  196.6 1.8 copy.267
  200.1 1.9 collective-permute-start.13
  202.0 3.6 collective-permute-start.12
  207.4 14.6 %forward.1 = (f32[128,8,1024]{2,1,0:T(8,128)}, f32[128,8,1024]{2,1,0:T(8,128)}, f32[2,8,1024]{2,1,0:T(8,128)}, f32[128,8,2]{2,1,0:T(8,128)}) custom-call(bf16[64,8,1024]{2,1,0:T(8,128)(2,1)} %bitcast.179, bf16[64,8,1024]{2,1,0:T(8,128)(2,1)} %bitcast.182, f32[2,8,1024]{2,1,0:T(8,128)} %maximum_convert_fusion.refs_2_, f32[128,8,2]{2,1,0:T(8,128)} %copy.249.refs_3_, ...), custom_call_target="tpu_custom_call" | custom-call | flops 31457280 | bytes 29360128 | tf_op jit(solution)/shard_map/forward/pallas_call | solution.py:169
  223.9 4.2 %collective-permute-start.16 = (f32[8,1024]{1,0:T(8,128)S(1)}, f32[8,1024]{1,0:T(8,128)S(1)}, u32[]{:S(2)}, u32[]{:S(2)}) collective-permute-start(f32[8,1024]{1,0:T(8,128)S(1)} %get-tuple-element.44), channel_id=1, source_target_pairs={{0,2},{2,4},{4,6},{6,8},{8,10},{10,12},{12,14},{14,16},{16,18},{18... | collective-permute-start | bytes 98312 | tf_op jit(solution)/shard_map/ppermute | solution.py:299
  228.2 1.9 collective-permute-start.17
  231.2 2.2 collective-permute-done.17
  234.0 4.8 %rim_lines.2 = bf16[16,128,256]{2,1,0:T(8,128)(2,1)} custom-call(f32[128,8,1024]{2,1,0:T(8,128)} %get-tuple-element.21.flat, f32[2,8,1024]{2,1,0:T(8,128)} %pad_maximum_fusion.rows_in, f32[128,8,2]{2,1,0:T(8,128)} %copy.251.sides), custom_call_target="tpu_custom_call" | custom-call | flops 4194304 | bytes 8388608 | tf_op jit(solution)/shard_map/rim_lines/pallas_call | solution.py:213
  238.8 7.0 %all-to-all-start.4 = ((bf16[16,128,256]{2,1,0:T(8,128)(2,1)}), bf16[16,128,256]{2,1,0:T(8,128)(2,1)S(1)}, u32[]{:S(2)}, u32[]{:S(2)}) async-start(bf16[16,128,256]{2,1,0:T(8,128)(2,1)} %rim_lines.2), calls=%async_computation.4 | async-start | bytes 2097152 | tf_op jit(solution)/shard_map/all_to_all | solution.py:230
  245.8 4.7 %rim_lines.3 = bf16[16,128,256]{2,1,0:T(8,128)(2,1)} custom-call(f32[128,8,1024]{2,1,0:T(8,128)} %get-tuple-element.21.flat, f32[2,8,1024]{2,1,0:T(8,128)} %pad_maximum_fusion.rows_in, f32[128,8,2]{2,1,0:T(8,128)} %copy.251.sides), custom_call_target="tpu_custom_call" | custom-call | flops 4194304 | bytes 8388608 | tf_op jit(solution)/shard_map/rim_lines/pallas_call | solution.py:213
  250.5 20.2 %all-to-all-done.4 = bf16[16,128,256]{2,1,0:T(8,128)(2,1)S(1)} async-done(((bf16[16,128,256]{2,1,0:T(8,128)(2,1)}), bf16[16,128,256]{2,1,0:T(8,128)(2,1)S(1)}, u32[]{:S(2)}, u32[]{:S(2)}) %all-to-all-start.4) | async-done | bytes 1048608 | tf_op jit(solution)/shard_map/all_to_all | solution.py:230
  270.6 5.0 %all-to-all-start.5 = ((bf16[16,128,256]{2,1,0:T(8,128)(2,1)}), bf16[16,128,256]{2,1,0:T(8,128)(2,1)S(1)}, u32[]{:S(2)}, u32[]{:S(2)}) async-start(bf16[16,128,256]{2,1,0:T(8,128)(2,1)} %rim_lines.3), calls=%async_computation.5 | async-start | bytes 2097152 | tf_op jit(solution)/shard_map/all_to_all | solution.py:230
  275.7 3.6 fusion.51
  279.3 2.2 fusion.3
  285.7 14.8 %all-to-all-done.5 = bf16[16,128,256]{2,1,0:T(8,128)(2,1)S(1)} async-done(((bf16[16,128,256]{2,1,0:T(8,128)(2,1)}), bf16[16,128,256]{2,1,0:T(8,128)(2,1)S(1)}, u32[]{:S(2)}, u32[]{:S(2)}) %all-to-all-start.5) | async-done | bytes 1048608 | tf_op jit(solution)/shard_map/all_to_all | solution.py:230
  300.5 3.6 fusion.52
  304.2 2.2 fusion.2
  311.5 2.9 fusion.26
  316.7 2.9 fusion.30
  328.3 5.0 %all-to-all-start.7 = ((bf16[16,64,512]{2,1,0:T(8,128)(2,1)}), bf16[16,64,512]{2,1,0:T(8,128)(2,1)S(1)}, u32[]{:S(2)}, u32[]{:S(2)}) async-start(bf16[16,64,512]{2,1,0:T(8,128)(2,1)} %add_convert_fusion), calls=%async_computation.7 | async-start | bytes 2097152 | tf_op jit(solution)/shard_map/all_to_all | solution.py:230
  339.4 9.2 %collective-permute-done.25 = bf16[16,64,256]{2,1,0:T(8,128)(2,1)S(1)} collective-permute-done((bf16[16,64,256]{2,1,0:T(8,128)(2,1)}, bf16[16,64,256]{2,1,0:T(8,128)(2,1)S(1)}, u32[]{:S(2)}, u32[]{:S(2)}) %collective-permute-start.25) | collective-permute-done | bytes 524320 | tf_op jit(solution)/shard_map/ppermute | solution.py:239
  351.8 1.8 add_convert_fusion.1
  353.6 4.5 %all-to-all-done.7.lines = bf16[16,64,512]{2,1,0:T(8,128)(2,1)S(1)} async-done(((bf16[16,64,512]{2,1,0:T(8,128)(2,1)}), bf16[16,64,512]{2,1,0:T(8,128)(2,1)S(1)}, u32[]{:S(2)}, u32[]{:S(2)}) %all-to-all-start.7) | async-done | bytes 1048608 | tf_op jit(solution)/shard_map/all_to_all | solution.py:230
  358.1 5.0 %all-to-all-start.6 = ((bf16[16,64,512]{2,1,0:T(8,128)(2,1)}), bf16[16,64,512]{2,1,0:T(8,128)(2,1)S(1)}, u32[]{:S(2)}, u32[]{:S(2)}) async-start(bf16[16,64,512]{2,1,0:T(8,128)(2,1)} %add_convert_fusion.1), calls=%async_computation.6 | async-start | bytes 2097152 | tf_op jit(solution)/shard_map/all_to_all | solution.py:230
  363.1 2.8 add_lines.2.rest_0_
  366.0 22.0 %all-to-all-done.6.lines = bf16[16,64,512]{2,1,0:T(8,128)(2,1)S(1)} async-done(((bf16[16,64,512]{2,1,0:T(8,128)(2,1)}), bf16[16,64,512]{2,1,0:T(8,128)(2,1)S(1)}, u32[]{:S(2)}, u32[]{:S(2)}) %all-to-all-start.6) | async-done | bytes 1048608 | tf_op jit(solution)/shard_map/all_to_all | solution.py:230
  389.0 2.8 add_lines.3
  (142 shorter events, 62.1 us)
Async XLA Ops:
  7.2 68.5 %all-gather.3.cloned.1.call-start = ((), (), s32[]{:S(2)}) async-start(), calls=%async_computation.8 | async-start | bytes 4456448 | tf_op jit(solution)/shard_map/all_gather | solution.py:322
  8.9 46.2 %copy-start.9 = (bf16[128,2048]{1,0:T(8,128)(2,1)S(1)}, bf16[128,2048]{1,0:T(8,128)(2,1)}, u32[]{:S(2)}) copy-start(bf16[128,2048]{1,0:T(8,128)(2,1)} %param.12) | copy-start | bytes 1572868
  8.9 124.6 %all-gather.5.cloned.1.call-start = ((), (), s32[]{:S(2)}) async-start(), calls=%async_computation.9 | async-start | bytes 4456448 | tf_op jit(solution)/shard_map/all_gather | solution.py:328
  59.7 36.0 %all-to-all-start = ((bf16[16,128,256]{2,1,0:T(8,128)(2,1)}), bf16[16,128,256]{2,1,0:T(8,128)(2,1)S(1)}, u32[]{:S(2)}, u32[]{:S(2)}) async-start(bf16[16,128,256]{2,1,0:T(8,128)(2,1)} %as_lines.2), calls=%async_computation | async-start | bytes 2097152 | tf_op jit(solution)/shard_map/all_to_all | solution.py:230
  79.4 34.3 %collective-permute-start.4 = (bf16[16,64,256]{2,1,0:T(8,128)(2,1)S(1)}, bf16[16,64,256]{2,1,0:T(8,128)(2,1)}, u32[]{:S(2)}, u32[]{:S(2)}) collective-permute-start(bf16[16,64,256]{2,1,0:T(8,128)(2,1)S(1)} %bitcast.187), channel_id=1, source_target_pairs={{0,1},{1,0},{2,3},{3,2},{4,5},{5,4},{6,7},{7,6},{8,9},{9,8},{10,11... | collective-permute-start | bytes 1572872 | tf_op jit(solution)/shard_map/ppermute | solution.py:239
  81.5 34.7 %collective-permute-start.3 = (bf16[16,64,256]{2,1,0:T(8,128)(2,1)S(1)}, bf16[16,64,256]{2,1,0:T(8,128)(2,1)}, u32[]{:S(2)}, u32[]{:S(2)}) collective-permute-start(bf16[16,64,256]{2,1,0:T(8,128)(2,1)S(1)} %bitcast.188), channel_id=1, source_target_pairs={{0,2},{2,0},{4,6},{6,4},{8,10},{10,8},{12,14},{14,12},{16,18},{18,... | collective-permute-start | bytes 1572872 | tf_op jit(solution)/shard_map/ppermute | solution.py:240
  95.7 6.4 %copy-start = (bf16[1024,2048]{1,0:T(8,128)(2,1)S(1)}, bf16[1024,2048]{1,0:T(8,128)(2,1)}, u32[]{:S(2)}) copy-start(bf16[1024,2048]{1,0:T(8,128)(2,1)} %param.13) | copy-start | bytes 12582916
  99.3 12.3 %collective-permute-start.1 = (bf16[16,64,256]{2,1,0:T(8,128)(2,1)S(1)}, bf16[16,64,256]{2,1,0:T(8,128)(2,1)S(1)}, u32[]{:S(2)}, u32[]{:S(2)}) collective-permute-start(bf16[16,64,256]{2,1,0:T(8,128)(2,1)S(1)} %bitcast.200), channel_id=1, source_target_pairs={{0,1},{1,0},{2,3},{3,2},{4,5},{5,4},{6,7},{7,6},{8,9},{9,8},{10,11... | collective-permute-start | bytes 1572872 | tf_op jit(solution)/shard_map/ppermute | solution.py:239
  100.5 15.2 %collective-permute-start = (bf16[16,64,256]{2,1,0:T(8,128)(2,1)S(1)}, bf16[16,64,256]{2,1,0:T(8,128)(2,1)S(1)}, u32[]{:S(2)}, u32[]{:S(2)}) collective-permute-start(bf16[16,64,256]{2,1,0:T(8,128)(2,1)S(1)} %bitcast.201), channel_id=1, source_target_pairs={{0,2},{2,0},{4,6},{6,4},{8,10},{10,8},{12,14},{14,12},{16,18},{18,... | collective-permute-start | bytes 1572872 | tf_op jit(solution)/shard_map/ppermute | solution.py:240
  111.6 6.2 %collective-permute-start.2 = (bf16[16,64,256]{2,1,0:T(8,128)(2,1)S(1)}, bf16[16,64,256]{2,1,0:T(8,128)(2,1)S(1)}, u32[]{:S(2)}, u32[]{:S(2)}) collective-permute-start(bf16[16,64,256]{2,1,0:T(8,128)(2,1)S(1)} %collective-permute-done.1), channel_id=1, source_target_pairs={{0,2},{2,0},{4,6},{6,4},{8,10},{10,8},{12,14},{14,12},{16,18},{18,... | collective-permute-start | bytes 1572872 | tf_op jit(solution)/shard_map/ppermute | solution.py:241
  113.7 4.5 %collective-permute-start.5 = (bf16[16,64,256]{2,1,0:T(8,128)(2,1)}, bf16[16,64,256]{2,1,0:T(8,128)(2,1)S(1)}, u32[]{:S(2)}, u32[]{:S(2)}) collective-permute-start(bf16[16,64,256]{2,1,0:T(8,128)(2,1)} %collective-permute-done.4), channel_id=1, source_target_pairs={{0,2},{2,0},{4,6},{6,4},{8,10},{10,8},{12,14},{14,12},{16,18},{18,... | collective-permute-start | bytes 1572872 | tf_op jit(solution)/shard_map/ppermute | solution.py:241
  120.2 46.5 %all-to-all-start.2 = ((bf16[16,64,512]{2,1,0:T(8,128)(2,1)}), bf16[16,64,512]{2,1,0:T(8,128)(2,1)S(1)}, u32[]{:S(2)}, u32[]{:S(2)}) async-start(bf16[16,64,512]{2,1,0:T(8,128)(2,1)} %add_convert_fusion.3), calls=%async_computation.2 | async-start | bytes 2097152 | tf_op jit(solution)/shard_map/all_to_all | solution.py:230
  133.6 5.4 %copy-start.13 = (bf16[1024,2048]{1,0:T(8,128)(2,1)S(1)}, bf16[1024,2048]{1,0:T(8,128)(2,1)}, u32[]{:S(2)}) copy-start(bf16[1024,2048]{1,0:T(8,128)(2,1)} %all-gather.5.cloned.1.call-done) | copy-start | bytes 12582916
  137.2 3.7 copy-start.1
  137.2 13.3 %collective-permute-start.10 = (bf16[16,64,256]{2,1,0:T(8,128)(2,1)S(1)}, bf16[16,64,256]{2,1,0:T(8,128)(2,1)S(1)}, u32[]{:S(2)}, u32[]{:S(2)}) collective-permute-start(bf16[16,64,256]{2,1,0:T(8,128)(2,1)S(1)} %bitcast.194), channel_id=1, source_target_pairs={{0,1},{1,0},{2,3},{3,2},{4,5},{5,4},{6,7},{7,6},{8,9},{9,8},{10,11... | collective-permute-start | bytes 1572872 | tf_op jit(solution)/shard_map/ppermute | solution.py:239
  138.4 24.9 %collective-permute-start.9 = (bf16[16,64,256]{2,1,0:T(8,128)(2,1)S(1)}, bf16[16,64,256]{2,1,0:T(8,128)(2,1)S(1)}, u32[]{:S(2)}, u32[]{:S(2)}) collective-permute-start(bf16[16,64,256]{2,1,0:T(8,128)(2,1)S(1)} %bitcast.195), channel_id=1, source_target_pairs={{0,2},{2,0},{4,6},{6,4},{8,10},{10,8},{12,14},{14,12},{16,18},{18,... | collective-permute-start | bytes 1572872 | tf_op jit(solution)/shard_map/ppermute | solution.py:240
  140.2 21.5 %collective-permute-start.7 = (bf16[16,64,256]{2,1,0:T(8,128)(2,1)S(1)}, bf16[16,64,256]{2,1,0:T(8,128)(2,1)S(1)}, u32[]{:S(2)}, u32[]{:S(2)}) collective-permute-start(bf16[16,64,256]{2,1,0:T(8,128)(2,1)S(1)} %bitcast.197), channel_id=1, source_target_pairs={{0,1},{1,0},{2,3},{3,2},{4,5},{5,4},{6,7},{7,6},{8,9},{9,8},{10,11... | collective-permute-start | bytes 1572872 | tf_op jit(solution)/shard_map/ppermute | solution.py:239
  140.6 23.2 %collective-permute-start.6 = (bf16[16,64,256]{2,1,0:T(8,128)(2,1)S(1)}, bf16[16,64,256]{2,1,0:T(8,128)(2,1)S(1)}, u32[]{:S(2)}, u32[]{:S(2)}) collective-permute-start(bf16[16,64,256]{2,1,0:T(8,128)(2,1)S(1)} %bitcast.198), channel_id=1, source_target_pairs={{0,2},{2,0},{4,6},{6,4},{8,10},{10,8},{12,14},{14,12},{16,18},{18,... | collective-permute-start | bytes 1572872 | tf_op jit(solution)/shard_map/ppermute | solution.py:240
  151.0 13.8 %collective-permute-start.11 = (bf16[16,64,256]{2,1,0:T(8,128)(2,1)S(1)}, bf16[16,64,256]{2,1,0:T(8,128)(2,1)S(1)}, u32[]{:S(2)}, u32[]{:S(2)}) collective-permute-start(bf16[16,64,256]{2,1,0:T(8,128)(2,1)S(1)} %collective-permute-done.10), channel_id=1, source_target_pairs={{0,2},{2,0},{4,6},{6,4},{8,10},{10,8},{12,14},{14,12},{16,18},{18,... | collective-permute-start | bytes 1572872 | tf_op jit(solution)/shard_map/ppermute | solution.py:241
  161.7 2.6 collective-permute-start.8
  166.7 28.9 %all-to-all-start.3 = ((bf16[16,64,512]{2,1,0:T(8,128)(2,1)}), bf16[16,64,512]{2,1,0:T(8,128)(2,1)S(1)}, u32[]{:S(2)}, u32[]{:S(2)}) async-start(bf16[16,64,512]{2,1,0:T(8,128)(2,1)} %add_convert_fusion.2), calls=%async_computation.3 | async-start | bytes 2097152 | tf_op jit(solution)/shard_map/all_to_all | solution.py:230
  171.3 28.8 %copy-start.4 = (bf16[8,2,64,512]{3,0,1,2:T(8,128)(2,1)}, bf16[8,2,64,512]{3,0,1,2:T(8,128)(2,1)S(1)}, u32[]{:S(2)}) copy-start(bf16[8,2,64,512]{3,0,1,2:T(8,128)(2,1)S(1)} %copy.268) | copy-start | bytes 3145732
  174.0 56.1 %collective-permute-start.15 = (bf16[1024,512]{1,0:T(8,128)(2,1)}, bf16[1024,512]{1,0:T(8,128)(2,1)S(1)}, u32[]{:S(2)}, u32[]{:S(2)}) collective-permute-start(bf16[1024,512]{1,0:T(8,128)(2,1)} %constant_dynamic-slice_fusion), channel_id=1, source_target_pairs={{0,1},{1,0},{2,3},{3,2},{4,5},{5,4},{6,7},{7,6},{8,9},{9,8},{10,11... | collective-permute-start | bytes 3145736 | tf_op jit(solution)/shard_map/ppermute | solution.py:274
  198.4 9.0 %copy-start.5 = (bf16[8,2,64,512]{3,0,1,2:T(8,128)(2,1)}, bf16[8,2,64,512]{3,0,1,2:T(8,128)(2,1)S(1)}, u32[]{:S(2)}) copy-start(bf16[8,2,64,512]{3,0,1,2:T(8,128)(2,1)S(1)} %copy.267) | copy-start | bytes 3145732
  198.9 6.8 %collective-permute-start.14 = (bf16[128,8]{0,1:T(8,128)(2,1)S(1)}, bf16[128,8]{0,1:T(8,128)(2,1)S(1)}, u32[]{:S(2)}, u32[]{:S(2)}) collective-permute-start(bf16[128,8]{0,1:T(8,128)(2,1)S(1)} %maximum_select_fusion), channel_id=1, source_target_pairs={{0,1},{1,0},{2,3},{3,2},{4,5},{5,4},{6,7},{7,6},{8,9},{9,8},{10,11... | collective-permute-start | bytes 6152 | tf_op jit(solution)/shard_map/ppermute | solution.py:305
  200.1 6.7 %collective-permute-start.13 = (bf16[8,1024]{1,0:T(8,128)(2,1)S(1)}, bf16[8,1024]{1,0:T(8,128)(2,1)S(1)}, u32[]{:S(2)}, u32[]{:S(2)}) collective-permute-start(bf16[8,1024]{1,0:T(8,128)(2,1)S(1)} %bitcast.209), channel_id=1, source_target_pairs={{2,0},{4,2},{6,4},{8,6},{10,8},{12,10},{14,12},{16,14},{18,16},{20... | collective-permute-start | bytes 49160 | tf_op jit(solution)/shard_map/ppermute | solution.py:299
  202.0 4.7 %collective-permute-start.12 = (bf16[8,1024]{1,0:T(8,128)(2,1)S(1)}, bf16[8,1024]{1,0:T(8,128)(2,1)S(1)}, u32[]{:S(2)}, u32[]{:S(2)}) collective-permute-start(bf16[8,1024]{1,0:T(8,128)(2,1)S(1)} %bitcast.210), channel_id=1, source_target_pairs={{0,2},{2,4},{4,6},{6,8},{8,10},{10,12},{12,14},{14,16},{16,18},{18... | collective-permute-start | bytes 49160 | tf_op jit(solution)/shard_map/ppermute | solution.py:299
  223.6 6.5 %collective-permute-start.18 = (f32[128,8]{0,1:T(8,128)S(1)}, f32[128,8]{0,1:T(8,128)S(1)}, u32[]{:S(2)}, u32[]{:S(2)}) collective-permute-start(f32[128,8]{0,1:T(8,128)S(1)} %bitcast.217), channel_id=1, source_target_pairs={{0,1},{1,0},{2,3},{3,2},{4,5},{5,4},{6,7},{7,6},{8,9},{9,8},{10,11... | collective-permute-start | bytes 12296 | tf_op jit(solution)/shard_map/ppermute | solution.py:305
  223.9 7.2 %collective-permute-start.16 = (f32[8,1024]{1,0:T(8,128)S(1)}, f32[8,1024]{1,0:T(8,128)S(1)}, u32[]{:S(2)}, u32[]{:S(2)}) collective-permute-start(f32[8,1024]{1,0:T(8,128)S(1)} %get-tuple-element.44), channel_id=1, source_target_pairs={{0,2},{2,4},{4,6},{6,8},{8,10},{10,12},{12,14},{14,16},{16,18},{18... | collective-permute-start | bytes 98312 | tf_op jit(solution)/shard_map/ppermute | solution.py:299
  228.2 5.2 %collective-permute-start.17 = (f32[8,1024]{1,0:T(8,128)S(1)}, f32[8,1024]{1,0:T(8,128)S(1)}, u32[]{:S(2)}, u32[]{:S(2)}) collective-permute-start(f32[8,1024]{1,0:T(8,128)S(1)} %get-tuple-element.45), channel_id=1, source_target_pairs={{2,0},{4,2},{6,4},{8,6},{10,8},{12,10},{14,12},{16,14},{18,16},{20... | collective-permute-start | bytes 98312 | tf_op jit(solution)/shard_map/ppermute | solution.py:299
  238.8 31.8 %all-to-all-start.4 = ((bf16[16,128,256]{2,1,0:T(8,128)(2,1)}), bf16[16,128,256]{2,1,0:T(8,128)(2,1)S(1)}, u32[]{:S(2)}, u32[]{:S(2)}) async-start(bf16[16,128,256]{2,1,0:T(8,128)(2,1)} %rim_lines.2), calls=%async_computation.4 | async-start | bytes 2097152 | tf_op jit(solution)/shard_map/all_to_all | solution.py:230
  270.6 29.8 %all-to-all-start.5 = ((bf16[16,128,256]{2,1,0:T(8,128)(2,1)}), bf16[16,128,256]{2,1,0:T(8,128)(2,1)S(1)}, u32[]{:S(2)}, u32[]{:S(2)}) async-start(bf16[16,128,256]{2,1,0:T(8,128)(2,1)} %rim_lines.3), calls=%async_computation.5 | async-start | bytes 2097152 | tf_op jit(solution)/shard_map/all_to_all | solution.py:230
  275.7 3.7 copy-start.11
  284.1 35.5 %collective-permute-start.27 = (bf16[16,64,256]{2,1,0:T(8,128)(2,1)}, bf16[16,64,256]{2,1,0:T(8,128)(2,1)}, u32[]{:S(2)}, u32[]{:S(2)}) collective-permute-start(bf16[16,64,256]{2,1,0:T(8,128)(2,1)} %get-tuple-element.28), channel_id=1, source_target_pairs={{0,2},{2,0},{4,6},{6,4},{8,10},{10,8},{12,14},{14,12},{16,18},{18,... | collective-permute-start | bytes 1572872 | tf_op jit(solution)/shard_map/ppermute | solution.py:240
  284.5 35.4 %collective-permute-start.28 = (bf16[16,64,256]{2,1,0:T(8,128)(2,1)}, bf16[16,64,256]{2,1,0:T(8,128)(2,1)}, u32[]{:S(2)}, u32[]{:S(2)}) collective-permute-start(bf16[16,64,256]{2,1,0:T(8,128)(2,1)} %get-tuple-element.28), channel_id=1, source_target_pairs={{0,1},{1,0},{2,3},{3,2},{4,5},{5,4},{6,7},{7,6},{8,9},{9,8},{10,11... | collective-permute-start | bytes 1572872 | tf_op jit(solution)/shard_map/ppermute | solution.py:239
  308.8 15.2 %collective-permute-start.30 = (bf16[16,64,256]{2,1,0:T(8,128)(2,1)S(1)}, bf16[16,64,256]{2,1,0:T(8,128)(2,1)S(1)}, u32[]{:S(2)}, u32[]{:S(2)}) collective-permute-start(bf16[16,64,256]{2,1,0:T(8,128)(2,1)S(1)} %get-tuple-element.32), channel_id=1, source_target_pairs={{0,2},{2,0},{4,6},{6,4},{8,10},{10,8},{12,14},{14,12},{16,18},{18,... | collective-permute-start | bytes 1572872 | tf_op jit(solution)/shard_map/ppermute | solution.py:240
  308.8 14.6 %collective-permute-start.23 = (bf16[16,64,256]{2,1,0:T(8,128)(2,1)S(1)}, bf16[16,64,256]{2,1,0:T(8,128)(2,1)S(1)}, u32[]{:S(2)}, u32[]{:S(2)}) collective-permute-start(bf16[16,64,256]{2,1,0:T(8,128)(2,1)S(1)} %get-tuple-element.32), channel_id=1, source_target_pairs={{0,1},{1,0},{2,3},{3,2},{4,5},{5,4},{6,7},{7,6},{8,9},{9,8},{10,11... | collective-permute-start | bytes 1572872 | tf_op jit(solution)/shard_map/ppermute | solution.py:239
  314.4 21.7 %collective-permute-start.19 = (bf16[16,64,256]{2,1,0:T(8,128)(2,1)}, bf16[16,64,256]{2,1,0:T(8,128)(2,1)S(1)}, u32[]{:S(2)}, u32[]{:S(2)}) collective-permute-start(bf16[16,64,256]{2,1,0:T(8,128)(2,1)} %get-tuple-element.29), channel_id=1, source_target_pairs={{0,2},{2,0},{4,6},{6,4},{8,10},{10,8},{12,14},{14,12},{16,18},{18,... | collective-permute-start | bytes 1572872 | tf_op jit(solution)/shard_map/ppermute | solution.py:240
  319.6 14.1 %collective-permute-start.20 = (bf16[16,64,256]{2,1,0:T(8,128)(2,1)}, bf16[16,64,256]{2,1,0:T(8,128)(2,1)S(1)}, u32[]{:S(2)}, u32[]{:S(2)}) collective-permute-start(bf16[16,64,256]{2,1,0:T(8,128)(2,1)} %get-tuple-element.29), channel_id=1, source_target_pairs={{0,1},{1,0},{2,3},{3,2},{4,5},{5,4},{6,7},{7,6},{8,9},{9,8},{10,11... | collective-permute-start | bytes 1572872 | tf_op jit(solution)/shard_map/ppermute | solution.py:239
  319.9 4.6 %collective-permute-start.29 = (bf16[16,64,256]{2,1,0:T(8,128)(2,1)}, bf16[16,64,256]{2,1,0:T(8,128)(2,1)S(1)}, u32[]{:S(2)}, u32[]{:S(2)}) collective-permute-start(bf16[16,64,256]{2,1,0:T(8,128)(2,1)} %collective-permute-done.28), channel_id=1, source_target_pairs={{0,2},{2,0},{4,6},{6,4},{8,10},{10,8},{12,14},{14,12},{16,18},{18,... | collective-permute-start | bytes 1572872 | tf_op jit(solution)/shard_map/ppermute | solution.py:241
  323.4 14.3 %collective-permute-start.22 = (bf16[16,64,256]{2,1,0:T(8,128)(2,1)}, bf16[16,64,256]{2,1,0:T(8,128)(2,1)}, u32[]{:S(2)}, u32[]{:S(2)}) collective-permute-start(bf16[16,64,256]{2,1,0:T(8,128)(2,1)} %get-tuple-element.25), channel_id=1, source_target_pairs={{0,2},{2,0},{4,6},{6,4},{8,10},{10,8},{12,14},{14,12},{16,18},{18,... | collective-permute-start | bytes 1572872 | tf_op jit(solution)/shard_map/ppermute | solution.py:240
  324.1 2.4 collective-permute-start.24
  328.3 29.9 %all-to-all-start.7 = ((bf16[16,64,512]{2,1,0:T(8,128)(2,1)}), bf16[16,64,512]{2,1,0:T(8,128)(2,1)S(1)}, u32[]{:S(2)}, u32[]{:S(2)}) async-start(bf16[16,64,512]{2,1,0:T(8,128)(2,1)} %add_convert_fusion), calls=%async_computation.7 | async-start | bytes 2097152 | tf_op jit(solution)/shard_map/all_to_all | solution.py:230
  334.2 15.3 %collective-permute-start.21 = (bf16[16,64,256]{2,1,0:T(8,128)(2,1)S(1)}, bf16[16,64,256]{2,1,0:T(8,128)(2,1)S(1)}, u32[]{:S(2)}, u32[]{:S(2)}) collective-permute-start(bf16[16,64,256]{2,1,0:T(8,128)(2,1)S(1)} %collective-permute-done.20), channel_id=1, source_target_pairs={{0,2},{2,0},{4,6},{6,4},{8,10},{10,8},{12,14},{14,12},{16,18},{18,... | collective-permute-start | bytes 1572872 | tf_op jit(solution)/shard_map/ppermute | solution.py:241
  334.9 13.7 %collective-permute-start.25 = (bf16[16,64,256]{2,1,0:T(8,128)(2,1)}, bf16[16,64,256]{2,1,0:T(8,128)(2,1)S(1)}, u32[]{:S(2)}, u32[]{:S(2)}) collective-permute-start(bf16[16,64,256]{2,1,0:T(8,128)(2,1)} %get-tuple-element.25), channel_id=1, source_target_pairs={{0,1},{1,0},{2,3},{3,2},{4,5},{5,4},{6,7},{7,6},{8,9},{9,8},{10,11... | collective-permute-start | bytes 1572872 | tf_op jit(solution)/shard_map/ppermute | solution.py:239
  348.6 2.4 collective-permute-start.26
  358.1 5.0 %copy-start.6 = (bf16[16,64,512]{2,1,0:T(8,128)(2,1)}, bf16[16,64,512]{2,1,0:T(8,128)(2,1)S(1)}, u32[]{:S(2)}) copy-start(bf16[16,64,512]{2,1,0:T(8,128)(2,1)S(1)} %all-to-all-done.7.lines) | copy-start | bytes 3145732
  358.1 29.8 %all-to-all-start.6 = ((bf16[16,64,512]{2,1,0:T(8,128)(2,1)}), bf16[16,64,512]{2,1,0:T(8,128)(2,1)S(1)}, u32[]{:S(2)}, u32[]{:S(2)}) async-start(bf16[16,64,512]{2,1,0:T(8,128)(2,1)} %add_convert_fusion.1), calls=%async_computation.6 | async-start | bytes 2097152 | tf_op jit(solution)/shard_map/all_to_all | solution.py:230
  (6 other events, 11.1 us)
Sparse Core Ops, SparseCore 0:
  10.7 64.8 all-gather.2
  77.8 55.6 all-gather.4
